TPU v7x, 32 devices: a whole 2x2x4 slice. The times are simulated.
32 devices in a mesh: gx: 4 (over y, x), gy: 8 (over z, core).
Axes of the slice: x: 2, y: 2, z: 4, core: 2. Of those that a mesh axis runs over, the one named last changes fastest.
Arguments:
- image: float32 [512, 32768], P('gx', 'gy'), may hold values from -6 to 6
- psfs: bfloat16 [16, 16, 32, 1024], P('gx', 'gy'), may hold values from -0.11035156 to 0.11035156
Outputs:
- hessian_image: float32 [512, 32768], P('gx', 'gy')
All inputs are finite; a program needn't handle non-finite values.
Results may differ from a plain program's by a relative error of at most 0.023.
Values may be sent and summed in bfloat16 or wider, within the bound.
No kernel may reach another device: no remote copies, remote signals or barrier semaphores. Data moves between devices by JAX's collectives and lax.ppermute only.
A program may use at most 128 MiB of HBM per device.

v0:
```python
import math

import jax
import jax.numpy as jnp
from jax import lax
from jax.sharding import PartitionSpec as P

PATCH = 64
PSFW = 32
DEPTH = 64


BLEND = (0.125, 0.375, 0.375, 0.125)


def padded(cells, sides, width):
    for axis, dim in sides:
        count = lax.axis_size(axis)
        ends = count - 1
        head = lax.slice_in_dim(cells, 0, width, axis=dim)
        tail = lax.slice_in_dim(cells, cells.shape[dim] - width, cells.shape[dim], axis=dim)
        cells = jnp.concatenate(
            [
                lax.ppermute(tail, axis, [(i, (i + 1) % count) for i in range(ends)]),
                cells,
                lax.ppermute(head, axis, [((i + 1) % count, i) for i in range(ends)]),
            ],
            axis=dim,
        )
    return cells


def shortened(value):

    def short(part):
        return part.astype(jnp.bfloat16) if part.dtype == jnp.float32 else part

    return jax.tree.map(short, value)


def twiddle(rows, columns, offset, length):
    first = lax.broadcasted_iota(jnp.int32, (rows, columns), 0)
    second = lax.broadcasted_iota(jnp.int32, (rows, columns), 1) + offset
    phase = (first * second % length).astype(jnp.float32) * (2.0 * math.pi / length)
    return (jnp.cos(phase), jnp.sin(phase))


def trailing(table, data):
    return lax.dot_general(
        table, data, (((1,), (data.ndim - 1,)), ((), ())), preferred_element_type=jnp.float32
    )


def leading(data, table):
    return lax.dot_general(
        data, table, (((0,), (0,)), ((), ())), preferred_element_type=jnp.float32
    )


def forward(cube, length):
    count = cube.shape[-1]
    cosine, sine = twiddle(length, count, 0, length)
    cosine = cosine.astype(jnp.bfloat16)
    sine = sine.astype(jnp.bfloat16)
    real_part = trailing(cosine, cube).astype(jnp.bfloat16)
    imag_part = (-trailing(sine, cube)).astype(jnp.bfloat16)
    for _ in range(2):
        new_real = (trailing(cosine, real_part) + trailing(sine, imag_part)).astype(jnp.bfloat16)
        new_imag = (trailing(cosine, imag_part) - trailing(sine, real_part)).astype(jnp.bfloat16)
        real_part, imag_part = (new_real, new_imag)
    return (real_part, imag_part)


def multiply(left, right):
    left_re = left[0].astype(jnp.float32)
    left_im = left[1].astype(jnp.float32)
    right_re = right[0].astype(jnp.float32)
    right_im = right[1].astype(jnp.float32)
    real_part = left_re * right_re - left_im * right_im
    imag_part = left_re * right_im + left_im * right_re
    return (real_part.astype(jnp.bfloat16), imag_part.astype(jnp.bfloat16))


def inverse(spectrum, length):
    cosine, sine = twiddle(length, length, 0, length)
    cosine = cosine.astype(jnp.bfloat16)
    sine = sine.astype(jnp.bfloat16)
    scale = 1.0 / length
    real_part, imag_part = spectrum
    for _ in range(2):
        new_real = ((leading(real_part, cosine) - leading(imag_part, sine)) * scale).astype(
            jnp.bfloat16
        )
        new_imag = ((leading(imag_part, cosine) + leading(real_part, sine)) * scale).astype(
            jnp.bfloat16
        )
        real_part, imag_part = (new_real, new_imag)
    depth_cos, depth_sin = twiddle(length, DEPTH, PSFW // 2, length)
    result = (
        leading(real_part, depth_cos.astype(jnp.bfloat16))
        - leading(imag_part, depth_sin.astype(jnp.bfloat16))
    ) * scale
    return result.reshape(length, length * DEPTH)


def padded_along(values, axis, before, after):
    widths = [(0, 0)] * values.ndim
    widths[axis] = (before, after)
    return jnp.pad(values, widths)


def edge_bands(values, axis, width, inner):
    lower = lax.slice_in_dim(values, 0, width, axis=axis)
    upper = lax.slice_in_dim(values, width + inner, 2 * width + inner, axis=axis)
    return jnp.concatenate([lower, upper], axis)


def fold_bands(values, received, axis, width, inner):
    middle = lax.slice_in_dim(values, width, width + inner, axis=axis)
    total_len = received.shape[axis]
    lower = lax.slice_in_dim(received, 0, width, axis=axis)
    upper = lax.slice_in_dim(received, total_len - width, total_len, axis=axis)
    return (
        middle
        + padded_along(lower, axis, 0, inner - width)
        + padded_along(upper, axis, inner - width, 0)
    )


def body(image, psfs):
    patches = image.shape[0] // PATCH
    half = PSFW // 2
    tile = patches * PATCH
    length = PATCH + PSFW
    volume = PSFW * PSFW * PSFW
    weights = jnp.array(BLEND, jnp.float32)
    offset = lax.broadcasted_iota(
        jnp.int32, (patches, 2 * patches + 2), 1
    ) - 2 * lax.broadcasted_iota(jnp.int32, (patches, 2 * patches + 2), 0)
    across = jnp.zeros((patches, 2 * patches + 2), jnp.float32)
    for place in range(4):
        across = across + jnp.where(offset == place, weights[place], 0.0)
    cells = image.astype(jnp.bfloat16).reshape(patches, PATCH, PATCH, DEPTH)
    wider = padded(psfs, (("gx", 0), ("gy", 1)), 1)
    mixing = (
        (across[:, :, None] * weights[None, None, :])
        .reshape(patches, 4 * (2 * patches + 2))
        .astype(jnp.bfloat16)
    )
    blended = jnp.dot(
        mixing, wider.reshape(4 * (2 * patches + 2), volume), preferred_element_type=jnp.float32
    ).astype(jnp.bfloat16)
    blended = blended.reshape(patches, PSFW, PSFW, PSFW)

    def respond(pair):
        block, kernel = pair
        return inverse(multiply(forward(block, length), forward(kernel, length)), length)

    responses = lax.map(respond, (cells, blended))
    columns = length * DEPTH
    head = responses[:, :PATCH].reshape(tile, columns)
    tail = jnp.pad(responses[:, PATCH:], ((0, 0), (0, PATCH - PSFW), (0, 0))).reshape(tile, columns)
    extended = (
        jnp.pad(head, ((0, PSFW), (0, 0))) + jnp.pad(tail, ((PATCH, 0), (0, 0)))[: tile + PSFW]
    )
    band = half * DEPTH
    inner_cols = PATCH * DEPTH
    received = padded(
        edge_bands(extended, 1, band, inner_cols).astype(jnp.bfloat16), (("gy", 1),), band
    ).astype(jnp.float32)
    merged = fold_bands(extended, received, 1, band, inner_cols)
    received = padded(shortened(edge_bands(merged, 0, half, tile)), (("gx", 0),), half)
    result = fold_bands(merged, received, 0, half, tile)
    return result


def solution(mesh):
    placed = (P("gx", "gy"), P("gx", "gy", None, None))
    return jax.shard_map(body, mesh=mesh, in_specs=placed, out_specs=P("gx", "gy"), check_vma=False)
```

profile of v0, /device:TPU:19, one launch (start us, length us, event | category | flops | bytes accessed | tf_op | source)
XLA Modules:
  0.0 177.7 jit_solution(6803035581679325733)
XLA Ops:
  1.1 3.1 %collective-permute-start = (bf16[1,2,32,1024]{3,2,1,0:T(8,128)(2,1)S(1)}, bf16[1,2,32,1024]{3,2,1,0:T(8,128)(2,1)S(1)}, u32[]{:S(2)}, u32[]{:S(2)}) collective-permute-start(bf16[1,2,32,1024]{3,2,1,0:T(8,128)(2,1)S(1)} %get-tuple-element.81), channel_id=1, source_target_pairs={{0,8},{8,16},{16,24},{1,9},{9,17},{17,25},{2,10},{10,18},{18,26},{... | collective-permute-start | bytes 393224 | tf_op jit(solution)/shard_map/ppermute | solution.py:24
  8.5 2.4 %collective-permute-done.1 = bf16[1,2,32,1024]{3,2,1,0:T(8,128)(2,1)S(1)} collective-permute-done((bf16[1,2,32,1024]{3,2,1,0:T(8,128)(2,1)S(1)}, bf16[1,2,32,1024]{3,2,1,0:T(8,128)(2,1)S(1)}, u32[]{:S(2)}, u32[]{:S(2)}) %collective-permute-start.1) | collective-permute-done | bytes 131104 | tf_op jit(solution)/shard_map/ppermute | solution.py:26
  12.7 5.2 %collective-permute-start.2 = (bf16[6,1,32,1024]{3,2,1,0:T(8,128)(2,1)}, bf16[6,1,32,1024]{3,2,1,0:T(8,128)(2,1)S(1)}, u32[]{:S(2)}, u32[]{:S(2)}) collective-permute-start(bf16[6,1,32,1024]{3,2,1,0:T(8,128)(2,1)} %get-tuple-element.78), channel_id=1, source_target_pairs={{0,1},{1,2},{2,3},{3,4},{4,5},{5,6},{6,7},{8,9},{9,10},{10,11},{11... | collective-permute-start | bytes 1179656 | tf_op jit(solution)/shard_map/ppermute | solution.py:24
  20.2 2.3 %reshape.79 = bf16[2,64,64,64]{3,2,1,0:T(8,128)(2,1)S(1)} reshape(bf16[128,4096]{1,0:T(8,128)(2,1)S(1)} %convert_element_type.343) | data formatting | bytes 2097152 | tf_op jit(solution)/shard_map/reshape | solution.py:143
  22.9 4.4 %collective-permute-done.3 = bf16[6,1,32,1024]{3,2,1,0:T(8,128)(2,1)} collective-permute-done((bf16[6,1,32,1024]{3,2,1,0:T(8,128)(2,1)}, bf16[6,1,32,1024]{3,2,1,0:T(8,128)(2,1)}, u32[]{:S(2)}, u32[]{:S(2)}) %collective-permute-start.3) | collective-permute-done | bytes 393248 | tf_op jit(solution)/shard_map/ppermute | solution.py:26
  30.4 105.7 %while.12 = (s32[]{:T(128)}, f32[2,96,6144]{1,2,0:T(8,128)}, bf16[2,64,64,64]{3,2,1,0:T(8,128)(2,1)S(1)}, bf16[2,32,32,32]{3,2,1,0:T(8,128)(2,1)S(1)}, s32[]{:T(128)}) while((s32[]{:T(128)}, f32[2,96,6144]{1,2,0:T(8,128)}, bf16[2,64,64,64]{3,2,1,0:T(8,128)(2,1)S(1)}, bf16[2,32,32,32]{3,2,1,0:T(8,128)(2,1)S(1)}, s32[]{:T(128)}) %tuple.35), condition=%wide.region_1.2_spmd, body=%wide.region_0.1_spmd.sunk | while | flops 2791944192 | bytes 191759440 | solution.py:159
  44.0 3.1 %fusion.367 = (bf16[96,96,96]{2,0,1:T(8,128)(2,1)S(1)}, bf16[96,96,96]{2,0,1:T(8,128)(2,1)S(1)}) fusion(bf16[96,96,96]{2,0,1:T(8,128)(2,1)S(1)} %add_convert_fusion.8, bf16[96,96,96]{2,0,1:T(8,128)(2,1)S(1)} %subtract_convert_fusion.10, bf16[96,96,96]{2,0,1:T(8,128)(2,1)S(1)} %subtract_convert_fusion.11, f32[96,96,96]{2,0,1:T(8,128)S(1)} %fusion.366, ...), kind=kOutput, calls=%fused_computation.5.clone.1 | convolution fusion | flops 69040128 | bytes 12976128 | tf_op jit(solution)/shard_map/while/body/eval_jaxpr/dot_general | solution.py:49
  49.4 2.6 %multiply_convert_fusion.9 = bf16[96,96,96]{2,1,0:T(8,128)(2,1)} fusion(f32[96,96,96]{2,1,0:T(8,128)S(1)} %fusion.368, bf16[96,96,96]{2,0,1:T(8,128)(2,1)S(1)} %get-tuple-element.110), kind=kOutput, calls=%fused_computation.10.clone.1 | convolution fusion | flops 172615680 | bytes 7077888 | tf_op jit(solution)/shard_map/while/body/eval_jaxpr/dot_general | solution.py:55
  51.9 3.9 %copy.90 = bf16[96,96,96]{0,2,1:T(8,128)(2,1)S(1)} copy(bf16[96,96,96]{2,1,0:T(8,128)(2,1)} %multiply_convert_fusion.9) | data formatting | bytes 3538944 | tf_op jit(solution)/shard_map/while/body/eval_jaxpr/convert_element_type | solution.py:94
  55.9 2.8 %fusion.370 = f32[96,96,96]{2,1,0:T(8,128)S(1)} fusion(bf16[96,96,96]{2,0,1:T(8,128)(2,1)} %copy-done), kind=kOutput, calls=%fused_computation.82.clone.1 | convolution fusion | flops 169961472 | bytes 5308416 | tf_op jit(solution)/shard_map/while/body/eval_jaxpr/dot_general | solution.py:55
  58.7 2.5 %multiply_convert_fusion.10 = bf16[96,96,96]{2,1,0:T(8,128)(2,1)} fusion(f32[96,96,96]{2,1,0:T(8,128)S(1)} %fusion.370, bf16[96,96,96]{2,0,1:T(8,128)(2,1)S(1)} %copy-done.3), kind=kOutput, calls=%fused_computation.11.clone.1 | convolution fusion | flops 172615680 | bytes 7077888 | tf_op jit(solution)/shard_map/while/body/eval_jaxpr/dot_general | solution.py:55
  61.2 5.0 %copy.91 = bf16[96,96,96]{0,2,1:T(8,128)(2,1)} copy(bf16[96,96,96]{2,1,0:T(8,128)(2,1)} %multiply_convert_fusion.10) | data formatting | bytes 3538944 | tf_op jit(solution)/shard_map/while/body/eval_jaxpr/convert_element_type | solution.py:91
  66.2 2.6 %fusion.372 = f32[96,96,96]{2,1,0:T(8,128)S(1)} fusion(bf16[96,96,96]{0,2,1:T(8,128)(2,1)} %copy.91), kind=kOutput, calls=%fused_computation.81.clone.1 | convolution fusion | flops 169961472 | bytes 5308416 | tf_op jit(solution)/shard_map/while/body/eval_jaxpr/dot_general | solution.py:55
  75.2 4.2 %copy.92 = f32[96,96,64]{0,2,1:T(8,128)} copy(f32[96,96,64]{1,2,0:T(8,128)S(1)} %subtract_multiply_fusion.2) | data formatting | bytes 4718592 | tf_op jit(solution)/shard_map/while/body/eval_jaxpr/mul | solution.py:99
  79.4 3.9 %constant_dynamic-update-slice_fusion.5 = f32[2,96,6144]{1,2,0:T(8,128)} fusion(f32[2,96,6144]{1,2,0:T(8,128)} %get-tuple-element.117, f32[1,96,6144]{1,2,0:T(8,128)} %bitcast.185, s32[]{:T(128)S(6)} %copy.98), kind=kLoop, calls=%fused_computation.133.clone.1 | loop fusion | bytes 6291460 | tf_op jit(solution)/shard_map/while/body/jit(dynamic_update_index_in_dim)/dynamic_update_slice | solution.py:159
  96.8 3.1 %fusion.367 = (bf16[96,96,96]{2,0,1:T(8,128)(2,1)S(1)}, bf16[96,96,96]{2,0,1:T(8,128)(2,1)S(1)}) fusion(bf16[96,96,96]{2,0,1:T(8,128)(2,1)S(1)} %add_convert_fusion.8, bf16[96,96,96]{2,0,1:T(8,128)(2,1)S(1)} %subtract_convert_fusion.10, bf16[96,96,96]{2,0,1:T(8,128)(2,1)S(1)} %subtract_convert_fusion.11, f32[96,96,96]{2,0,1:T(8,128)S(1)} %fusion.366, ...), kind=kOutput, calls=%fused_computation.5.clone.1 | convolution fusion | flops 69040128 | bytes 12976128 | tf_op jit(solution)/shard_map/while/body/eval_jaxpr/dot_general | solution.py:49
  102.1 2.6 %multiply_convert_fusion.9 = bf16[96,96,96]{2,1,0:T(8,128)(2,1)} fusion(f32[96,96,96]{2,1,0:T(8,128)S(1)} %fusion.368, bf16[96,96,96]{2,0,1:T(8,128)(2,1)S(1)} %get-tuple-element.110), kind=kOutput, calls=%fused_computation.10.clone.1 | convolution fusion | flops 172615680 | bytes 7077888 | tf_op jit(solution)/shard_map/while/body/eval_jaxpr/dot_general | solution.py:55
  104.6 3.9 %copy.90 = bf16[96,96,96]{0,2,1:T(8,128)(2,1)S(1)} copy(bf16[96,96,96]{2,1,0:T(8,128)(2,1)} %multiply_convert_fusion.9) | data formatting | bytes 3538944 | tf_op jit(solution)/shard_map/while/body/eval_jaxpr/convert_element_type | solution.py:94
  108.6 2.8 %fusion.370 = f32[96,96,96]{2,1,0:T(8,128)S(1)} fusion(bf16[96,96,96]{2,0,1:T(8,128)(2,1)} %copy-done), kind=kOutput, calls=%fused_computation.82.clone.1 | convolution fusion | flops 169961472 | bytes 5308416 | tf_op jit(solution)/shard_map/while/body/eval_jaxpr/dot_general | solution.py:55
  111.4 2.5 %multiply_convert_fusion.10 = bf16[96,96,96]{2,1,0:T(8,128)(2,1)} fusion(f32[96,96,96]{2,1,0:T(8,128)S(1)} %fusion.370, bf16[96,96,96]{2,0,1:T(8,128)(2,1)S(1)} %copy-done.3), kind=kOutput, calls=%fused_computation.11.clone.1 | convolution fusion | flops 172615680 | bytes 7077888 | tf_op jit(solution)/shard_map/while/body/eval_jaxpr/dot_general | solution.py:55
  113.9 5.0 %copy.91 = bf16[96,96,96]{0,2,1:T(8,128)(2,1)} copy(bf16[96,96,96]{2,1,0:T(8,128)(2,1)} %multiply_convert_fusion.10) | data formatting | bytes 3538944 | tf_op jit(solution)/shard_map/while/body/eval_jaxpr/convert_element_type | solution.py:91
  118.9 2.6 %fusion.372 = f32[96,96,96]{2,1,0:T(8,128)S(1)} fusion(bf16[96,96,96]{0,2,1:T(8,128)(2,1)} %copy.91), kind=kOutput, calls=%fused_computation.81.clone.1 | convolution fusion | flops 169961472 | bytes 5308416 | tf_op jit(solution)/shard_map/while/body/eval_jaxpr/dot_general | solution.py:55
  127.9 4.2 %copy.92 = f32[96,96,64]{0,2,1:T(8,128)} copy(f32[96,96,64]{1,2,0:T(8,128)S(1)} %subtract_multiply_fusion.2) | data formatting | bytes 4718592 | tf_op jit(solution)/shard_map/while/body/eval_jaxpr/mul | solution.py:99
  132.1 3.9 %constant_dynamic-update-slice_fusion.5 = f32[2,96,6144]{1,2,0:T(8,128)} fusion(f32[2,96,6144]{1,2,0:T(8,128)} %get-tuple-element.117, f32[1,96,6144]{1,2,0:T(8,128)} %bitcast.185, s32[]{:T(128)S(6)} %copy.98), kind=kLoop, calls=%fused_computation.133.clone.1 | loop fusion | bytes 6291460 | tf_op jit(solution)/shard_map/while/body/jit(dynamic_update_index_in_dim)/dynamic_update_slice | solution.py:159
  136.0 7.1 %slice.73 = f32[2,32,6144]{1,2,0:T(8,128)} slice(f32[2,96,6144]{1,2,0:T(8,128)} %get-tuple-element.59), slice={[0:2], [64:96], [0:6144]} | slice | bytes 3145728 | tf_op jit(solution)/shard_map/slice | solution.py:162
  143.1 4.4 %copy.33 = f32[2,64,6144]{2,1,0:T(8,128)S(1)} copy(f32[2,64,6144]{1,2,0:T(8,128)} %bitcast.186) | data formatting | bytes 6291456 | tf_op jit(solution)/shard_map/slice | solution.py:161
  147.5 5.5 %copy.41 = f32[2,32,6144]{2,1,0:T(8,128)} copy(f32[2,32,6144]{1,2,0:T(8,128)} %slice.73) | data formatting | bytes 3145728
  157.3 2.4 %collective-permute-start.5 = (bf16[160,1024]{1,0:T(8,128)(2,1)S(1)}, bf16[160,1024]{1,0:T(8,128)(2,1)S(1)}, u32[]{:S(2)}, u32[]{:S(2)}) collective-permute-start(bf16[160,1024]{1,0:T(8,128)(2,1)S(1)} %get-tuple-element.75), channel_id=1, source_target_pairs={{1,0},{2,1},{3,2},{4,3},{5,4},{6,5},{7,6},{9,8},{10,9},{11,10},{12... | collective-permute-start | bytes 983048 | tf_op jit(solution)/shard_map/ppermute | solution.py:26
  161.3 4.4 %collective-permute-done.5 = bf16[160,1024]{1,0:T(8,128)(2,1)S(1)} collective-permute-done((bf16[160,1024]{1,0:T(8,128)(2,1)S(1)}, bf16[160,1024]{1,0:T(8,128)(2,1)S(1)}, u32[]{:S(2)}, u32[]{:S(2)}) %collective-permute-start.5) | collective-permute-done | bytes 327712 | tf_op jit(solution)/shard_map/ppermute | solution.py:26
  166.6 2.2 %collective-permute-start.6 = (bf16[16,4096]{1,0:T(8,128)(2,1)S(1)}, bf16[16,4096]{1,0:T(8,128)(2,1)S(1)}, u32[]{:S(2)}, u32[]{:S(2)}) collective-permute-start(bf16[16,4096]{1,0:T(8,128)(2,1)S(1)} %get-tuple-element.76), channel_id=1, source_target_pairs={{0,8},{8,16},{16,24},{1,9},{9,17},{17,25},{2,10},{10,18},{18,26},{... | collective-permute-start | bytes 393224 | tf_op jit(solution)/shard_map/ppermute | solution.py:24
  168.8 3.1 %collective-permute-start.7 = (bf16[16,4096]{1,0:T(8,128)(2,1)S(1)}, bf16[16,4096]{1,0:T(8,128)(2,1)S(1)}, u32[]{:S(2)}, u32[]{:S(2)}) collective-permute-start(bf16[16,4096]{1,0:T(8,128)(2,1)S(1)} %get-tuple-element.77), channel_id=1, source_target_pairs={{8,0},{16,8},{24,16},{9,1},{17,9},{25,17},{10,2},{18,10},{26,18},{... | collective-permute-start | bytes 393224 | tf_op jit(solution)/shard_map/ppermute | solution.py:26
  172.8 3.4 %collective-permute-done.7 = bf16[16,4096]{1,0:T(8,128)(2,1)S(1)} collective-permute-done((bf16[16,4096]{1,0:T(8,128)(2,1)S(1)}, bf16[16,4096]{1,0:T(8,128)(2,1)S(1)}, u32[]{:S(2)}, u32[]{:S(2)}) %collective-permute-start.7) | collective-permute-done | bytes 131104 | tf_op jit(solution)/shard_map/ppermute | solution.py:26
  (122 shorter events, 65.8 us)
Async XLA Ops:
  0.0 19.9 %copy-start.11 = (f32[4]{0:T(128)S(1)}, f32[4]{0:T(128)}, u32[]{:S(2)}) copy-start(f32[4]{0:T(128)} %constant.87.clone) | copy-start | bytes 52
  0.0 20.1 %copy-start.9 = (f32[128,4096]{1,0:T(8,128)S(1)}, f32[128,4096]{1,0:T(8,128)}, u32[]{:S(2)}) copy-start(f32[128,4096]{1,0:T(8,128)} %param.5) | copy-start | bytes 6291460
  1.1 6.3 %collective-permute-start = (bf16[1,2,32,1024]{3,2,1,0:T(8,128)(2,1)S(1)}, bf16[1,2,32,1024]{3,2,1,0:T(8,128)(2,1)S(1)}, u32[]{:S(2)}, u32[]{:S(2)}) collective-permute-start(bf16[1,2,32,1024]{3,2,1,0:T(8,128)(2,1)S(1)} %get-tuple-element.81), channel_id=1, source_target_pairs={{0,8},{8,16},{16,24},{1,9},{9,17},{17,25},{2,10},{10,18},{18,26},{... | collective-permute-start | bytes 393224 | tf_op jit(solution)/shard_map/ppermute | solution.py:24
  4.3 6.6 %collective-permute-start.1 = (bf16[1,2,32,1024]{3,2,1,0:T(8,128)(2,1)S(1)}, bf16[1,2,32,1024]{3,2,1,0:T(8,128)(2,1)S(1)}, u32[]{:S(2)}, u32[]{:S(2)}) collective-permute-start(bf16[1,2,32,1024]{3,2,1,0:T(8,128)(2,1)S(1)} %get-tuple-element.80), channel_id=1, source_target_pairs={{8,0},{16,8},{24,16},{9,1},{17,9},{25,17},{10,2},{18,10},{26,18},{... | collective-permute-start | bytes 393224 | tf_op jit(solution)/shard_map/ppermute | solution.py:26
  10.9 0.9 copy-start.8
  12.7 10.2 %collective-permute-start.2 = (bf16[6,1,32,1024]{3,2,1,0:T(8,128)(2,1)}, bf16[6,1,32,1024]{3,2,1,0:T(8,128)(2,1)S(1)}, u32[]{:S(2)}, u32[]{:S(2)}) collective-permute-start(bf16[6,1,32,1024]{3,2,1,0:T(8,128)(2,1)} %get-tuple-element.78), channel_id=1, source_target_pairs={{0,1},{1,2},{2,3},{3,4},{4,5},{5,6},{6,7},{8,9},{9,10},{10,11},{11... | collective-permute-start | bytes 1179656 | tf_op jit(solution)/shard_map/ppermute | solution.py:24
  17.9 9.4 %collective-permute-start.3 = (bf16[6,1,32,1024]{3,2,1,0:T(8,128)(2,1)}, bf16[6,1,32,1024]{3,2,1,0:T(8,128)(2,1)}, u32[]{:S(2)}, u32[]{:S(2)}) collective-permute-start(bf16[6,1,32,1024]{3,2,1,0:T(8,128)(2,1)} %get-tuple-element.79), channel_id=1, source_target_pairs={{1,0},{2,1},{3,2},{4,3},{5,4},{6,5},{7,6},{9,8},{10,9},{11,10},{12... | collective-permute-start | bytes 1179656 | tf_op jit(solution)/shard_map/ppermute | solution.py:26
  30.5 1.8 copy-start.4
  30.6 1.8 copy-start.6
  47.1 1.5 copy-start
  47.1 2.2 %copy-start.2 = (bf16[96,96,96]{2,0,1:T(8,128)(2,1)}, bf16[96,96,96]{2,0,1:T(8,128)(2,1)S(1)}, u32[]{:S(2)}) copy-start(bf16[96,96,96]{2,0,1:T(8,128)(2,1)S(1)} %get-tuple-element.109) | copy-start | bytes 5308420 | tf_op jit(solution)/shard_map/while
  55.9 2.8 %copy-start.3 = (bf16[96,96,96]{2,0,1:T(8,128)(2,1)S(1)}, bf16[96,96,96]{2,0,1:T(8,128)(2,1)}, u32[]{:S(2)}) copy-start(bf16[96,96,96]{2,0,1:T(8,128)(2,1)} %copy-done.2) | copy-start | bytes 5308420 | tf_op jit(solution)/shard_map/while
  69.8 1.7 copy-start.1
  79.4 3.9 %copy-start.5 = (bf16[2,64,64,64]{3,2,1,0:T(8,128)(2,1)S(1)}, bf16[2,64,64,64]{3,2,1,0:T(8,128)(2,1)}, u32[]{:S(2)}) copy-start(bf16[2,64,64,64]{3,2,1,0:T(8,128)(2,1)} %copy-done.4) | copy-start | bytes 3145732 | tf_op jit(solution)/shard_map/while
  79.4 3.9 %copy-start.7 = (bf16[2,32,32,32]{3,2,1,0:T(8,128)(2,1)S(1)}, bf16[2,32,32,32]{3,2,1,0:T(8,128)(2,1)}, u32[]{:S(2)}) copy-start(bf16[2,32,32,32]{3,2,1,0:T(8,128)(2,1)} %copy-done.6) | copy-start | bytes 393220 | tf_op jit(solution)/shard_map/while
  83.3 1.7 copy-start.4
  83.3 1.8 copy-start.6
  99.8 1.5 copy-start
  99.9 2.2 %copy-start.2 = (bf16[96,96,96]{2,0,1:T(8,128)(2,1)}, bf16[96,96,96]{2,0,1:T(8,128)(2,1)S(1)}, u32[]{:S(2)}) copy-start(bf16[96,96,96]{2,0,1:T(8,128)(2,1)S(1)} %get-tuple-element.109) | copy-start | bytes 5308420 | tf_op jit(solution)/shard_map/while
  108.6 2.8 %copy-start.3 = (bf16[96,96,96]{2,0,1:T(8,128)(2,1)S(1)}, bf16[96,96,96]{2,0,1:T(8,128)(2,1)}, u32[]{:S(2)}) copy-start(bf16[96,96,96]{2,0,1:T(8,128)(2,1)} %copy-done.2) | copy-start | bytes 5308420 | tf_op jit(solution)/shard_map/while
  122.5 1.7 copy-start.1
  132.1 3.9 %copy-start.5 = (bf16[2,64,64,64]{3,2,1,0:T(8,128)(2,1)S(1)}, bf16[2,64,64,64]{3,2,1,0:T(8,128)(2,1)}, u32[]{:S(2)}) copy-start(bf16[2,64,64,64]{3,2,1,0:T(8,128)(2,1)} %copy-done.4) | copy-start | bytes 3145732 | tf_op jit(solution)/shard_map/while
  132.1 3.9 %copy-start.7 = (bf16[2,32,32,32]{3,2,1,0:T(8,128)(2,1)S(1)}, bf16[2,32,32,32]{3,2,1,0:T(8,128)(2,1)}, u32[]{:S(2)}) copy-start(bf16[2,32,32,32]{3,2,1,0:T(8,128)(2,1)} %copy-done.6) | copy-start | bytes 393220 | tf_op jit(solution)/shard_map/while
  155.4 5.9 %collective-permute-start.4 = (bf16[160,1024]{1,0:T(8,128)(2,1)S(1)}, bf16[160,1024]{1,0:T(8,128)(2,1)S(1)}, u32[]{:S(2)}, u32[]{:S(2)}) collective-permute-start(bf16[160,1024]{1,0:T(8,128)(2,1)S(1)} %get-tuple-element.74), channel_id=1, source_target_pairs={{0,1},{1,2},{2,3},{3,4},{4,5},{5,6},{6,7},{8,9},{9,10},{10,11},{11... | collective-permute-start | bytes 983048 | tf_op jit(solution)/shard_map/ppermute | solution.py:24
  157.3 8.7 %copy-start.10 = (pred[4096]{0:T(1024)(128)(4,1)S(1)}, pred[4096]{0:T(1024)(128)(4,1)}, u32[]{:S(2)}) copy-start(pred[4096]{0:T(1024)(128)(4,1)} %constant.85.clone.1) | copy-start | bytes 12292
  157.3 8.4 %collective-permute-start.5 = (bf16[160,1024]{1,0:T(8,128)(2,1)S(1)}, bf16[160,1024]{1,0:T(8,128)(2,1)S(1)}, u32[]{:S(2)}, u32[]{:S(2)}) collective-permute-start(bf16[160,1024]{1,0:T(8,128)(2,1)S(1)} %get-tuple-element.75), channel_id=1, source_target_pairs={{1,0},{2,1},{3,2},{4,3},{5,4},{6,5},{7,6},{9,8},{10,9},{11,10},{12... | collective-permute-start | bytes 983048 | tf_op jit(solution)/shard_map/ppermute | solution.py:26
  166.6 6.2 %collective-permute-start.6 = (bf16[16,4096]{1,0:T(8,128)(2,1)S(1)}, bf16[16,4096]{1,0:T(8,128)(2,1)S(1)}, u32[]{:S(2)}, u32[]{:S(2)}) collective-permute-start(bf16[16,4096]{1,0:T(8,128)(2,1)S(1)} %get-tuple-element.76), channel_id=1, source_target_pairs={{0,8},{8,16},{16,24},{1,9},{9,17},{17,25},{2,10},{10,18},{18,26},{... | collective-permute-start | bytes 393224 | tf_op jit(solution)/shard_map/ppermute | solution.py:24
  168.8 7.4 %collective-permute-start.7 = (bf16[16,4096]{1,0:T(8,128)(2,1)S(1)}, bf16[16,4096]{1,0:T(8,128)(2,1)S(1)}, u32[]{:S(2)}, u32[]{:S(2)}) collective-permute-start(bf16[16,4096]{1,0:T(8,128)(2,1)S(1)} %get-tuple-element.77), channel_id=1, source_target_pairs={{8,0},{16,8},{24,16},{9,1},{17,9},{25,17},{10,2},{18,10},{26,18},{... | collective-permute-start | bytes 393224 | tf_op jit(solution)/shard_map/ppermute | solution.py:26
where the time goes:
time: 179 us; the launch traced here: 178 us
  matrix products  67.5 us (38%)
  local copies, waits for them, and re-layouts  64.3 us (36%)
  starting transfers between devices  22 us (12%)
  waiting for transfers between devices  18.4 us (10%)
  other arithmetic  4.6 us (3%)
    dot_general x20, matrix products, leading(): lax.dot_general(data, table, (((0,), (0,)), ((), ())), preferred_element_...  34.2 us
    dot_general x40, matrix products, trailing(): lax.dot_general(table, data, (((1,), (data.ndim - 1,)), ((), ())), prefer...  32.9 us
    ppermute x4, waiting for transfers between devices, padded(): lax.ppermute(head, axis, [((i + 1) % count, i) for i in range(ends)])  14.6 us
    ppermute x4, starting transfers between devices, padded(): lax.ppermute(tail, axis, [(i, (i + 1) % count) for i in range(ends)])  12.4 us
    convert_element_type x2, local copies, waits for them, and re-layouts, inverse(): ((leading(real_part, cosine) - leading(imag_part, sine)) * scale).astype(...  10 us
    ppermute x4, starting transfers between devices, padded(): lax.ppermute(head, axis, [((i + 1) % count, i) for i in range(ends)])  9.57 us
    unnamed x12, local copies, waits for them, and re-layouts  8.38 us
    mul x2, local copies, waits for them, and re-layouts, inverse(): (leading(real_part, depth_cos.astype(jnp.bfloat16)) - leading(imag_part,...  8.38 us
  transfers between devices with their start and end apart: 8, of which 8 were waited for; matrix products, arithmetic and copies ran while one was open for 2% of the time, Pallas kernels for 0%

commit v1 on v0

v1 whole, which is shorter than its diff:
```python
import math

import jax
import jax.numpy as jnp
import ml_dtypes
import numpy as np
from jax import lax
from jax.experimental import pallas as pl
from jax.experimental.pallas import tpu as pltpu
from jax.sharding import PartitionSpec as P

PATCH = 64
PSFW = 32
DEPTH = 64
BLEND = (0.125, 0.375, 0.375, 0.125)

HALF = PSFW // 2
LONG = PATCH + PSFW
KX = LONG // 2
KZ = DEPTH + HALF
LANES = 128
YPER = LANES // DEPTH
PPER = LANES // PSFW
YROWS = PATCH // YPER
PROWS = PSFW // PPER
OROWS = LONG // YPER
F32 = jnp.float32
BF16 = jnp.bfloat16


def constant(values):
    return jnp.asarray(np.asarray(values, np.float32).astype(ml_dtypes.bfloat16))


def angle(k, n, length):
    return 2.0 * math.pi * np.outer(k, n) / length


def complex_block(theta, sign):
    cosine, sine = np.cos(theta), sign * np.sin(theta)
    return np.stack([np.stack([cosine, -sine], 1), np.stack([sine, cosine], 1)], 0)


def x_forward(count):
    theta = angle(np.arange(KX) + 0.5, np.arange(count), LONG)
    return np.concatenate([np.cos(theta), -np.sin(theta)], 0)


def z_forward(count, per):
    block = complex_block(angle(np.arange(KZ), np.arange(count), KZ), -1.0)
    table = np.zeros((2, per, count, per, 2, LANES))
    for y in range(per):
        table[:, y, :, y, :, :KZ] = block.transpose(2, 3, 0, 1)
    return table.reshape(2 * per * count, per * 2 * LANES)


def y_forward(count, per):
    block = complex_block(angle(np.arange(LONG), np.arange(count), LONG), -1.0)
    block = block.reshape(2, LONG, 2, count // per, per).transpose(0, 1, 4, 2, 3)
    return block.reshape(2 * LONG, 2 * count)


def y_inverse():
    block = complex_block(angle(np.arange(LONG), np.arange(LONG), LONG).T, 1.0) / LONG
    block = block.reshape(2, OROWS, YPER, 2 * LONG).transpose(2, 0, 1, 3)
    return block.reshape(2 * LONG, 2 * LONG)


def z_inverse():
    block = complex_block(angle(np.arange(DEPTH) + HALF, np.arange(KZ), KZ), 1.0) / KZ
    table = np.zeros((YPER, 2, LANES, 2, YPER, DEPTH))
    for y in range(YPER):
        table[y, :, :KZ, :, y, :] = block.transpose(2, 3, 0, 1)
    return table.reshape(YPER * 2 * LANES, 2 * YPER * DEPTH)


def x_inverse(patches):
    theta = angle(np.arange(LONG), np.arange(KX) + 0.5, LONG)
    block = np.stack([np.cos(theta), -np.sin(theta)], 1) * (2.0 / LONG)
    rows = patches * PATCH
    table = np.zeros((rows + PSFW, patches, 2, KX))
    for p in range(patches):
        table[p * PATCH : p * PATCH + LONG, p] = block
    table = np.concatenate([table[HALF : HALF + rows], table[:HALF], table[HALF + rows :]], 0)
    return table.reshape(rows + PSFW, patches * 2 * KX)


def dot(a, b):
    return jnp.dot(a, b, preferred_element_type=F32)


def full(shape):
    return pl.BlockSpec(shape, lambda *_: (0,) * len(shape))


def image_kernel(image_ref, tx_ref, tz_ref, ty_ref, out_ref, swap, mid):
    tile = 2 * LANES
    rows = 2 * KX

    def along_x(t, _):
        cells = image_ref[:, pl.ds(pl.multiple_of(t * tile, tile), tile)].astype(BF16)
        result = dot(tx_ref[...], cells)
        for h in range(2):
            swap[pl.ds(2 * t + h, rows, stride=YROWS), :] = result[:, h * LANES : (h + 1) * LANES]
        return 0

    lax.fori_loop(0, PATCH * DEPTH // tile, along_x, 0, unroll=4)

    half = KX * YROWS
    chunk = 8 * YROWS

    def along_z(t, _):
        start = pl.multiple_of(t * chunk, chunk)
        left = jnp.concatenate(
            [swap[pl.ds(start, chunk), :], swap[pl.ds(half + start, chunk), :]], 1
        ).astype(BF16)
        mid[pl.ds(start, chunk), :] = dot(left, tz_ref[...]).astype(BF16)
        return 0

    lax.fori_loop(0, half // chunk, along_z, 0, unroll=2)

    def along_y(t, _):
        pieces = []
        for h in range(2):
            rows_at = pl.ds(pl.multiple_of((2 * t + h) * YROWS, YROWS), YROWS)
            pieces.append(
                jnp.concatenate(
                    [mid[rows_at, b * LANES : (b + 1) * LANES] for b in range(2 * YPER)], 0
                )
            )
        result = dot(ty_ref[...], jnp.concatenate(pieces, 1)).astype(BF16)
        for h in range(2):
            out_ref[2 * t + h] = result[:, h * LANES : (h + 1) * LANES]
        return 0

    lax.fori_loop(0, KX // 2, along_y, 0, unroll=2)


def image_forward(image, patch):
    tables = (
        constant(x_forward(PATCH)),
        constant(z_forward(DEPTH, YPER)),
        constant(y_forward(PATCH, YPER)),
    )
    return pl.pallas_call(
        image_kernel,
        grid=(1,),
        in_specs=[pl.BlockSpec((PATCH, image.shape[1]), lambda _: (patch, 0))]
        + [full(t.shape) for t in tables],
        out_specs=full((KX, 2 * LONG, LANES)),
        out_shape=jax.ShapeDtypeStruct((KX, 2 * LONG, LANES), BF16),
        scratch_shapes=[
            pltpu.VMEM((2 * KX * YROWS, LANES), F32),
            pltpu.VMEM((KX * YROWS, 2 * YPER * LANES), BF16),
        ],
        compiler_params=pltpu.CompilerParams(vmem_limit_bytes=24 << 20),
        cost_estimate=pl.CostEstimate(
            flops=4_000_000_000, bytes_accessed=4_000_000, transcendentals=0
        ),
        name="image_forward",
    )(image, *tables)


def blend_kernel(psfs_ref, before_ref, after_ref, first_ref, last_ref):
    count = psfs_ref.shape[0]
    for column, out in ((0, first_ref), (1, last_ref)):
        nodes = [before_ref[0, column]]
        nodes += [psfs_ref[i, column] for i in range(count)]
        nodes += [after_ref[0, column]]
        nodes = [n.astype(F32) for n in nodes]
        for p in range(count // 2):
            total = (nodes[2 * p] + nodes[2 * p + 3]) * BLEND[0]
            total += (nodes[2 * p + 1] + nodes[2 * p + 2]) * BLEND[1]
            out[p] = total.astype(BF16)


def blend_x(psfs, before, after):
    patches = psfs.shape[0] // 2
    shape = (patches,) + psfs.shape[2:]
    return pl.pallas_call(
        blend_kernel,
        out_shape=(jax.ShapeDtypeStruct(shape, BF16),) * 2,
        name="blend_x",
    )(psfs, before, after)


def respond_kernel(
    patches,
    *refs,
):
    spectra = refs[:patches]
    columns = refs[patches : patches + 4]
    tpx, tpz, tpy, tiy, tiz, tix = refs[patches + 4 : patches + 10]
    mid_ref, low_ref, high_ref = refs[patches + 10 : patches + 13]
    pswap, pmid, rows_y, grid_x = refs[patches + 13 :]
    tile = 2 * LANES

    for p in range(patches):
        for t in range(PSFW * PSFW // tile):
            data = jnp.concatenate([c[p, :, t * tile : (t + 1) * tile] for c in columns], 0)
            result = dot(tpx[...], data)
            for h in range(2):
                pswap[p, pl.ds(2 * t + h, 2 * KX, stride=PROWS), :] = result[
                    :, h * LANES : (h + 1) * LANES
                ]
    half = KX * PROWS
    for p in range(patches):
        left = jnp.concatenate([pswap[p, :half, :], pswap[p, half:, :]], 1).astype(BF16)
        for b in range(PPER):
            result = dot(left, tpz[:, b * tile : (b + 1) * tile])
            result = result.reshape(KX, PROWS, tile)
            both = jnp.concatenate([result[:, :, :LANES], result[:, :, LANES:]], 1)
            pmid[p, :, 2 * b * PROWS : 2 * (b + 1) * PROWS, :] = both.astype(BF16)

    def along_y(t, _):
        for p in range(patches):
            psf = dot(tpy[...], jnp.concatenate([pmid[p, 2 * t], pmid[p, 2 * t + 1]], 1))
            field = jnp.concatenate([spectra[p][2 * t], spectra[p][2 * t + 1]], 1).astype(F32)
            are, aim = field[:LONG], field[LONG:]
            bre, bim = psf[:LONG], psf[LONG:]
            product = jnp.concatenate([are * bre - aim * bim, are * bim + aim * bre], 0)
            back = dot(tiy[...], product.astype(BF16)).astype(BF16)
            for h in range(2):
                rows_at = pl.ds(pl.multiple_of((2 * t + h) * OROWS, OROWS), OROWS)
                for b in range(2 * YPER):
                    rows_y[p, rows_at, b * LANES : (b + 1) * LANES] = back[
                        b * OROWS : (b + 1) * OROWS, h * LANES : (h + 1) * LANES
                    ]
        return 0

    lax.fori_loop(0, KX // 2, along_y, 0, unroll=1)

    group = 8

    def along_z(t, _):
        for p in range(patches):
            start = pl.multiple_of(t * group * OROWS, group * OROWS)
            result = dot(rows_y[p, pl.ds(start, group * OROWS), :], tiz[...])
            for k in range(group):
                for c in range(2):
                    grid_x[p, c, pl.ds(t * group + k, OROWS, stride=KX), :] = result[
                        k * OROWS : (k + 1) * OROWS, c * LANES : (c + 1) * LANES
                    ]
        return 0

    lax.fori_loop(0, KX // group, along_z, 0)

    def along_x(t):
        pieces = []
        for p in range(patches):
            for c in range(2):
                parts = []
                for h in range(2):
                    start = (2 * t + h) * KX
                    if not isinstance(start, int):
                        start = pl.multiple_of(start, KX)
                    parts.append(grid_x[p, c, pl.ds(start, KX), :])
                pieces.append(jnp.concatenate(parts, 1).astype(BF16))
        return dot(tix[...], jnp.concatenate(pieces, 0))

    rim = HALF * DEPTH // tile
    inner = PATCH * DEPTH // tile
    for t in range(rim):
        low_ref[:, t * tile : (t + 1) * tile] = along_x(t).astype(BF16)
        high_ref[:, t * tile : (t + 1) * tile] = along_x(rim + inner + t).astype(BF16)

    def middle(t, _):
        mid_ref[:, pl.ds(pl.multiple_of(t * tile, tile), tile)] = along_x(rim + t)
        return 0

    lax.fori_loop(0, inner, middle, 0, unroll=2)


def respond(spectra, columns):
    patches = len(spectra)
    weighted = np.concatenate([w * x_forward(PSFW) for w in BLEND], 1)
    tables = (
        constant(weighted),
        constant(z_forward(PSFW, PPER)),
        constant(y_forward(PSFW, PPER)),
        constant(y_inverse()),
        constant(z_inverse()),
        constant(x_inverse(patches)),
    )
    rows = patches * PATCH + PSFW
    rim = (rows, HALF * DEPTH)
    operands = (*spectra, *columns, *tables)
    return pl.pallas_call(
        lambda *refs: respond_kernel(patches, *refs),
        out_shape=(
            jax.ShapeDtypeStruct((rows, PATCH * DEPTH), F32),
            jax.ShapeDtypeStruct(rim, BF16),
            jax.ShapeDtypeStruct(rim, BF16),
        ),
        scratch_shapes=[
            pltpu.VMEM((patches, 2 * KX * PROWS, LANES), F32),
            pltpu.VMEM((patches, KX, 2 * PSFW, LANES), BF16),
            pltpu.VMEM((patches, KX * OROWS, 2 * YPER * LANES), BF16),
            pltpu.VMEM((patches, 2, OROWS * KX, LANES), F32),
        ],
        compiler_params=pltpu.CompilerParams(vmem_limit_bytes=48 << 20),
        name="respond",
    )(*operands)


def rim_kernel(mid_ref, low_ref, high_ref, first_ref, last_ref):
    band = low_ref.shape[1]
    rows = mid_ref.shape[0] // 2
    for k, out in ((0, first_ref), (1, last_ref)):
        at = slice(k * rows, (k + 1) * rows)
        out[...] = mid_ref[at, :].astype(BF16)
        out[:, :band] = (mid_ref[at, :band] + low_ref[at, :].astype(F32)).astype(BF16)
        out[:, -band:] = (mid_ref[at, -band:] + high_ref[at, :].astype(F32)).astype(BF16)


def x_rims(mid, low, high):
    start = (mid.shape[0] - PSFW) // PSFW
    shape = jax.ShapeDtypeStruct((HALF, mid.shape[1]), BF16)
    return pl.pallas_call(
        rim_kernel,
        grid=(1,),
        in_specs=[
            pl.BlockSpec((PSFW, mid.shape[1]), lambda _: (start, 0)),
            pl.BlockSpec((PSFW, low.shape[1]), lambda _: (start, 0)),
            pl.BlockSpec((PSFW, high.shape[1]), lambda _: (start, 0)),
        ],
        out_specs=(full(shape.shape),) * 2,
        out_shape=(shape,) * 2,
        name="x_rims",
    )(mid, low, high)


def fold_kernel(mid_ref, low_ref, high_ref, before_ref, after_ref, out_ref):
    rows, band = out_ref.shape[0], low_ref.shape[1]
    out_ref[...] = mid_ref[...]
    out_ref[:, :band] += low_ref[...].astype(F32)
    out_ref[:, -band:] += high_ref[...].astype(F32)
    out_ref[:HALF, :] += before_ref[...].astype(F32)
    out_ref[rows - HALF :, :] += after_ref[...].astype(F32)


def fold(mid, low, high, before, after):
    rows = mid.shape[0] - PSFW
    return pl.pallas_call(
        fold_kernel,
        grid=(1,),
        in_specs=[
            pl.BlockSpec((rows, mid.shape[1]), lambda _: (0, 0)),
            pl.BlockSpec((rows, low.shape[1]), lambda _: (0, 0)),
            pl.BlockSpec((rows, high.shape[1]), lambda _: (0, 0)),
            full(before.shape),
            full(after.shape),
        ],
        out_specs=full((rows, mid.shape[1])),
        out_shape=jax.ShapeDtypeStruct((rows, mid.shape[1]), F32),
        compiler_params=pltpu.CompilerParams(vmem_limit_bytes=24 << 20),
        name="fold",
    )(mid, low, high, before, after)


def onward(value, axis):
    return lax.ppermute(value, axis, [(i, i + 1) for i in range(lax.axis_size(axis) - 1)])


def backward(value, axis):
    return lax.ppermute(value, axis, [(i + 1, i) for i in range(lax.axis_size(axis) - 1)])


def body(image, psfs):
    patches = image.shape[0] // PATCH
    before = onward(psfs[-1:], "gx")
    after = backward(psfs[:1], "gx")
    spectra = [image_forward(image, 0)]
    first, last = blend_x(psfs, before, after)
    left = onward(last, "gy")
    right = backward(first, "gy")
    spectra += [image_forward(image, p) for p in range(1, patches)]
    mid, low, high = respond(spectra, (left, first, last, right))
    from_left = onward(high, "gy")
    from_right = backward(low, "gy")
    first, last = x_rims(mid, from_left, from_right)
    before = onward(last, "gx")
    after = backward(first, "gx")
    return fold(mid, from_left, from_right, before, after)


def solution(mesh):
    placed = (P("gx", "gy"), P("gx", "gy", None, None))
    return jax.shard_map(body, mesh=mesh, in_specs=placed, out_specs=P("gx", "gy"), check_vma=False)
```

time: 179 us -> 84.8 us (0.47)
  matrix products: 67.5 us -> 0 us
  local copies, waits for them, and re-layouts: 64.3 us -> 10.5 us
  Pallas kernels: 0 us -> 38.6 us
  waiting for transfers between devices: 18.4 us -> 11 us
  other arithmetic: 4.6 us -> 0 us
    dot_general x61 -> x0, matrix products: 67.5 us -> none  [the longest x20 34.2 us: leading(): lax.dot_general(data, table, (((0,), (0,)), ((), ())), preferred_element_...]
    pallas_call x0 -> x6, Pallas kernels: none -> 38.6 us  [the longest x1 23.9 us: respond(): pl.pallas_call(lambda *refs: respond_kernel(patches, *refs), out_shape=(j...]
    convert_element_type x5 -> x0, local copies, waits for them, and re-layouts: 18 us -> none  [the longest x2 10 us: inverse(): ((leading(real_part, cosine) - leading(imag_part, sine)) * scale).astype(...]
    slice x7 -> x1, local copies, waits for them, and re-layouts: 13.6 us -> 0.98 us  [body(): after = backward(psfs[:1], 'gx')]
    mul x2 -> x0, local copies, waits for them, and re-layouts: 8.38 us -> none  [inverse(): (leading(real_part, depth_cos.astype(jnp.bfloat16)) - leading(imag_part,...]
    dynamic_update_slice x2 -> x0, local copies, waits for them, and re-layouts: 7.78 us -> none  [body(): responses = lax.map(respond, (cells, blended))]
    ppermute x8, waiting for transfers between devices: 18.4 us -> 11 us  [the longest x4 7.8 us: backward(): lax.ppermute(value, axis, [(i + 1, i) for i in range(lax.axis_size(axis)...]
    while x32 -> x0, local copies, waits for them, and re-layouts: 3.94 us -> none
  transfers between devices with their start and end apart: 8 -> 8, of which waited for: 8 -> 4; matrix products, arithmetic and copies ran while one was open for 2% -> 0% of each run, Pallas kernels for 0% -> 11%
where the time goes in v1:
time: 84.8 us; the launch traced here: 84.1 us
  Pallas kernels  38.6 us (46%)
  starting transfers between devices  23.6 us (28%)
  waiting for transfers between devices  11 us (13%)
  local copies, waits for them, and re-layouts  10.5 us (12%)
    pallas_call x1, Pallas kernels, respond(): pl.pallas_call(lambda *refs: respond_kernel(patches, *refs), out_shape=(j...  23.9 us
    ppermute x4, starting transfers between devices, onward(): lax.ppermute(value, axis, [(i, i + 1) for i in range(lax.axis_size(axis)...  14.4 us
    unnamed x48, local copies, waits for them, and re-layouts  9.53 us
    pallas_call x2, Pallas kernels, image_forward(): pl.pallas_call(image_kernel, grid=(1,), in_specs=[pl.BlockSpec((PATCH, im...  9.43 us
    ppermute x4, starting transfers between devices, backward(): lax.ppermute(value, axis, [(i + 1, i) for i in range(lax.axis_size(axis)...  9.2 us
    ppermute x4, waiting for transfers between devices, backward(): lax.ppermute(value, axis, [(i + 1, i) for i in range(lax.axis_size(axis)...  7.8 us
    ppermute x4, waiting for transfers between devices, onward(): lax.ppermute(value, axis, [(i, i + 1) for i in range(lax.axis_size(axis)...  3.22 us
    pallas_call x1, Pallas kernels, blend_x(): pl.pallas_call(blend_kernel, out_shape=(jax.ShapeDtypeStruct(shape, BF16)...  1.94 us
  transfers between devices with their start and end apart: 8, of which 4 were waited for; matrix products, arithmetic and copies ran while one was open for 0% of the time, Pallas kernels for 11%

profile of v1, /device:TPU:19, one launch (start us, length us, event | category | flops | bytes accessed | tf_op | source)
XLA Modules:
  0.0 84.1 jit_solution(11012035504421285679)
XLA Ops:
  0.0 1.0 %fusion = (bf16[1,2,32,1024]{3,2,1,0:T(8,128)(2,1)S(1)}, bf16[1,2,32,1024]{3,2,1,0:T(8,128)(2,1)S(1)}) fusion(bf16[4,2,32,1024]{3,2,1,0:T(8,128)(2,1)} %psfs_ref.1), kind=kLoop, calls=%fused_computation | loop fusion | bytes 524288 | tf_op jit(solution)/shard_map/slice | solution.py:372
  1.0 2.2 %collective-permute-start.1 = (bf16[1,2,32,1024]{3,2,1,0:T(8,128)(2,1)S(1)}, bf16[1,2,32,1024]{3,2,1,0:T(8,128)(2,1)S(1)}, u32[]{:S(2)}, u32[]{:S(2)}) collective-permute-start(bf16[1,2,32,1024]{3,2,1,0:T(8,128)(2,1)S(1)} %get-tuple-element.19), channel_id=1, source_target_pairs={{8,0},{16,8},{24,16},{9,1},{17,9},{25,17},{10,2},{18,10},{26,18},{... | collective-permute-start | bytes 393224 | tf_op jit(solution)/shard_map/ppermute | solution.py:366
  3.2 4.0 %collective-permute-start = (bf16[1,2,32,1024]{3,2,1,0:T(8,128)(2,1)S(1)}, bf16[1,2,32,1024]{3,2,1,0:T(8,128)(2,1)S(1)}, u32[]{:S(2)}, u32[]{:S(2)}) collective-permute-start(bf16[1,2,32,1024]{3,2,1,0:T(8,128)(2,1)S(1)} %get-tuple-element.20), channel_id=1, source_target_pairs={{0,8},{8,16},{16,24},{1,9},{9,17},{17,25},{2,10},{10,18},{18,26},{... | collective-permute-start | bytes 393224 | tf_op jit(solution)/shard_map/ppermute | solution.py:362
  7.2 1.6 %copy-done.14 = f32[128,4096]{1,0:T(8,128)S(1)} copy-done((f32[128,4096]{1,0:T(8,128)S(1)}, f32[128,4096]{1,0:T(8,128)}, u32[]{:S(2)}) %copy-start.14) | copy-done | bytes 2097176
  8.8 0.9 %copy-done.16 = bf16[256,512]{1,0:T(8,128)(2,1)S(1)} copy-done((bf16[256,512]{1,0:T(8,128)(2,1)S(1)}, bf16[256,512]{1,0:T(8,128)(2,1)}, u32[]{:S(2)}) %copy-start.16) | copy-done | bytes 262168
  9.7 0.8 copy-done.18
  10.5 0.7 copy-done.20
  11.3 4.7 %image_forward.3.refs_1_ = bf16[48,192,128]{2,1,0:T(8,128)(2,1)S(1)} custom-call(f32[128,4096]{1,0:T(8,128)S(1)} %copy-done.14, bf16[96,64]{1,0:T(8,128)(2,1)S(1)} %copy-done.20, bf16[256,512]{1,0:T(8,128)(2,1)S(1)} %copy-done.16, bf16[192,128]{1,0:T(8,128)(2,1)S(1)} %copy-done.18), custom_call_target="tpu_custom_call" | custom-call | flops 4000000000 | bytes 4000000 | tf_op jit(solution)/shard_map/image_forward/pallas_call | solution.py:145
  16.0 1.4 %copy-done.1 = bf16[48,192,128]{2,1,0:T(8,128)(2,1)} copy-done((bf16[48,192,128]{2,1,0:T(8,128)(2,1)}, bf16[48,192,128]{2,1,0:T(8,128)(2,1)S(1)}, u32[]{:S(2)}) %copy-start.1) | copy-done | bytes 2359320
  17.5 0.6 copy-done.22
  18.1 0.7 copy-done.23
  18.7 1.9 %blend_x.1 = (bf16[2,32,1024]{2,1,0:T(8,128)(2,1)}, bf16[2,32,1024]{2,1,0:T(8,128)(2,1)}) custom-call(bf16[4,2,32,1024]{3,2,1,0:T(8,128)(2,1)} %psfs_ref.1, bf16[1,2,32,1024]{3,2,1,0:T(8,128)(2,1)} %copy-done.23, bf16[1,2,32,1024]{3,2,1,0:T(8,128)(2,1)} %copy-done.22), custom_call_target="tpu_custom_call" | custom-call | tf_op jit(solution)/shard_map/blend_x/pallas_call | solution.py:180
  20.7 4.3 %collective-permute-start.2 = (bf16[2,32,1024]{2,1,0:T(8,128)(2,1)}, bf16[2,32,1024]{2,1,0:T(8,128)(2,1)S(1)}, u32[]{:S(2)}, u32[]{:S(2)}) collective-permute-start(bf16[2,32,1024]{2,1,0:T(8,128)(2,1)} %get-tuple-element.12.refs_4_), channel_id=1, source_target_pairs={{0,1},{1,2},{2,3},{3,4},{4,5},{5,6},{6,7},{8,9},{9,10},{10,11},{11... | collective-permute-start | bytes 393224 | tf_op jit(solution)/shard_map/ppermute | solution.py:362
  25.0 0.0 copy-start.6
  25.1 0.0 copy-start.10
  25.1 0.0 copy-start.11
  25.1 2.1 %collective-permute-start.3 = (bf16[2,32,1024]{2,1,0:T(8,128)(2,1)}, bf16[2,32,1024]{2,1,0:T(8,128)(2,1)S(1)}, u32[]{:S(2)}, u32[]{:S(2)}) collective-permute-start(bf16[2,32,1024]{2,1,0:T(8,128)(2,1)} %get-tuple-element.13.refs_3_), channel_id=1, source_target_pairs={{1,0},{2,1},{3,2},{4,3},{5,4},{6,5},{7,6},{9,8},{10,9},{11,10},{12... | collective-permute-start | bytes 393224 | tf_op jit(solution)/shard_map/ppermute | solution.py:366
  27.2 4.7 %image_forward.2.refs_0_ = bf16[48,192,128]{2,1,0:T(8,128)(2,1)S(1)} custom-call(f32[128,4096]{1,0:T(8,128)S(1)} %copy-done.15, bf16[96,64]{1,0:T(8,128)(2,1)S(1)} %copy-done.21, bf16[256,512]{1,0:T(8,128)(2,1)S(1)} %copy-done.17, bf16[192,128]{1,0:T(8,128)(2,1)S(1)} %copy-done.19), custom_call_target="tpu_custom_call" | custom-call | flops 4000000000 | bytes 4000000 | tf_op jit(solution)/shard_map/image_forward/pallas_call | solution.py:145
  32.0 23.9 %respond.1 = (f32[160,4096]{1,0:T(8,128)}, bf16[160,1024]{1,0:T(8,128)(2,1)S(1)}, bf16[160,1024]{1,0:T(8,128)(2,1)S(1)}) custom-call(bf16[48,192,128]{2,1,0:T(8,128)(2,1)S(1)} %image_forward.2.refs_0_, bf16[48,192,128]{2,1,0:T(8,128)(2,1)} %copy-done.1, bf16[2,32,1024]{2,1,0:T(8,128)(2,1)S(1)} %collective-permute-done.2.refs_2_, ...), custom_call_target="tpu_custom_call" | custom-call | tf_op jit(solution)/shard_map/respond/pallas_call | solution.py:288
  55.9 3.9 %collective-permute-start.4 = (bf16[160,1024]{1,0:T(8,128)(2,1)S(1)}, bf16[160,1024]{1,0:T(8,128)(2,1)S(1)}, u32[]{:S(2)}, u32[]{:S(2)}) collective-permute-start(bf16[160,1024]{1,0:T(8,128)(2,1)S(1)} %get-tuple-element.15), channel_id=1, source_target_pairs={{0,1},{1,2},{2,3},{3,4},{4,5},{5,6},{6,7},{8,9},{9,10},{10,11},{11... | collective-permute-start | bytes 983048 | tf_op jit(solution)/shard_map/ppermute | solution.py:362
  59.8 1.9 %collective-permute-start.5 = (bf16[160,1024]{1,0:T(8,128)(2,1)S(1)}, bf16[160,1024]{1,0:T(8,128)(2,1)S(1)}, u32[]{:S(2)}, u32[]{:S(2)}) collective-permute-start(bf16[160,1024]{1,0:T(8,128)(2,1)S(1)} %get-tuple-element.16), channel_id=1, source_target_pairs={{1,0},{2,1},{3,2},{4,3},{5,4},{6,5},{7,6},{9,8},{10,9},{11,10},{12... | collective-permute-start | bytes 983048 | tf_op jit(solution)/shard_map/ppermute | solution.py:366
  61.7 2.1 %collective-permute-done.4.low_ref = bf16[160,1024]{1,0:T(8,128)(2,1)S(1)} collective-permute-done((bf16[160,1024]{1,0:T(8,128)(2,1)S(1)}, bf16[160,1024]{1,0:T(8,128)(2,1)S(1)}, u32[]{:S(2)}, u32[]{:S(2)}) %collective-permute-start.4) | collective-permute-done | bytes 327712 | tf_op jit(solution)/shard_map/ppermute | solution.py:362
  63.8 4.4 %collective-permute-done.5.high_ref = bf16[160,1024]{1,0:T(8,128)(2,1)S(1)} collective-permute-done((bf16[160,1024]{1,0:T(8,128)(2,1)S(1)}, bf16[160,1024]{1,0:T(8,128)(2,1)S(1)}, u32[]{:S(2)}, u32[]{:S(2)}) %collective-permute-start.5) | collective-permute-done | bytes 327712 | tf_op jit(solution)/shard_map/ppermute | solution.py:366
  68.2 0.7 copy-done.4
  68.9 1.8 %x_rims.1 = (bf16[16,4096]{1,0:T(8,128)(2,1)}, bf16[16,4096]{1,0:T(8,128)(2,1)}) custom-call(f32[160,4096]{1,0:T(8,128)} %get-tuple-element.14.mid_ref, bf16[160,1024]{1,0:T(8,128)(2,1)} %copy-done.2, bf16[160,1024]{1,0:T(8,128)(2,1)} %copy-done.4), custom_call_target="tpu_custom_call" | custom-call | tf_op jit(solution)/shard_map/x_rims/pallas_call | solution.py:319
  70.7 2.2 %collective-permute-start.6 = (bf16[16,4096]{1,0:T(8,128)(2,1)}, bf16[16,4096]{1,0:T(8,128)(2,1)S(1)}, u32[]{:S(2)}, u32[]{:S(2)}) collective-permute-start(bf16[16,4096]{1,0:T(8,128)(2,1)} %get-tuple-element.17), channel_id=1, source_target_pairs={{0,8},{8,16},{16,24},{1,9},{9,17},{17,25},{2,10},{10,18},{18,26},{... | collective-permute-start | bytes 393224 | tf_op jit(solution)/shard_map/ppermute | solution.py:362
  72.9 3.1 %collective-permute-start.7 = (bf16[16,4096]{1,0:T(8,128)(2,1)}, bf16[16,4096]{1,0:T(8,128)(2,1)S(1)}, u32[]{:S(2)}, u32[]{:S(2)}) collective-permute-start(bf16[16,4096]{1,0:T(8,128)(2,1)} %get-tuple-element.18), channel_id=1, source_target_pairs={{8,0},{16,8},{24,16},{9,1},{17,9},{25,17},{10,2},{18,10},{26,18},{... | collective-permute-start | bytes 393224 | tf_op jit(solution)/shard_map/ppermute | solution.py:366
  76.0 1.1 %collective-permute-done.6.before_ref = bf16[16,4096]{1,0:T(8,128)(2,1)S(1)} collective-permute-done((bf16[16,4096]{1,0:T(8,128)(2,1)}, bf16[16,4096]{1,0:T(8,128)(2,1)S(1)}, u32[]{:S(2)}, u32[]{:S(2)}) %collective-permute-start.6) | collective-permute-done | bytes 131104 | tf_op jit(solution)/shard_map/ppermute | solution.py:362
  77.1 3.4 %collective-permute-done.7.after_ref = bf16[16,4096]{1,0:T(8,128)(2,1)S(1)} collective-permute-done((bf16[16,4096]{1,0:T(8,128)(2,1)}, bf16[16,4096]{1,0:T(8,128)(2,1)S(1)}, u32[]{:S(2)}, u32[]{:S(2)}) %collective-permute-start.7) | collective-permute-done | bytes 131104 | tf_op jit(solution)/shard_map/ppermute | solution.py:366
  80.6 1.0 %copy-done.3 = bf16[160,1024]{1,0:T(8,128)(2,1)S(1)} copy-done((bf16[160,1024]{1,0:T(8,128)(2,1)S(1)}, bf16[160,1024]{1,0:T(8,128)(2,1)}, u32[]{:S(2)}) %copy-start.3) | copy-done | bytes 327704
  81.5 1.0 %copy-done.5 = bf16[160,1024]{1,0:T(8,128)(2,1)S(1)} copy-done((bf16[160,1024]{1,0:T(8,128)(2,1)S(1)}, bf16[160,1024]{1,0:T(8,128)(2,1)}, u32[]{:S(2)}) %copy-start.5) | copy-done | bytes 327704
  82.5 1.6 %fold.1 = f32[128,4096]{1,0:T(8,128)} custom-call(f32[160,4096]{1,0:T(8,128)S(1)} %copy-done, bf16[160,1024]{1,0:T(8,128)(2,1)S(1)} %copy-done.3, bf16[160,1024]{1,0:T(8,128)(2,1)S(1)} %copy-done.5, bf16[16,4096]{1,0:T(8,128)(2,1)S(1)} %collective-permute-done.6.before_ref, bf16[16,4096]{1,0:T(8,128)(2,1)S(1)} %collective-permute-done.7.after_ref), custom_call_target="tpu_custom_call" | custom-call | tf_op jit(solution)/shard_map/fold/pallas_call | solution.py:344
  (39 shorter events, 0.1 us)
Async XLA Ops:
  1.0 16.5 %collective-permute-start.1 = (bf16[1,2,32,1024]{3,2,1,0:T(8,128)(2,1)S(1)}, bf16[1,2,32,1024]{3,2,1,0:T(8,128)(2,1)S(1)}, u32[]{:S(2)}, u32[]{:S(2)}) collective-permute-start(bf16[1,2,32,1024]{3,2,1,0:T(8,128)(2,1)S(1)} %get-tuple-element.19), channel_id=1, source_target_pairs={{8,0},{16,8},{24,16},{9,1},{17,9},{25,17},{10,2},{18,10},{26,18},{... | collective-permute-start | bytes 393224 | tf_op jit(solution)/shard_map/ppermute | solution.py:366
  3.2 14.3 %collective-permute-start = (bf16[1,2,32,1024]{3,2,1,0:T(8,128)(2,1)S(1)}, bf16[1,2,32,1024]{3,2,1,0:T(8,128)(2,1)S(1)}, u32[]{:S(2)}, u32[]{:S(2)}) collective-permute-start(bf16[1,2,32,1024]{3,2,1,0:T(8,128)(2,1)S(1)} %get-tuple-element.20), channel_id=1, source_target_pairs={{0,8},{8,16},{16,24},{1,9},{9,17},{17,25},{2,10},{10,18},{18,26},{... | collective-permute-start | bytes 393224 | tf_op jit(solution)/shard_map/ppermute | solution.py:362
  7.2 1.6 %copy-start.14 = (f32[128,4096]{1,0:T(8,128)S(1)}, f32[128,4096]{1,0:T(8,128)}, u32[]{:S(2)}) copy-start(f32[128,4096]{1,0:T(8,128)} %image_ref.3) | copy-start | bytes 6291460
  8.8 0.9 %copy-start.16 = (bf16[256,512]{1,0:T(8,128)(2,1)S(1)}, bf16[256,512]{1,0:T(8,128)(2,1)}, u32[]{:S(2)}) copy-start(bf16[256,512]{1,0:T(8,128)(2,1)} %constant.19.clone.tz_ref) | copy-start | bytes 786436
  9.7 0.8 copy-start.18
  10.5 0.7 copy-start.20
  11.3 15.9 %copy-start.15 = (f32[128,4096]{1,0:T(8,128)S(1)}, f32[128,4096]{1,0:T(8,128)}, u32[]{:S(2)}) copy-start(f32[128,4096]{1,0:T(8,128)} %image_ref.3) | copy-start | bytes 6291460
  11.3 15.9 %copy-start.17 = (bf16[256,512]{1,0:T(8,128)(2,1)S(1)}, bf16[256,512]{1,0:T(8,128)(2,1)}, u32[]{:S(2)}) copy-start(bf16[256,512]{1,0:T(8,128)(2,1)} %constant.19.clone.tz_ref) | copy-start | bytes 786436
  11.3 15.9 %copy-start.19 = (bf16[192,128]{1,0:T(8,128)(2,1)S(1)}, bf16[192,128]{1,0:T(8,128)(2,1)}, u32[]{:S(2)}) copy-start(bf16[192,128]{1,0:T(8,128)(2,1)} %constant.20.clone.ty_ref) | copy-start | bytes 147460
  11.3 15.9 %copy-start.21 = (bf16[96,64]{1,0:T(8,128)(2,1)S(1)}, bf16[96,64]{1,0:T(8,128)(2,1)}, u32[]{:S(2)}) copy-start(bf16[96,64]{1,0:T(8,128)(2,1)} %constant.18.clone.tx_ref) | copy-start | bytes 36868
  16.0 1.4 %copy-start.1 = (bf16[48,192,128]{2,1,0:T(8,128)(2,1)}, bf16[48,192,128]{2,1,0:T(8,128)(2,1)S(1)}, u32[]{:S(2)}) copy-start(bf16[48,192,128]{2,1,0:T(8,128)(2,1)S(1)} %image_forward.3.refs_1_) | copy-start | bytes 7077892
  17.4 0.6 copy-start.22
  18.1 0.7 copy-start.23
  20.7 11.2 %collective-permute-start.2 = (bf16[2,32,1024]{2,1,0:T(8,128)(2,1)}, bf16[2,32,1024]{2,1,0:T(8,128)(2,1)S(1)}, u32[]{:S(2)}, u32[]{:S(2)}) collective-permute-start(bf16[2,32,1024]{2,1,0:T(8,128)(2,1)} %get-tuple-element.12.refs_4_), channel_id=1, source_target_pairs={{0,1},{1,2},{2,3},{3,4},{4,5},{5,6},{6,7},{8,9},{9,10},{10,11},{11... | collective-permute-start | bytes 393224 | tf_op jit(solution)/shard_map/ppermute | solution.py:362
  25.0 6.9 %copy-start.6 = (bf16[256,1024]{1,0:T(8,128)(2,1)S(1)}, bf16[256,1024]{1,0:T(8,128)(2,1)}, u32[]{:S(2)}) copy-start(bf16[256,1024]{1,0:T(8,128)(2,1)} %constant.22.clone.refs_7_) | copy-start | bytes 1572868
  25.0 6.9 %copy-start.7 = (bf16[512,256]{1,0:T(8,128)(2,1)S(1)}, bf16[512,256]{1,0:T(8,128)(2,1)}, u32[]{:S(2)}) copy-start(bf16[512,256]{1,0:T(8,128)(2,1)} %constant.25.clone.refs_10_) | copy-start | bytes 786436
  25.0 6.9 %copy-start.8 = (bf16[2,32,1024]{2,1,0:T(8,128)(2,1)S(1)}, bf16[2,32,1024]{2,1,0:T(8,128)(2,1)}, u32[]{:S(2)}) copy-start(bf16[2,32,1024]{2,1,0:T(8,128)(2,1)} %get-tuple-element.13.refs_3_) | copy-start | bytes 393220
  25.0 6.9 %copy-start.9 = (bf16[2,32,1024]{2,1,0:T(8,128)(2,1)S(1)}, bf16[2,32,1024]{2,1,0:T(8,128)(2,1)}, u32[]{:S(2)}) copy-start(bf16[2,32,1024]{2,1,0:T(8,128)(2,1)} %get-tuple-element.12.refs_4_) | copy-start | bytes 393220
  25.1 6.9 %copy-start.10 = (bf16[192,192]{1,0:T(8,128)(2,1)S(1)}, bf16[192,192]{1,0:T(8,128)(2,1)}, u32[]{:S(2)}) copy-start(bf16[192,192]{1,0:T(8,128)(2,1)} %constant.24.clone.refs_9_) | copy-start | bytes 221188
  25.1 6.9 %copy-start.11 = (bf16[160,192]{1,0:T(8,128)(2,1)S(1)}, bf16[160,192]{1,0:T(8,128)(2,1)}, u32[]{:S(2)}) copy-start(bf16[160,192]{1,0:T(8,128)(2,1)} %constant.26.clone.refs_11_) | copy-start | bytes 184324
  25.1 6.9 %copy-start.12 = (bf16[192,64]{1,0:T(8,128)(2,1)S(1)}, bf16[192,64]{1,0:T(8,128)(2,1)}, u32[]{:S(2)}) copy-start(bf16[192,64]{1,0:T(8,128)(2,1)} %constant.23.clone.refs_8_) | copy-start | bytes 73732
  25.1 6.9 %copy-start.13 = (bf16[96,128]{1,0:T(8,128)(2,1)S(1)}, bf16[96,128]{1,0:T(8,128)(2,1)}, u32[]{:S(2)}) copy-start(bf16[96,128]{1,0:T(8,128)(2,1)} %constant.21.clone.refs_6_) | copy-start | bytes 73732
  25.1 6.8 %collective-permute-start.3 = (bf16[2,32,1024]{2,1,0:T(8,128)(2,1)}, bf16[2,32,1024]{2,1,0:T(8,128)(2,1)S(1)}, u32[]{:S(2)}, u32[]{:S(2)}) collective-permute-start(bf16[2,32,1024]{2,1,0:T(8,128)(2,1)} %get-tuple-element.13.refs_3_), channel_id=1, source_target_pairs={{1,0},{2,1},{3,2},{4,3},{5,4},{6,5},{7,6},{9,8},{10,9},{11,10},{12... | collective-permute-start | bytes 393224 | tf_op jit(solution)/shard_map/ppermute | solution.py:366
  55.9 24.6 %copy-start = (f32[160,4096]{1,0:T(8,128)S(1)}, f32[160,4096]{1,0:T(8,128)}, u32[]{:S(2)}) copy-start(f32[160,4096]{1,0:T(8,128)} %get-tuple-element.14.mid_ref) | copy-start | bytes 7864324
  55.9 7.9 %collective-permute-start.4 = (bf16[160,1024]{1,0:T(8,128)(2,1)S(1)}, bf16[160,1024]{1,0:T(8,128)(2,1)S(1)}, u32[]{:S(2)}, u32[]{:S(2)}) collective-permute-start(bf16[160,1024]{1,0:T(8,128)(2,1)S(1)} %get-tuple-element.15), channel_id=1, source_target_pairs={{0,1},{1,2},{2,3},{3,4},{4,5},{5,6},{6,7},{8,9},{9,10},{10,11},{11... | collective-permute-start | bytes 983048 | tf_op jit(solution)/shard_map/ppermute | solution.py:362
  59.8 8.4 %collective-permute-start.5 = (bf16[160,1024]{1,0:T(8,128)(2,1)S(1)}, bf16[160,1024]{1,0:T(8,128)(2,1)S(1)}, u32[]{:S(2)}, u32[]{:S(2)}) collective-permute-start(bf16[160,1024]{1,0:T(8,128)(2,1)S(1)} %get-tuple-element.16), channel_id=1, source_target_pairs={{1,0},{2,1},{3,2},{4,3},{5,4},{6,5},{7,6},{9,8},{10,9},{11,10},{12... | collective-permute-start | bytes 983048 | tf_op jit(solution)/shard_map/ppermute | solution.py:366
  63.8 4.4 %copy-start.2 = (bf16[160,1024]{1,0:T(8,128)(2,1)}, bf16[160,1024]{1,0:T(8,128)(2,1)S(1)}, u32[]{:S(2)}) copy-start(bf16[160,1024]{1,0:T(8,128)(2,1)S(1)} %collective-permute-done.4.low_ref) | copy-start | bytes 983044
  68.2 0.7 copy-start.4
  70.7 6.4 %collective-permute-start.6 = (bf16[16,4096]{1,0:T(8,128)(2,1)}, bf16[16,4096]{1,0:T(8,128)(2,1)S(1)}, u32[]{:S(2)}, u32[]{:S(2)}) collective-permute-start(bf16[16,4096]{1,0:T(8,128)(2,1)} %get-tuple-element.17), channel_id=1, source_target_pairs={{0,8},{8,16},{16,24},{1,9},{9,17},{17,25},{2,10},{10,18},{18,26},{... | collective-permute-start | bytes 393224 | tf_op jit(solution)/shard_map/ppermute | solution.py:362
  72.9 7.6 %collective-permute-start.7 = (bf16[16,4096]{1,0:T(8,128)(2,1)}, bf16[16,4096]{1,0:T(8,128)(2,1)S(1)}, u32[]{:S(2)}, u32[]{:S(2)}) collective-permute-start(bf16[16,4096]{1,0:T(8,128)(2,1)} %get-tuple-element.18), channel_id=1, source_target_pairs={{8,0},{16,8},{24,16},{9,1},{17,9},{25,17},{10,2},{18,10},{26,18},{... | collective-permute-start | bytes 393224 | tf_op jit(solution)/shard_map/ppermute | solution.py:366
  80.6 1.0 %copy-start.3 = (bf16[160,1024]{1,0:T(8,128)(2,1)S(1)}, bf16[160,1024]{1,0:T(8,128)(2,1)}, u32[]{:S(2)}) copy-start(bf16[160,1024]{1,0:T(8,128)(2,1)} %copy-done.2) | copy-start | bytes 983044
  81.5 1.0 %copy-start.5 = (bf16[160,1024]{1,0:T(8,128)(2,1)S(1)}, bf16[160,1024]{1,0:T(8,128)(2,1)}, u32[]{:S(2)}) copy-start(bf16[160,1024]{1,0:T(8,128)(2,1)} %copy-done.4) | copy-start | bytes 983044

commit v2 on v1

--- a/solution.py
+++ b/solution.py
@@ -1,3 +1,4 @@
+import functools
 import math
 
 import jax
@@ -93,18 +94,27 @@
     return pl.BlockSpec(shape, lambda *_: (0,) * len(shape))
 
 
-def image_kernel(image_ref, tx_ref, tz_ref, ty_ref, out_ref, swap, mid):
+def parity(axis):
+    return lax.rem(lax.axis_index(axis), 2)
+
+
+def pick(flag, even, odd):
+    return jnp.where(flag == 0, even, odd)
+
+
+def image_kernel(patch, image_ref, tx_ref, tz_ref, ty_ref, out_ref, swap, mid):
     tile = 2 * LANES
     rows = 2 * KX
 
     def along_x(t, _):
-        cells = image_ref[:, pl.ds(pl.multiple_of(t * tile, tile), tile)].astype(BF16)
+        at = pl.ds(pl.multiple_of(t * tile, tile), tile)
+        cells = image_ref[patch * PATCH : (patch + 1) * PATCH, at].astype(BF16)
         result = dot(tx_ref[...], cells)
         for h in range(2):
             swap[pl.ds(2 * t + h, rows, stride=YROWS), :] = result[:, h * LANES : (h + 1) * LANES]
         return 0
 
-    lax.fori_loop(0, PATCH * DEPTH // tile, along_x, 0, unroll=4)
+    lax.fori_loop(0, PATCH * DEPTH // tile, along_x, 0, unroll=8)
 
     half = KX * YROWS
     chunk = 8 * YROWS
@@ -117,7 +127,7 @@
         mid[pl.ds(start, chunk), :] = dot(left, tz_ref[...]).astype(BF16)
         return 0
 
-    lax.fori_loop(0, half // chunk, along_z, 0, unroll=2)
+    lax.fori_loop(0, half // chunk, along_z, 0, unroll=3)
 
     def along_y(t, _):
         pieces = []
@@ -133,7 +143,7 @@
             out_ref[2 * t + h] = result[:, h * LANES : (h + 1) * LANES]
         return 0
 
-    lax.fori_loop(0, KX // 2, along_y, 0, unroll=2)
+    lax.fori_loop(0, KX // 2, along_y, 0, unroll=8)
 
 
 def image_forward(image, patch):
@@ -143,17 +153,13 @@
         constant(y_forward(PATCH, YPER)),
     )
     return pl.pallas_call(
-        image_kernel,
-        grid=(1,),
-        in_specs=[pl.BlockSpec((PATCH, image.shape[1]), lambda _: (patch, 0))]
-        + [full(t.shape) for t in tables],
-        out_specs=full((KX, 2 * LONG, LANES)),
+        functools.partial(image_kernel, patch),
         out_shape=jax.ShapeDtypeStruct((KX, 2 * LONG, LANES), BF16),
         scratch_shapes=[
             pltpu.VMEM((2 * KX * YROWS, LANES), F32),
             pltpu.VMEM((KX * YROWS, 2 * YPER * LANES), BF16),
         ],
-        compiler_params=pltpu.CompilerParams(vmem_limit_bytes=24 << 20),
+        compiler_params=pltpu.CompilerParams(vmem_limit_bytes=16 << 20),
         cost_estimate=pl.CostEstimate(
             flops=4_000_000_000, bytes_accessed=4_000_000, transcendentals=0
         ),
@@ -161,37 +167,36 @@
     )(image, *tables)
 
 
-def blend_kernel(psfs_ref, before_ref, after_ref, first_ref, last_ref):
+def blend_kernel(psfs_ref, even_ref, odd_ref, to_even_ref, to_odd_ref):
     count = psfs_ref.shape[0]
-    for column, out in ((0, first_ref), (1, last_ref)):
-        nodes = [before_ref[0, column]]
-        nodes += [psfs_ref[i, column] for i in range(count)]
-        nodes += [after_ref[0, column]]
-        nodes = [n.astype(F32) for n in nodes]
+    gx, gy = parity("gx"), parity("gy")
+    for out, column in ((to_even_ref, 1 - gy), (to_odd_ref, gy)):
+        from_even = even_ref[0, column].astype(F32)
+        from_odd = odd_ref[0, column].astype(F32)
+        nodes = [pick(gx, from_odd, from_even)]
+        nodes += [psfs_ref[i, column].astype(F32) for i in range(count)]
+        nodes += [pick(gx, from_even, from_odd)]
         for p in range(count // 2):
             total = (nodes[2 * p] + nodes[2 * p + 3]) * BLEND[0]
             total += (nodes[2 * p + 1] + nodes[2 * p + 2]) * BLEND[1]
             out[p] = total.astype(BF16)
 
 
-def blend_x(psfs, before, after):
-    patches = psfs.shape[0] // 2
-    shape = (patches,) + psfs.shape[2:]
+def blend_x(psfs, even, odd):
+    shape = (psfs.shape[0] // 2,) + psfs.shape[2:]
     return pl.pallas_call(
         blend_kernel,
         out_shape=(jax.ShapeDtypeStruct(shape, BF16),) * 2,
+        compiler_params=pltpu.CompilerParams(vmem_limit_bytes=16 << 20),
         name="blend_x",
-    )(psfs, before, after)
-
-
-def respond_kernel(
-    patches,
-    *refs,
-):
+    )(psfs, even, odd)
+
+
+def respond_kernel(patches, *refs):
     spectra = refs[:patches]
     columns = refs[patches : patches + 4]
     tpx, tpz, tpy, tiy, tiz, tix = refs[patches + 4 : patches + 10]
-    mid_ref, low_ref, high_ref = refs[patches + 10 : patches + 13]
+    mid_ref, to_even_ref, to_odd_ref = refs[patches + 10 : patches + 13]
     pswap, pmid, rows_y, grid_x = refs[patches + 13 :]
     tile = 2 * LANES
 
@@ -228,7 +233,7 @@
                     ]
         return 0
 
-    lax.fori_loop(0, KX // 2, along_y, 0, unroll=1)
+    lax.fori_loop(0, KX // 2, along_y, 0, unroll=8)
 
     group = 8
 
@@ -243,7 +248,7 @@
                     ]
         return 0
 
-    lax.fori_loop(0, KX // group, along_z, 0)
+    lax.fori_loop(0, KX // group, along_z, 0, unroll=2)
 
     def along_x(t):
         pieces = []
@@ -251,24 +256,23 @@
             for c in range(2):
                 parts = []
                 for h in range(2):
-                    start = (2 * t + h) * KX
-                    if not isinstance(start, int):
-                        start = pl.multiple_of(start, KX)
+                    start = pl.multiple_of((2 * t + h) * KX, KX)
                     parts.append(grid_x[p, c, pl.ds(start, KX), :])
                 pieces.append(jnp.concatenate(parts, 1).astype(BF16))
         return dot(tix[...], jnp.concatenate(pieces, 0))
 
     rim = HALF * DEPTH // tile
     inner = PATCH * DEPTH // tile
-    for t in range(rim):
-        low_ref[:, t * tile : (t + 1) * tile] = along_x(t).astype(BF16)
-        high_ref[:, t * tile : (t + 1) * tile] = along_x(rim + inner + t).astype(BF16)
+    flag = parity("gy")
+    for out, first in ((to_even_ref, 1 - flag), (to_odd_ref, flag)):
+        for t in range(rim):
+            out[:, t * tile : (t + 1) * tile] = along_x(first * (rim + inner) + t).astype(BF16)
 
     def middle(t, _):
         mid_ref[:, pl.ds(pl.multiple_of(t * tile, tile), tile)] = along_x(rim + t)
         return 0
 
-    lax.fori_loop(0, inner, middle, 0, unroll=2)
+    lax.fori_loop(0, inner, middle, 0, unroll=4)
 
 
 def respond(spectra, columns):
@@ -286,7 +290,7 @@
     rim = (rows, HALF * DEPTH)
     operands = (*spectra, *columns, *tables)
     return pl.pallas_call(
-        lambda *refs: respond_kernel(patches, *refs),
+        functools.partial(respond_kernel, patches),
         out_shape=(
             jax.ShapeDtypeStruct((rows, PATCH * DEPTH), F32),
             jax.ShapeDtypeStruct(rim, BF16),
@@ -298,90 +302,88 @@
             pltpu.VMEM((patches, KX * OROWS, 2 * YPER * LANES), BF16),
             pltpu.VMEM((patches, 2, OROWS * KX, LANES), F32),
         ],
-        compiler_params=pltpu.CompilerParams(vmem_limit_bytes=48 << 20),
+        compiler_params=pltpu.CompilerParams(vmem_limit_bytes=32 << 20),
         name="respond",
     )(*operands)
 
 
-def rim_kernel(mid_ref, low_ref, high_ref, first_ref, last_ref):
-    band = low_ref.shape[1]
-    rows = mid_ref.shape[0] // 2
-    for k, out in ((0, first_ref), (1, last_ref)):
-        at = slice(k * rows, (k + 1) * rows)
-        out[...] = mid_ref[at, :].astype(BF16)
-        out[:, :band] = (mid_ref[at, :band] + low_ref[at, :].astype(F32)).astype(BF16)
-        out[:, -band:] = (mid_ref[at, -band:] + high_ref[at, :].astype(F32)).astype(BF16)
-
-
-def x_rims(mid, low, high):
-    start = (mid.shape[0] - PSFW) // PSFW
+def rim_kernel(mid_ref, even_ref, odd_ref, to_even_ref, to_odd_ref):
+    band = even_ref.shape[1]
+    rows = mid_ref.shape[0] - PSFW
+    gx, gy = parity("gx"), parity("gy")
+    for out, side in ((to_even_ref, 1 - gx), (to_odd_ref, gx)):
+        at = pl.ds(pl.multiple_of(rows + side * HALF, HALF), HALF)
+        low = pick(gy, odd_ref[at, :], even_ref[at, :]).astype(F32)
+        high = pick(gy, even_ref[at, :], odd_ref[at, :]).astype(F32)
+        out[:, band:-band] = mid_ref[at, band:-band].astype(BF16)
+        out[:, :band] = (mid_ref[at, :band] + low).astype(BF16)
+        out[:, -band:] = (mid_ref[at, -band:] + high).astype(BF16)
+
+
+def x_rims(mid, even, odd):
     shape = jax.ShapeDtypeStruct((HALF, mid.shape[1]), BF16)
     return pl.pallas_call(
         rim_kernel,
-        grid=(1,),
-        in_specs=[
-            pl.BlockSpec((PSFW, mid.shape[1]), lambda _: (start, 0)),
-            pl.BlockSpec((PSFW, low.shape[1]), lambda _: (start, 0)),
-            pl.BlockSpec((PSFW, high.shape[1]), lambda _: (start, 0)),
-        ],
-        out_specs=(full(shape.shape),) * 2,
         out_shape=(shape,) * 2,
+        compiler_params=pltpu.CompilerParams(vmem_limit_bytes=16 << 20),
         name="x_rims",
-    )(mid, low, high)
-
-
-def fold_kernel(mid_ref, low_ref, high_ref, before_ref, after_ref, out_ref):
-    rows, band = out_ref.shape[0], low_ref.shape[1]
-    out_ref[...] = mid_ref[...]
-    out_ref[:, :band] += low_ref[...].astype(F32)
-    out_ref[:, -band:] += high_ref[...].astype(F32)
-    out_ref[:HALF, :] += before_ref[...].astype(F32)
-    out_ref[rows - HALF :, :] += after_ref[...].astype(F32)
-
-
-def fold(mid, low, high, before, after):
+    )(mid, even, odd)
+
+
+def fold_kernel(mid_ref, even_y_ref, odd_y_ref, even_x_ref, odd_x_ref, out_ref):
+    rows, columns = out_ref.shape
+    band = even_y_ref.shape[1]
+    gx, gy = parity("gx"), parity("gy")
+    out_ref[...] = mid_ref[:rows, :]
+    for ref, side in ((even_y_ref, 1 - gy), (odd_y_ref, gy)):
+        at = pl.ds(pl.multiple_of(side * (columns - band), band), band)
+        out_ref[:, at] += ref[:rows, :].astype(F32)
+    for ref, side in ((even_x_ref, 1 - gx), (odd_x_ref, gx)):
+        at = pl.ds(pl.multiple_of(side * (rows - HALF), HALF), HALF)
+        out_ref[at, :] += ref[...].astype(F32)
+
+
+def fold(mid, *received):
     rows = mid.shape[0] - PSFW
     return pl.pallas_call(
         fold_kernel,
-        grid=(1,),
-        in_specs=[
-            pl.BlockSpec((rows, mid.shape[1]), lambda _: (0, 0)),
-            pl.BlockSpec((rows, low.shape[1]), lambda _: (0, 0)),
-            pl.BlockSpec((rows, high.shape[1]), lambda _: (0, 0)),
-            full(before.shape),
-            full(after.shape),
-        ],
-        out_specs=full((rows, mid.shape[1])),
         out_shape=jax.ShapeDtypeStruct((rows, mid.shape[1]), F32),
-        compiler_params=pltpu.CompilerParams(vmem_limit_bytes=24 << 20),
+        compiler_params=pltpu.CompilerParams(vmem_limit_bytes=16 << 20),
         name="fold",
-    )(mid, low, high, before, after)
-
-
-def onward(value, axis):
-    return lax.ppermute(value, axis, [(i, i + 1) for i in range(lax.axis_size(axis) - 1)])
-
-
-def backward(value, axis):
-    return lax.ppermute(value, axis, [(i + 1, i) for i in range(lax.axis_size(axis) - 1)])
+    )(mid, *received)
+
+
+def swap_even(value, axis):
+    count = lax.axis_size(axis)
+    return lax.ppermute(value, axis, [(i, i ^ 1) for i in range(count) if i ^ 1 < count])
+
+
+def swap_odd(value, axis):
+    ends = [i + 1 if i % 2 else i - 1 for i in range(lax.axis_size(axis))]
+    pairs = [(i, j) for i, j in enumerate(ends) if 0 <= j < len(ends)]
+    return lax.ppermute(value, axis, pairs)
 
 
 def body(image, psfs):
     patches = image.shape[0] // PATCH
-    before = onward(psfs[-1:], "gx")
-    after = backward(psfs[:1], "gx")
+    last = psfs.shape[0] - 1
+    gx = parity("gx")
+    to_odd = lax.dynamic_slice_in_dim(psfs, gx * last, 1, 0)
+    to_even = lax.dynamic_slice_in_dim(psfs, (1 - gx) * last, 1, 0)
+    odd = swap_odd(to_odd, "gx")
+    even = swap_even(to_even, "gx")
     spectra = [image_forward(image, 0)]
-    first, last = blend_x(psfs, before, after)
-    left = onward(last, "gy")
-    right = backward(first, "gy")
+    to_even, to_odd = blend_x(psfs, even, odd)
+    odd = swap_odd(to_odd, "gy")
+    even = swap_even(to_even, "gy")
     spectra += [image_forward(image, p) for p in range(1, patches)]
-    mid, low, high = respond(spectra, (left, first, last, right))
-    from_left = onward(high, "gy")
-    from_right = backward(low, "gy")
-    first, last = x_rims(mid, from_left, from_right)
-    before = onward(last, "gx")
-    after = backward(first, "gx")
-    return fold(mid, from_left, from_right, before, after)
+    mid, out_even, out_odd = respond(spectra, (odd, to_odd, to_even, even))
+    odd_y = swap_odd(out_odd, "gy")
+    even_y = swap_even(out_even, "gy")
+    out_even, out_odd = x_rims(mid, even_y, odd_y)
+    odd_x = swap_odd(out_odd, "gx")
+    even_x = swap_even(out_even, "gx")
+    return fold(mid, even_y, odd_y, even_x, odd_x)
 
 
 def solution(mesh):

time: 84.8 us -> 49.5 us (0.58)
  Pallas kernels: 38.6 us -> 17.7 us
  starting transfers between devices: 23.6 us -> 15.3 us
  local copies, waits for them, and re-layouts: 10.5 us -> 5.15 us
    pallas_call x5, Pallas kernels: 36.7 us -> 17.5 us  [the longest x1 9.89 us: respond(): pl.pallas_call(functools.partial(respond_kernel, patches), out_shape=(jax...]
    ppermute x8, starting transfers between devices: 23.6 us -> 15.3 us  [the longest x4 12.9 us: swap_odd(): return lax.ppermute(value, axis, pairs)]
    unnamed x48 -> x22, local copies, waits for them, and re-layouts: 9.53 us -> 4.17 us
    pallas_call x1, Pallas kernels: 1.94 us -> 0.21 us  [blend_x(): pl.pallas_call(blend_kernel, out_shape=(jax.ShapeDtypeStruct(shape, BF16)...]
    dynamic_slice x0 -> x1, local copies, waits for them, and re-layouts: none -> 0.98 us  [body(): to_odd = lax.dynamic_slice_in_dim(psfs, gx * last, 1, 0)]
    slice x1 -> x0, local copies, waits for them, and re-layouts: 0.98 us -> none  [body(): after = backward(psfs[:1], 'gx')]
  transfers between devices with their start and end apart: 8 -> 8, of which waited for: 4 -> 3; matrix products, arithmetic and copies ran while one was open for 0% -> 0% of each run, Pallas kernels for 11% -> 12%
where the time goes in v2:
time: 49.5 us; the launch traced here: 48.6 us
  Pallas kernels  17.7 us (36%)
  starting transfers between devices  15.3 us (31%)
  waiting for transfers between devices  10.2 us (21%)
  local copies, waits for them, and re-layouts  5.15 us (10%)
    ppermute x4, starting transfers between devices, swap_odd(): return lax.ppermute(value, axis, pairs)  12.9 us
    pallas_call x1, Pallas kernels, respond(): pl.pallas_call(functools.partial(respond_kernel, patches), out_shape=(jax...  9.89 us
    ppermute x4, waiting for transfers between devices, swap_odd(): return lax.ppermute(value, axis, pairs)  9.53 us
    pallas_call x2, Pallas kernels, image_forward(): pl.pallas_call(functools.partial(image_kernel, patch), out_shape=jax.Shap...  5.93 us
    unnamed x22, local copies, waits for them, and re-layouts  4.17 us
    ppermute x4, starting transfers between devices, swap_even(): lax.ppermute(value, axis, [(i, i ^ 1) for i in range(count) if i ^ 1 < co...  2.43 us
    pallas_call x1, Pallas kernels, fold(): pl.pallas_call(fold_kernel, out_shape=jax.ShapeDtypeStruct((rows, mid.sha...  1.61 us
  transfers between devices with their start and end apart: 8, of which 3 were waited for; matrix products, arithmetic and copies ran while one was open for 0% of the time, Pallas kernels for 12%

profile of v2, /device:TPU:19, one launch (start us, length us, event | category | flops | bytes accessed | tf_op | source)
XLA Modules:
  0.0 48.6 jit_solution(8532364846759421074)
XLA Ops:
  0.0 1.0 %constant_dynamic-slice_fusion = (bf16[1,2,32,1024]{3,2,1,0:T(8,128)(2,1)S(1)}, bf16[1,2,32,1024]{3,2,1,0:T(8,128)(2,1)S(1)}) fusion(bf16[4,2,32,1024]{3,2,1,0:T(8,128)(2,1)} %psfs_ref.1, s32[]{:T(128)S(6)} %select_n.7, s32[]{:T(128)S(6)} %select_n.6), kind=kLoop, calls=%fused_computation | loop fusion | bytes 524296 | tf_op jit(solution)/shard_map/dynamic_slice | solution.py:371
  1.0 3.1 %collective-permute-start.1 = (bf16[1,2,32,1024]{3,2,1,0:T(8,128)(2,1)S(1)}, bf16[1,2,32,1024]{3,2,1,0:T(8,128)(2,1)S(1)}, u32[]{:S(2)}, u32[]{:S(2)}) collective-permute-start(bf16[1,2,32,1024]{3,2,1,0:T(8,128)(2,1)S(1)} %get-tuple-element.19), channel_id=1, source_target_pairs={{8,16},{16,8},{9,17},{17,9},{10,18},{18,10},{11,19},{19,11},{12,20... | collective-permute-start | bytes 393224 | tf_op jit(solution)/shard_map/ppermute | solution.py:364
  4.1 0.0 copy-start
  4.1 0.1 collective-permute-start
  4.2 0.0 copy-start.7
  4.2 1.6 %copy-done.7 = f32[128,4096]{1,0:T(8,128)S(1)} copy-done((f32[128,4096]{1,0:T(8,128)S(1)}, f32[128,4096]{1,0:T(8,128)}, u32[]{:S(2)}) %copy-start.7) | copy-done | bytes 2097176
  5.9 0.9 %copy-done.8 = bf16[256,512]{1,0:T(8,128)(2,1)S(1)} copy-done((bf16[256,512]{1,0:T(8,128)(2,1)S(1)}, bf16[256,512]{1,0:T(8,128)(2,1)}, u32[]{:S(2)}) %copy-start.8) | copy-done | bytes 262168
  6.8 0.8 %copy-done.9 = bf16[192,128]{1,0:T(8,128)(2,1)S(1)} copy-done((bf16[192,128]{1,0:T(8,128)(2,1)S(1)}, bf16[192,128]{1,0:T(8,128)(2,1)}, u32[]{:S(2)}) %copy-start.9) | copy-done | bytes 49176
  7.6 0.7 %copy-done.10 = bf16[96,64]{1,0:T(8,128)(2,1)S(1)} copy-done((bf16[96,64]{1,0:T(8,128)(2,1)S(1)}, bf16[96,64]{1,0:T(8,128)(2,1)}, u32[]{:S(2)}) %copy-start.10) | copy-done | bytes 12312
  8.3 3.0 %image_forward.3.refs_1_ = bf16[48,192,128]{2,1,0:T(8,128)(2,1)S(1)} custom-call(f32[128,4096]{1,0:T(8,128)S(1)} %copy-done.7, bf16[96,64]{1,0:T(8,128)(2,1)S(1)} %copy-done.10, bf16[256,512]{1,0:T(8,128)(2,1)S(1)} %copy-done.8, bf16[192,128]{1,0:T(8,128)(2,1)S(1)} %copy-done.9), custom_call_target="tpu_custom_call" | custom-call | flops 4000000000 | bytes 4000000 | tf_op jit(solution)/shard_map/image_forward/pallas_call | solution.py:155
  11.3 0.0 collective-permute-done.even_ref
  11.3 0.2 blend_x.1
  11.6 4.1 %collective-permute-start.2 = (bf16[2,32,1024]{2,1,0:T(8,128)(2,1)S(1)}, bf16[2,32,1024]{2,1,0:T(8,128)(2,1)S(1)}, u32[]{:S(2)}, u32[]{:S(2)}) collective-permute-start(bf16[2,32,1024]{2,1,0:T(8,128)(2,1)S(1)} %get-tuple-element.12.refs_3_), channel_id=1, source_target_pairs={{1,2},{2,1},{3,4},{4,3},{5,6},{6,5},{9,10},{10,9},{11,12},{12,11},... | collective-permute-start | bytes 393224 | tf_op jit(solution)/shard_map/ppermute | solution.py:364
  15.6 0.0 copy-start.1
  15.6 0.0 copy-start.2
  15.6 0.0 copy-start.3
  15.7 0.0 copy-start.4
  15.7 0.0 copy-start.5
  15.7 0.0 copy-start.6
  15.7 0.1 collective-permute-start.3
  15.8 3.0 %image_forward.2.refs_0_ = bf16[48,192,128]{2,1,0:T(8,128)(2,1)S(1)} custom-call(f32[128,4096]{1,0:T(8,128)S(1)} %copy-done.7, bf16[96,64]{1,0:T(8,128)(2,1)S(1)} %copy-done.10, bf16[256,512]{1,0:T(8,128)(2,1)S(1)} %copy-done.8, bf16[192,128]{1,0:T(8,128)(2,1)S(1)} %copy-done.9), custom_call_target="tpu_custom_call" | custom-call | flops 4000000000 | bytes 4000000 | tf_op jit(solution)/shard_map/image_forward/pallas_call | solution.py:155
  18.8 0.0 collective-permute-done.3.refs_5_
  18.8 9.9 %respond.1 = (f32[160,4096]{1,0:T(8,128)S(1)}, bf16[160,1024]{1,0:T(8,128)(2,1)S(1)}, bf16[160,1024]{1,0:T(8,128)(2,1)S(1)}) custom-call(bf16[48,192,128]{2,1,0:T(8,128)(2,1)S(1)} %image_forward.2.refs_0_, bf16[48,192,128]{2,1,0:T(8,128)(2,1)S(1)} %image_forward.3.refs_1_, bf16[2,32,1024]{2,1,0:T(8,128)(2,1)S(1)} %collective-permute-done.2.refs_2_, ...), custom_call_target="tpu_custom_call" | custom-call | tf_op jit(solution)/shard_map/respond/pallas_call | solution.py:292
  28.7 0.6 %collective-permute-start.4 = (bf16[160,1024]{1,0:T(8,128)(2,1)S(1)}, bf16[160,1024]{1,0:T(8,128)(2,1)S(1)}, u32[]{:S(2)}, u32[]{:S(2)}) collective-permute-start(bf16[160,1024]{1,0:T(8,128)(2,1)S(1)} %get-tuple-element.15), channel_id=1, source_target_pairs={{0,1},{1,0},{2,3},{3,2},{4,5},{5,4},{6,7},{7,6},{8,9},{9,8},{10,11... | collective-permute-start | bytes 983048 | tf_op jit(solution)/shard_map/ppermute | solution.py:358
  29.3 2.6 %collective-permute-start.5 = (bf16[160,1024]{1,0:T(8,128)(2,1)S(1)}, bf16[160,1024]{1,0:T(8,128)(2,1)S(1)}, u32[]{:S(2)}, u32[]{:S(2)}) collective-permute-start(bf16[160,1024]{1,0:T(8,128)(2,1)S(1)} %get-tuple-element.16), channel_id=1, source_target_pairs={{1,2},{2,1},{3,4},{4,3},{5,6},{6,5},{9,10},{10,9},{11,12},{12,11},... | collective-permute-start | bytes 983048 | tf_op jit(solution)/shard_map/ppermute | solution.py:364
  31.9 0.0 collective-permute-done.4.even_ref.even_y_ref
  32.0 5.7 %collective-permute-done.5.odd_ref.odd_y_ref = bf16[160,1024]{1,0:T(8,128)(2,1)S(1)} collective-permute-done((bf16[160,1024]{1,0:T(8,128)(2,1)S(1)}, bf16[160,1024]{1,0:T(8,128)(2,1)S(1)}, u32[]{:S(2)}, u32[]{:S(2)}) %collective-permute-start.5) | collective-permute-done | bytes 327712 | tf_op jit(solution)/shard_map/ppermute | solution.py:364
  37.7 1.7 %collective-permute-start.6 = (bf16[16,4096]{1,0:T(8,128)(2,1)S(1)}, bf16[16,4096]{1,0:T(8,128)(2,1)S(1)}, u32[]{:S(2)}, u32[]{:S(2)}) collective-permute-start(bf16[16,4096]{1,0:T(8,128)(2,1)S(1)} %get-tuple-element.17), channel_id=1, source_target_pairs={{0,8},{8,0},{16,24},{24,16},{1,9},{9,1},{17,25},{25,17},{2,10},{10... | collective-permute-start | bytes 393224 | tf_op jit(solution)/shard_map/ppermute | solution.py:358
  39.5 3.0 %collective-permute-start.7 = (bf16[16,4096]{1,0:T(8,128)(2,1)S(1)}, bf16[16,4096]{1,0:T(8,128)(2,1)S(1)}, u32[]{:S(2)}, u32[]{:S(2)}) collective-permute-start(bf16[16,4096]{1,0:T(8,128)(2,1)S(1)} %get-tuple-element.18), channel_id=1, source_target_pairs={{8,16},{16,8},{9,17},{17,9},{10,18},{18,10},{11,19},{19,11},{12,20... | collective-permute-start | bytes 393224 | tf_op jit(solution)/shard_map/ppermute | solution.py:364
  42.5 0.7 %collective-permute-done.6.even_x_ref = bf16[16,4096]{1,0:T(8,128)(2,1)S(1)} collective-permute-done((bf16[16,4096]{1,0:T(8,128)(2,1)S(1)}, bf16[16,4096]{1,0:T(8,128)(2,1)S(1)}, u32[]{:S(2)}, u32[]{:S(2)}) %collective-permute-start.6) | collective-permute-done | bytes 131104 | tf_op jit(solution)/shard_map/ppermute | solution.py:358
  43.2 3.8 %collective-permute-done.7.odd_x_ref = bf16[16,4096]{1,0:T(8,128)(2,1)S(1)} collective-permute-done((bf16[16,4096]{1,0:T(8,128)(2,1)S(1)}, bf16[16,4096]{1,0:T(8,128)(2,1)S(1)}, u32[]{:S(2)}, u32[]{:S(2)}) %collective-permute-start.7) | collective-permute-done | bytes 131104 | tf_op jit(solution)/shard_map/ppermute | solution.py:364
  47.0 1.6 %fold.1 = f32[128,4096]{1,0:T(8,128)} custom-call(f32[160,4096]{1,0:T(8,128)S(1)} %get-tuple-element.14.mid_ref, bf16[160,1024]{1,0:T(8,128)(2,1)S(1)} %collective-permute-done.4.even_ref.even_y_ref, bf16[160,1024]{1,0:T(8,128)(2,1)S(1)} %collective-permute-done.5.odd_ref.odd_y_ref, bf16[16,4096]{1,0:T(8,128)(2,1)S(1)} %collective-permute-done.6.even_x_ref, ...), custom_call_target="tpu_custom_call" | custom-call | tf_op jit(solution)/shard_map/fold/pallas_call | solution.py:348
  (13 shorter events, 0.1 us)
Async XLA Ops:
  1.0 10.3 %collective-permute-start.1 = (bf16[1,2,32,1024]{3,2,1,0:T(8,128)(2,1)S(1)}, bf16[1,2,32,1024]{3,2,1,0:T(8,128)(2,1)S(1)}, u32[]{:S(2)}, u32[]{:S(2)}) collective-permute-start(bf16[1,2,32,1024]{3,2,1,0:T(8,128)(2,1)S(1)} %get-tuple-element.19), channel_id=1, source_target_pairs={{8,16},{16,8},{9,17},{17,9},{10,18},{18,10},{11,19},{19,11},{12,20... | collective-permute-start | bytes 393224 | tf_op jit(solution)/shard_map/ppermute | solution.py:364
  4.1 7.2 %copy-start = (bf16[4,2,32,1024]{3,2,1,0:T(8,128)(2,1)S(1)}, bf16[4,2,32,1024]{3,2,1,0:T(8,128)(2,1)}, u32[]{:S(2)}) copy-start(bf16[4,2,32,1024]{3,2,1,0:T(8,128)(2,1)} %psfs_ref.1) | copy-start | bytes 1572868
  4.1 7.2 %collective-permute-start = (bf16[1,2,32,1024]{3,2,1,0:T(8,128)(2,1)S(1)}, bf16[1,2,32,1024]{3,2,1,0:T(8,128)(2,1)S(1)}, u32[]{:S(2)}, u32[]{:S(2)}) collective-permute-start(bf16[1,2,32,1024]{3,2,1,0:T(8,128)(2,1)S(1)} %get-tuple-element.20), channel_id=1, source_target_pairs={{0,8},{8,0},{16,24},{24,16},{1,9},{9,1},{17,25},{25,17},{2,10},{10... | collective-permute-start | bytes 393224 | tf_op jit(solution)/shard_map/ppermute | solution.py:358
  4.2 1.6 %copy-start.7 = (f32[128,4096]{1,0:T(8,128)S(1)}, f32[128,4096]{1,0:T(8,128)}, u32[]{:S(2)}) copy-start(f32[128,4096]{1,0:T(8,128)} %image_ref.3) | copy-start | bytes 6291460
  5.9 0.9 %copy-start.8 = (bf16[256,512]{1,0:T(8,128)(2,1)S(1)}, bf16[256,512]{1,0:T(8,128)(2,1)}, u32[]{:S(2)}) copy-start(bf16[256,512]{1,0:T(8,128)(2,1)} %constant.35.clone.tz_ref) | copy-start | bytes 786436
  6.8 0.8 %copy-start.9 = (bf16[192,128]{1,0:T(8,128)(2,1)S(1)}, bf16[192,128]{1,0:T(8,128)(2,1)}, u32[]{:S(2)}) copy-start(bf16[192,128]{1,0:T(8,128)(2,1)} %constant.36.clone.ty_ref) | copy-start | bytes 147460
  7.6 0.7 %copy-start.10 = (bf16[96,64]{1,0:T(8,128)(2,1)S(1)}, bf16[96,64]{1,0:T(8,128)(2,1)}, u32[]{:S(2)}) copy-start(bf16[96,64]{1,0:T(8,128)(2,1)} %constant.34.clone.tx_ref) | copy-start | bytes 36868
  11.6 7.2 %collective-permute-start.2 = (bf16[2,32,1024]{2,1,0:T(8,128)(2,1)S(1)}, bf16[2,32,1024]{2,1,0:T(8,128)(2,1)S(1)}, u32[]{:S(2)}, u32[]{:S(2)}) collective-permute-start(bf16[2,32,1024]{2,1,0:T(8,128)(2,1)S(1)} %get-tuple-element.12.refs_3_), channel_id=1, source_target_pairs={{1,2},{2,1},{3,4},{4,3},{5,6},{6,5},{9,10},{10,9},{11,12},{12,11},... | collective-permute-start | bytes 393224 | tf_op jit(solution)/shard_map/ppermute | solution.py:364
  15.6 3.2 %copy-start.1 = (bf16[256,1024]{1,0:T(8,128)(2,1)S(1)}, bf16[256,1024]{1,0:T(8,128)(2,1)}, u32[]{:S(2)}) copy-start(bf16[256,1024]{1,0:T(8,128)(2,1)} %constant.38.clone.refs_7_) | copy-start | bytes 1572868
  15.6 3.2 %copy-start.2 = (bf16[512,256]{1,0:T(8,128)(2,1)S(1)}, bf16[512,256]{1,0:T(8,128)(2,1)}, u32[]{:S(2)}) copy-start(bf16[512,256]{1,0:T(8,128)(2,1)} %constant.41.clone.refs_10_) | copy-start | bytes 786436
  15.6 3.2 %copy-start.3 = (bf16[192,192]{1,0:T(8,128)(2,1)S(1)}, bf16[192,192]{1,0:T(8,128)(2,1)}, u32[]{:S(2)}) copy-start(bf16[192,192]{1,0:T(8,128)(2,1)} %constant.40.clone.refs_9_) | copy-start | bytes 221188
  15.7 3.2 %copy-start.4 = (bf16[160,192]{1,0:T(8,128)(2,1)S(1)}, bf16[160,192]{1,0:T(8,128)(2,1)}, u32[]{:S(2)}) copy-start(bf16[160,192]{1,0:T(8,128)(2,1)} %constant.42.clone.refs_11_) | copy-start | bytes 184324
  15.7 3.1 %copy-start.5 = (bf16[192,64]{1,0:T(8,128)(2,1)S(1)}, bf16[192,64]{1,0:T(8,128)(2,1)}, u32[]{:S(2)}) copy-start(bf16[192,64]{1,0:T(8,128)(2,1)} %constant.39.clone.refs_8_) | copy-start | bytes 73732
  15.7 3.1 %copy-start.6 = (bf16[96,128]{1,0:T(8,128)(2,1)S(1)}, bf16[96,128]{1,0:T(8,128)(2,1)}, u32[]{:S(2)}) copy-start(bf16[96,128]{1,0:T(8,128)(2,1)} %constant.37.clone.refs_6_) | copy-start | bytes 73732
  15.7 3.1 %collective-permute-start.3 = (bf16[2,32,1024]{2,1,0:T(8,128)(2,1)S(1)}, bf16[2,32,1024]{2,1,0:T(8,128)(2,1)S(1)}, u32[]{:S(2)}, u32[]{:S(2)}) collective-permute-start(bf16[2,32,1024]{2,1,0:T(8,128)(2,1)S(1)} %get-tuple-element.13.refs_4_), channel_id=1, source_target_pairs={{0,1},{1,0},{2,3},{3,2},{4,5},{5,4},{6,7},{7,6},{8,9},{9,8},{10,11... | collective-permute-start | bytes 393224 | tf_op jit(solution)/shard_map/ppermute | solution.py:358
  28.7 3.2 %collective-permute-start.4 = (bf16[160,1024]{1,0:T(8,128)(2,1)S(1)}, bf16[160,1024]{1,0:T(8,128)(2,1)S(1)}, u32[]{:S(2)}, u32[]{:S(2)}) collective-permute-start(bf16[160,1024]{1,0:T(8,128)(2,1)S(1)} %get-tuple-element.15), channel_id=1, source_target_pairs={{0,1},{1,0},{2,3},{3,2},{4,5},{5,4},{6,7},{7,6},{8,9},{9,8},{10,11... | collective-permute-start | bytes 983048 | tf_op jit(solution)/shard_map/ppermute | solution.py:358
  29.3 8.4 %collective-permute-start.5 = (bf16[160,1024]{1,0:T(8,128)(2,1)S(1)}, bf16[160,1024]{1,0:T(8,128)(2,1)S(1)}, u32[]{:S(2)}, u32[]{:S(2)}) collective-permute-start(bf16[160,1024]{1,0:T(8,128)(2,1)S(1)} %get-tuple-element.16), channel_id=1, source_target_pairs={{1,2},{2,1},{3,4},{4,3},{5,6},{6,5},{9,10},{10,9},{11,12},{12,11},... | collective-permute-start | bytes 983048 | tf_op jit(solution)/shard_map/ppermute | solution.py:364
  37.7 5.5 %collective-permute-start.6 = (bf16[16,4096]{1,0:T(8,128)(2,1)S(1)}, bf16[16,4096]{1,0:T(8,128)(2,1)S(1)}, u32[]{:S(2)}, u32[]{:S(2)}) collective-permute-start(bf16[16,4096]{1,0:T(8,128)(2,1)S(1)} %get-tuple-element.17), channel_id=1, source_target_pairs={{0,8},{8,0},{16,24},{24,16},{1,9},{9,1},{17,25},{25,17},{2,10},{10... | collective-permute-start | bytes 393224 | tf_op jit(solution)/shard_map/ppermute | solution.py:358
  39.5 7.6 %collective-permute-start.7 = (bf16[16,4096]{1,0:T(8,128)(2,1)S(1)}, bf16[16,4096]{1,0:T(8,128)(2,1)S(1)}, u32[]{:S(2)}, u32[]{:S(2)}) collective-permute-start(bf16[16,4096]{1,0:T(8,128)(2,1)S(1)} %get-tuple-element.18), channel_id=1, source_target_pairs={{8,16},{16,8},{9,17},{17,9},{10,18},{18,10},{11,19},{19,11},{12,20... | collective-permute-start | bytes 393224 | tf_op jit(solution)/shard_map/ppermute | solution.py:364

commit v3 on v2

--- a/solution.py
+++ b/solution.py
@@ -25,6 +25,8 @@
 YROWS = PATCH // YPER
 PROWS = PSFW // PPER
 OROWS = LONG // YPER
+RIM = HALF // YPER
+EDGE = 2 * RIM
 F32 = jnp.float32
 BF16 = jnp.bfloat16
 
@@ -64,6 +66,7 @@
 def y_inverse():
     block = complex_block(angle(np.arange(LONG), np.arange(LONG), LONG).T, 1.0) / LONG
     block = block.reshape(2, OROWS, YPER, 2 * LONG).transpose(2, 0, 1, 3)
+    block = np.concatenate([block[:, :, :RIM], block[:, :, -RIM:], block[:, :, RIM:-RIM]], 2)
     return block.reshape(2 * LONG, 2 * LONG)
 
 
@@ -102,7 +105,7 @@
     return jnp.where(flag == 0, even, odd)
 
 
-def image_kernel(patch, image_ref, tx_ref, tz_ref, ty_ref, out_ref, swap, mid):
+def image_kernel(patch, image_ref, tx_ref, tz_ref, ty_ref, out_ref, swap, mid, ready=None):
     tile = 2 * LANES
     rows = 2 * KX
 
@@ -114,7 +117,13 @@
             swap[pl.ds(2 * t + h, rows, stride=YROWS), :] = result[:, h * LANES : (h + 1) * LANES]
         return 0
 
-    lax.fori_loop(0, PATCH * DEPTH // tile, along_x, 0, unroll=8)
+    steps = PATCH * DEPTH // tile
+    if ready is None:
+        lax.fori_loop(0, steps, along_x, 0, unroll=8)
+    else:
+        for t in range(steps):
+            ready(t, steps)
+            along_x(t, 0)
 
     half = KX * YROWS
     chunk = 8 * YROWS
@@ -146,25 +155,75 @@
     lax.fori_loop(0, KX // 2, along_y, 0, unroll=8)
 
 
+PARTS = 4
+
+
+def fetching_kernel(patch, image_hbm, *refs):
+    tables_hbm, out_ref, swap, mid, cells = refs[:3], *refs[3:7]
+    tables, sems = refs[7:10], refs[10]
+    width = cells.shape[1] // PARTS
+    parts = [
+        pltpu.make_async_copy(
+            image_hbm.at[pl.ds(patch * PATCH, PATCH), pl.ds(k * width, width)],
+            cells.at[:, pl.ds(k * width, width)],
+            sems.at[k],
+        )
+        for k in range(PARTS)
+    ]
+    fetched = [
+        pltpu.make_async_copy(a, b, sems.at[PARTS + k])
+        for k, (a, b) in enumerate(zip(tables_hbm, tables))
+    ]
+    for copy in [fetched[0], parts[0], *fetched[1:], *parts[1:]]:
+        copy.start()
+
+    def ready(t, steps):
+        if t == 0:
+            fetched[0].wait()
+        if t % (steps // PARTS) == 0:
+            parts[t // (steps // PARTS)].wait()
+        if t == steps - 1:
+            fetched[1].wait()
+            fetched[2].wait()
+
+    image_kernel(0, cells, *tables, out_ref, swap, mid, ready)
+
+
 def image_forward(image, patch):
     tables = (
         constant(x_forward(PATCH)),
         constant(z_forward(DEPTH, YPER)),
         constant(y_forward(PATCH, YPER)),
     )
-    return pl.pallas_call(
-        functools.partial(image_kernel, patch),
+    scratch = [
+        pltpu.VMEM((2 * KX * YROWS, LANES), F32),
+        pltpu.VMEM((KX * YROWS, 2 * YPER * LANES), BF16),
+    ]
+    common = dict(
         out_shape=jax.ShapeDtypeStruct((KX, 2 * LONG, LANES), BF16),
-        scratch_shapes=[
-            pltpu.VMEM((2 * KX * YROWS, LANES), F32),
-            pltpu.VMEM((KX * YROWS, 2 * YPER * LANES), BF16),
-        ],
         compiler_params=pltpu.CompilerParams(vmem_limit_bytes=16 << 20),
         cost_estimate=pl.CostEstimate(
             flops=4_000_000_000, bytes_accessed=4_000_000, transcendentals=0
         ),
-        name="image_forward",
-    )(image, *tables)
+    )
+    if patch:
+        return pl.pallas_call(
+            functools.partial(image_kernel, patch),
+            scratch_shapes=scratch,
+            name="image_forward",
+            **common,
+        )(image, *tables)
+    return pl.pallas_call(
+        functools.partial(fetching_kernel, patch),
+        in_specs=[pl.BlockSpec(memory_space=pltpu.HBM)] * 4,
+        out_specs=pl.BlockSpec(memory_space=pltpu.VMEM),
+        scratch_shapes=scratch
+        + [pltpu.VMEM((PATCH, image.shape[1]), F32)]
+        + [pltpu.VMEM(t.shape, BF16) for t in tables]
+        + [pltpu.SemaphoreType.DMA((PARTS + len(tables),))],
+        name="image_first",
+        **common,
+    )(*[pltpu.with_memory_space_constraint(x, pltpu.HBM) for x in (image, *tables)])
 
 
 def blend_kernel(psfs_ref, even_ref, odd_ref, to_even_ref, to_odd_ref):
@@ -192,12 +251,38 @@
     )(psfs, even, odd)
 
 
+def z_swapped(rows_ref, tiz, grid_ref, p, pairs, group):
+    def along_z(t, _):
+        start = pl.multiple_of(t * group * pairs, group * pairs)
+        result = dot(rows_ref[p, pl.ds(start, group * pairs), :], tiz[...])
+        for k in range(group):
+            for c in range(2):
+                grid_ref[p, c, pl.ds(t * group + k, pairs, stride=KX), :] = result[
+                    k * pairs : (k + 1) * pairs, c * LANES : (c + 1) * LANES
+                ]
+        return 0
+
+    lax.fori_loop(0, KX // group, along_z, 0, unroll=True)
+
+
+def x_inverted(grid_ref, tix, t):
+    pieces = []
+    for p in range(grid_ref.shape[0]):
+        for c in range(2):
+            parts = []
+            for h in range(2):
+                start = pl.multiple_of((2 * t + h) * KX, KX)
+                parts.append(grid_ref[p, c, pl.ds(start, KX), :])
+            pieces.append(jnp.concatenate(parts, 1).astype(BF16))
+    return dot(tix[...], jnp.concatenate(pieces, 0))
+
+
 def respond_kernel(patches, *refs):
     spectra = refs[:patches]
     columns = refs[patches : patches + 4]
     tpx, tpz, tpy, tiy, tiz, tix = refs[patches + 4 : patches + 10]
-    mid_ref, to_even_ref, to_odd_ref = refs[patches + 10 : patches + 13]
-    pswap, pmid, rows_y, grid_x = refs[patches + 13 :]
+    inner_ref, to_even_ref, to_odd_ref = refs[patches + 10 : patches + 13]
+    pswap, pmid, edge_rows, grid_x = refs[patches + 13 :]
     tile = 2 * LANES
 
     for p in range(patches):
@@ -217,6 +302,8 @@
             both = jnp.concatenate([result[:, :, :LANES], result[:, :, LANES:]], 1)
             pmid[p, :, 2 * b * PROWS : 2 * (b + 1) * PROWS, :] = both.astype(BF16)
 
+    inner = OROWS - EDGE
+
     def along_y(t, _):
         for p in range(patches):
             psf = dot(tpy[...], jnp.concatenate([pmid[p, 2 * t], pmid[p, 2 * t + 1]], 1))
@@ -226,85 +313,85 @@
             product = jnp.concatenate([are * bre - aim * bim, are * bim + aim * bre], 0)
             back = dot(tiy[...], product.astype(BF16)).astype(BF16)
             for h in range(2):
-                rows_at = pl.ds(pl.multiple_of((2 * t + h) * OROWS, OROWS), OROWS)
+                edge_at = pl.ds(pl.multiple_of((2 * t + h) * EDGE, EDGE), EDGE)
+                inner_at = pl.ds(pl.multiple_of((2 * t + h) * inner, inner), inner)
                 for b in range(2 * YPER):
-                    rows_y[p, rows_at, b * LANES : (b + 1) * LANES] = back[
-                        b * OROWS : (b + 1) * OROWS, h * LANES : (h + 1) * LANES
-                    ]
+                    block = back[b * OROWS : (b + 1) * OROWS, h * LANES : (h + 1) * LANES]
+                    at = slice(b * LANES, (b + 1) * LANES)
+                    edge_rows[p, edge_at, at] = block[:EDGE]
+                    inner_ref[p, inner_at, at] = block[EDGE:]
         return 0
 
     lax.fori_loop(0, KX // 2, along_y, 0, unroll=8)
 
-    group = 8
-
-    def along_z(t, _):
-        for p in range(patches):
-            start = pl.multiple_of(t * group * OROWS, group * OROWS)
-            result = dot(rows_y[p, pl.ds(start, group * OROWS), :], tiz[...])
-            for k in range(group):
-                for c in range(2):
-                    grid_x[p, c, pl.ds(t * group + k, OROWS, stride=KX), :] = result[
-                        k * OROWS : (k + 1) * OROWS, c * LANES : (c + 1) * LANES
-                    ]
-        return 0
-
-    lax.fori_loop(0, KX // group, along_z, 0, unroll=2)
-
-    def along_x(t):
-        pieces = []
-        for p in range(patches):
-            for c in range(2):
-                parts = []
-                for h in range(2):
-                    start = pl.multiple_of((2 * t + h) * KX, KX)
-                    parts.append(grid_x[p, c, pl.ds(start, KX), :])
-                pieces.append(jnp.concatenate(parts, 1).astype(BF16))
-        return dot(tix[...], jnp.concatenate(pieces, 0))
-
-    rim = HALF * DEPTH // tile
-    inner = PATCH * DEPTH // tile
+    for p in range(patches):
+        z_swapped(edge_rows, tiz, grid_x, p, EDGE, KX // 2)
     flag = parity("gy")
+    rim = RIM // 2
     for out, first in ((to_even_ref, 1 - flag), (to_odd_ref, flag)):
         for t in range(rim):
-            out[:, t * tile : (t + 1) * tile] = along_x(first * (rim + inner) + t).astype(BF16)
-
-    def middle(t, _):
-        mid_ref[:, pl.ds(pl.multiple_of(t * tile, tile), tile)] = along_x(rim + t)
-        return 0
-
-    lax.fori_loop(0, inner, middle, 0, unroll=4)
+            out[:, t * tile : (t + 1) * tile] = x_inverted(grid_x, tix, first * rim + t).astype(BF16)
 
 
 def respond(spectra, columns):
     patches = len(spectra)
     weighted = np.concatenate([w * x_forward(PSFW) for w in BLEND], 1)
+    z_table = constant(z_inverse())
+    x_table = constant(x_inverse(patches))
     tables = (
         constant(weighted),
         constant(z_forward(PSFW, PPER)),
         constant(y_forward(PSFW, PPER)),
         constant(y_inverse()),
-        constant(z_inverse()),
-        constant(x_inverse(patches)),
+        z_table,
+        x_table,
     )
     rows = patches * PATCH + PSFW
     rim = (rows, HALF * DEPTH)
-    operands = (*spectra, *columns, *tables)
-    return pl.pallas_call(
+    inner = OROWS - EDGE
+    inner_rows, out_even, out_odd = pl.pallas_call(
         functools.partial(respond_kernel, patches),
         out_shape=(
-            jax.ShapeDtypeStruct((rows, PATCH * DEPTH), F32),
+            jax.ShapeDtypeStruct((patches, KX * inner, 2 * YPER * LANES), BF16),
             jax.ShapeDtypeStruct(rim, BF16),
             jax.ShapeDtypeStruct(rim, BF16),
         ),
         scratch_shapes=[
             pltpu.VMEM((patches, 2 * KX * PROWS, LANES), F32),
             pltpu.VMEM((patches, KX, 2 * PSFW, LANES), BF16),
-            pltpu.VMEM((patches, KX * OROWS, 2 * YPER * LANES), BF16),
-            pltpu.VMEM((patches, 2, OROWS * KX, LANES), F32),
+            pltpu.VMEM((patches, KX * EDGE, 2 * YPER * LANES), BF16),
+            pltpu.VMEM((patches, 2, EDGE * KX, LANES), F32),
         ],
-        compiler_params=pltpu.CompilerParams(vmem_limit_bytes=32 << 20),
+        compiler_params=pltpu.CompilerParams(vmem_limit_bytes=24 << 20),
         name="respond",
-    )(*operands)
+    )(*spectra, *columns, *tables)
+
+    def middle():
+        return pl.pallas_call(
+            middle_kernel,
+            out_shape=jax.ShapeDtypeStruct((rows, PATCH * DEPTH), F32),
+            scratch_shapes=[pltpu.VMEM((patches, 2, inner * KX, LANES), F32)],
+            compiler_params=pltpu.CompilerParams(vmem_limit_bytes=24 << 20),
+            cost_estimate=pl.CostEstimate(
+                flops=3_000_000_000, bytes_accessed=6_000_000, transcendentals=0
+            ),
+            name="middle",
+        )(inner_rows, z_table, x_table)
+
+    return middle, out_even, out_odd
+
+
+def middle_kernel(rows_ref, tiz, tix, out_ref, grid_x):
+    tile = 2 * LANES
+    inner = OROWS - EDGE
+    for p in range(rows_ref.shape[0]):
+        z_swapped(rows_ref, tiz, grid_x, p, inner, KX // 4)
+
+    def along_x(t, _):
+        out_ref[:, pl.ds(pl.multiple_of(t * tile, tile), tile)] = x_inverted(grid_x, tix, t)
+        return 0
+
+    lax.fori_loop(0, inner // 2, along_x, 0, unroll=4)
 
 
 def rim_kernel(mid_ref, even_ref, odd_ref, to_even_ref, to_odd_ref):
@@ -370,19 +457,22 @@
     gx = parity("gx")
     to_odd = lax.dynamic_slice_in_dim(psfs, gx * last, 1, 0)
     to_even = lax.dynamic_slice_in_dim(psfs, (1 - gx) * last, 1, 0)
+    even = swap_even(to_even, "gx")
     odd = swap_odd(to_odd, "gx")
-    even = swap_even(to_even, "gx")
     spectra = [image_forward(image, 0)]
+    spectra[0], even, odd = lax.optimization_barrier((spectra[0], even, odd))
     to_even, to_odd = blend_x(psfs, even, odd)
+    image, to_even, to_odd = lax.optimization_barrier((image, to_even, to_odd))
+    even = swap_even(to_even, "gy")
     odd = swap_odd(to_odd, "gy")
-    even = swap_even(to_even, "gy")
     spectra += [image_forward(image, p) for p in range(1, patches)]
-    mid, out_even, out_odd = respond(spectra, (odd, to_odd, to_even, even))
+    middle, out_even, out_odd = respond(spectra, (odd, to_odd, to_even, even))
     odd_y = swap_odd(out_odd, "gy")
     even_y = swap_even(out_even, "gy")
+    mid = middle()
     out_even, out_odd = x_rims(mid, even_y, odd_y)
+    even_x = swap_even(out_even, "gx")
     odd_x = swap_odd(out_odd, "gx")
-    even_x = swap_even(out_even, "gx")
     return fold(mid, even_y, odd_y, even_x, odd_x)
 
 

time: 49.5 us -> 44.6 us (0.901)
  local copies, waits for them, and re-layouts: 5.15 us -> 1.06 us
  waiting for transfers between devices: 10.2 us -> 7.82 us
  starting transfers between devices: 15.3 us -> 16.6 us
  Pallas kernels: 17.7 us -> 18.2 us
    pallas_call x2 -> x3, Pallas kernels: 5.93 us -> 10.1 us  [the longest x1 4.56 us: image_forward(): pl.pallas_call(functools.partial(fetching_kernel, patch), in_specs=[pl.Bl...]
    unnamed x22, local copies, waits for them, and re-layouts: 4.17 us -> 0.07 us
    pallas_call x1, Pallas kernels: 9.89 us -> 6.25 us  [respond(): pl.pallas_call(functools.partial(respond_kernel, patches), out_shape=(jax...]
    ppermute x4, waiting for transfers between devices: 9.53 us -> 6.8 us  [swap_odd(): return lax.ppermute(value, axis, pairs)]
    ppermute x4, starting transfers between devices: 12.9 us -> 13.9 us  [swap_odd(): return lax.ppermute(value, axis, pairs)]
  transfers between devices with their start and end apart: 8 -> 8, of which waited for: 3 -> 4; matrix products, arithmetic and copies ran while one was open for 0% -> 0% of each run, Pallas kernels for 12% -> 23%
where the time goes in v3:
time: 44.6 us; the launch traced here: 43.9 us
  Pallas kernels  18.2 us (41%)
  starting transfers between devices  16.6 us (37%)
  waiting for transfers between devices  7.82 us (18%)
  local copies, waits for them, and re-layouts  1.06 us (2%)
    ppermute x4, starting transfers between devices, swap_odd(): return lax.ppermute(value, axis, pairs)  13.9 us
    ppermute x4, waiting for transfers between devices, swap_odd(): return lax.ppermute(value, axis, pairs)  6.8 us
    pallas_call x1, Pallas kernels, respond(): pl.pallas_call(functools.partial(respond_kernel, patches), out_shape=(jax...  6.25 us
    pallas_call x1, Pallas kernels, image_forward(): pl.pallas_call(functools.partial(fetching_kernel, patch), in_specs=[pl.Bl...  4.56 us
    pallas_call x1, Pallas kernels, image_forward(): pl.pallas_call(functools.partial(image_kernel, patch), scratch_shapes=scr...  2.98 us
    ppermute x4, starting transfers between devices, swap_even(): lax.ppermute(value, axis, [(i, i ^ 1) for i in range(count) if i ^ 1 < co...  2.7 us
    pallas_call x1, Pallas kernels, middle(): pl.pallas_call(middle_kernel, out_shape=jax.ShapeDtypeStruct((rows, PATCH...  2.59 us
    pallas_call x1, Pallas kernels, fold(): pl.pallas_call(fold_kernel, out_shape=jax.ShapeDtypeStruct((rows, mid.sha...  1.61 us
  transfers between devices with their start and end apart: 8, of which 4 were waited for; matrix products, arithmetic and copies ran while one was open for 0% of the time, Pallas kernels for 23%

profile of v3, /device:TPU:19, one launch (start us, length us, event | category | flops | bytes accessed | tf_op | source)
XLA Modules:
  0.0 43.9 jit_solution(11565271178237071111)
XLA Ops:
  0.0 1.0 %constant_dynamic-slice_fusion = (bf16[1,2,32,1024]{3,2,1,0:T(8,128)(2,1)S(1)}, bf16[1,2,32,1024]{3,2,1,0:T(8,128)(2,1)S(1)}) fusion(bf16[4,2,32,1024]{3,2,1,0:T(8,128)(2,1)} %psfs_ref.1, s32[]{:T(128)S(6)} %select_n.7, s32[]{:T(128)S(6)} %select_n.6), kind=kLoop, calls=%fused_computation | loop fusion | bytes 524296 | tf_op jit(solution)/shard_map/dynamic_slice | solution.py:458
  1.0 3.1 %collective-permute-start.1 = (bf16[1,2,32,1024]{3,2,1,0:T(8,128)(2,1)S(1)}, bf16[1,2,32,1024]{3,2,1,0:T(8,128)(2,1)S(1)}, u32[]{:S(2)}, u32[]{:S(2)}) collective-permute-start(bf16[1,2,32,1024]{3,2,1,0:T(8,128)(2,1)S(1)} %get-tuple-element.31), channel_id=1, source_target_pairs={{8,16},{16,8},{9,17},{17,9},{10,18},{18,10},{11,19},{19,11},{12,20... | collective-permute-start | bytes 393224 | tf_op jit(solution)/shard_map/ppermute | solution.py:451
  4.1 0.0 copy-start
  4.1 0.0 copy-start.7
  4.1 0.0 copy-start.8
  4.2 0.0 copy-start.9
  4.2 0.0 copy-start.10
  4.2 0.1 collective-permute-start
  4.3 4.6 %image_first.1.refs_0_ = bf16[48,192,128]{2,1,0:T(8,128)(2,1)S(1)} custom-call(f32[128,4096]{1,0:T(8,128)} %image_ref, bf16[96,64]{1,0:T(8,128)(2,1)} %constant.34.clone.refs_0_.tx_ref, bf16[256,512]{1,0:T(8,128)(2,1)} %constant.35.clone.refs_1_.tz_ref, bf16[192,128]{1,0:T(8,128)(2,1)} %constant.36.clone.refs_2_.ty_ref), custom_call_target="tpu_custom_call" | custom-call | flops 4000000000 | bytes 4000000 | tf_op jit(solution)/shard_map/image_first/pallas_call | solution.py:216
  8.8 0.0 collective-permute-done.1.odd_ref
  8.8 0.2 collective-permute-done.even_ref
  9.1 0.2 blend_x.1
  9.3 0.0 copy-start.1
  9.3 0.0 copy-start.2
  9.3 0.0 copy-start.3
  9.3 0.0 copy-start.4
  9.3 0.0 copy-start.5
  9.3 0.0 copy-start.6
  9.3 5.0 %collective-permute-start.2 = (bf16[2,32,1024]{2,1,0:T(8,128)(2,1)S(1)}, bf16[2,32,1024]{2,1,0:T(8,128)(2,1)S(1)}, u32[]{:S(2)}, u32[]{:S(2)}) collective-permute-start(bf16[2,32,1024]{2,1,0:T(8,128)(2,1)S(1)} %get-tuple-element.24.refs_3_), channel_id=1, source_target_pairs={{1,2},{2,1},{3,4},{4,3},{5,6},{6,5},{9,10},{10,9},{11,12},{12,11},... | collective-permute-start | bytes 393224 | tf_op jit(solution)/shard_map/ppermute | solution.py:451
  14.4 0.1 collective-permute-start.3
  14.5 3.0 %image_forward.1.refs_1_ = bf16[48,192,128]{2,1,0:T(8,128)(2,1)S(1)} custom-call(f32[128,4096]{1,0:T(8,128)S(1)} %copy-done.7, bf16[96,64]{1,0:T(8,128)(2,1)S(1)} %copy-done.10, bf16[256,512]{1,0:T(8,128)(2,1)S(1)} %copy-done.8, bf16[192,128]{1,0:T(8,128)(2,1)S(1)} %copy-done.9), custom_call_target="tpu_custom_call" | custom-call | flops 4000000000 | bytes 4000000 | tf_op jit(solution)/shard_map/image_forward/pallas_call | solution.py:210
  17.5 0.0 collective-permute-done.2.refs_2_
  17.5 6.2 %respond.1 = (bf16[2,1536,512]{2,1,0:T(8,128)(2,1)S(1)}, bf16[160,1024]{1,0:T(8,128)(2,1)S(1)}, bf16[160,1024]{1,0:T(8,128)(2,1)S(1)}) custom-call(bf16[48,192,128]{2,1,0:T(8,128)(2,1)S(1)} %image_first.1.refs_0_, bf16[48,192,128]{2,1,0:T(8,128)(2,1)S(1)} %image_forward.1.refs_1_, bf16[2,32,1024]{2,1,0:T(8,128)(2,1)S(1)} %collective-permute-done.2.refs_2_, ...), custom_call_target="tpu_custom_call" | custom-call | tf_op jit(solution)/shard_map/respond/pallas_call | solution.py:352
  23.8 0.5 %collective-permute-start.4 = (bf16[160,1024]{1,0:T(8,128)(2,1)S(1)}, bf16[160,1024]{1,0:T(8,128)(2,1)S(1)}, u32[]{:S(2)}, u32[]{:S(2)}) collective-permute-start(bf16[160,1024]{1,0:T(8,128)(2,1)S(1)} %get-tuple-element.27), channel_id=1, source_target_pairs={{0,1},{1,0},{2,3},{3,2},{4,5},{5,4},{6,7},{7,6},{8,9},{9,8},{10,11... | collective-permute-start | bytes 983048 | tf_op jit(solution)/shard_map/ppermute | solution.py:445
  24.3 2.7 %collective-permute-start.5 = (bf16[160,1024]{1,0:T(8,128)(2,1)S(1)}, bf16[160,1024]{1,0:T(8,128)(2,1)S(1)}, u32[]{:S(2)}, u32[]{:S(2)}) collective-permute-start(bf16[160,1024]{1,0:T(8,128)(2,1)S(1)} %get-tuple-element.28), channel_id=1, source_target_pairs={{1,2},{2,1},{3,4},{4,3},{5,6},{6,5},{9,10},{10,9},{11,12},{12,11},... | collective-permute-start | bytes 983048 | tf_op jit(solution)/shard_map/ppermute | solution.py:451
  27.0 2.6 %middle.1.mid_ref = f32[160,4096]{1,0:T(8,128)S(1)} custom-call(bf16[2,1536,512]{2,1,0:T(8,128)(2,1)S(1)} %get-tuple-element.26.rows_ref, bf16[512,256]{1,0:T(8,128)(2,1)S(1)} %copy-done.2, bf16[160,192]{1,0:T(8,128)(2,1)S(1)} %copy-done.4), custom_call_target="tpu_custom_call" | custom-call | flops 3000000000 | bytes 6000000 | tf_op jit(solution)/shard_map/middle/pallas_call | solution.py:370
  29.6 3.1 %collective-permute-done.5.odd_ref.odd_y_ref = bf16[160,1024]{1,0:T(8,128)(2,1)S(1)} collective-permute-done((bf16[160,1024]{1,0:T(8,128)(2,1)S(1)}, bf16[160,1024]{1,0:T(8,128)(2,1)S(1)}, u32[]{:S(2)}, u32[]{:S(2)}) %collective-permute-start.5) | collective-permute-done | bytes 327712 | tf_op jit(solution)/shard_map/ppermute | solution.py:451
  32.8 2.0 %collective-permute-start.6 = (bf16[16,4096]{1,0:T(8,128)(2,1)S(1)}, bf16[16,4096]{1,0:T(8,128)(2,1)S(1)}, u32[]{:S(2)}, u32[]{:S(2)}) collective-permute-start(bf16[16,4096]{1,0:T(8,128)(2,1)S(1)} %get-tuple-element.29), channel_id=1, source_target_pairs={{0,8},{8,0},{16,24},{24,16},{1,9},{9,1},{17,25},{25,17},{2,10},{10... | collective-permute-start | bytes 393224 | tf_op jit(solution)/shard_map/ppermute | solution.py:445
  34.8 3.0 %collective-permute-start.7 = (bf16[16,4096]{1,0:T(8,128)(2,1)S(1)}, bf16[16,4096]{1,0:T(8,128)(2,1)S(1)}, u32[]{:S(2)}, u32[]{:S(2)}) collective-permute-start(bf16[16,4096]{1,0:T(8,128)(2,1)S(1)} %get-tuple-element.30), channel_id=1, source_target_pairs={{8,16},{16,8},{9,17},{17,9},{10,18},{18,10},{11,19},{19,11},{12,20... | collective-permute-start | bytes 393224 | tf_op jit(solution)/shard_map/ppermute | solution.py:451
  37.8 0.8 %collective-permute-done.6.even_x_ref = bf16[16,4096]{1,0:T(8,128)(2,1)S(1)} collective-permute-done((bf16[16,4096]{1,0:T(8,128)(2,1)S(1)}, bf16[16,4096]{1,0:T(8,128)(2,1)S(1)}, u32[]{:S(2)}, u32[]{:S(2)}) %collective-permute-start.6) | collective-permute-done | bytes 131104 | tf_op jit(solution)/shard_map/ppermute | solution.py:445
  38.6 3.7 %collective-permute-done.7.odd_x_ref = bf16[16,4096]{1,0:T(8,128)(2,1)S(1)} collective-permute-done((bf16[16,4096]{1,0:T(8,128)(2,1)S(1)}, bf16[16,4096]{1,0:T(8,128)(2,1)S(1)}, u32[]{:S(2)}, u32[]{:S(2)}) %collective-permute-start.7) | collective-permute-done | bytes 131104 | tf_op jit(solution)/shard_map/ppermute | solution.py:451
  42.3 1.6 %fold.1 = f32[128,4096]{1,0:T(8,128)} custom-call(f32[160,4096]{1,0:T(8,128)S(1)} %middle.1.mid_ref, bf16[160,1024]{1,0:T(8,128)(2,1)S(1)} %collective-permute-done.4.even_ref.even_y_ref, bf16[160,1024]{1,0:T(8,128)(2,1)S(1)} %collective-permute-done.5.odd_ref.odd_y_ref, bf16[16,4096]{1,0:T(8,128)(2,1)S(1)} %collective-permute-done.6.even_x_ref, ...), custom_call_target="tpu_custom_call" | custom-call | tf_op jit(solution)/shard_map/fold/pallas_call | solution.py:435
  (14 shorter events, 0.1 us)
Async XLA Ops:
  1.0 7.8 %collective-permute-start.1 = (bf16[1,2,32,1024]{3,2,1,0:T(8,128)(2,1)S(1)}, bf16[1,2,32,1024]{3,2,1,0:T(8,128)(2,1)S(1)}, u32[]{:S(2)}, u32[]{:S(2)}) collective-permute-start(bf16[1,2,32,1024]{3,2,1,0:T(8,128)(2,1)S(1)} %get-tuple-element.31), channel_id=1, source_target_pairs={{8,16},{16,8},{9,17},{17,9},{10,18},{18,10},{11,19},{19,11},{12,20... | collective-permute-start | bytes 393224 | tf_op jit(solution)/shard_map/ppermute | solution.py:451
  4.1 5.0 %copy-start = (bf16[4,2,32,1024]{3,2,1,0:T(8,128)(2,1)S(1)}, bf16[4,2,32,1024]{3,2,1,0:T(8,128)(2,1)}, u32[]{:S(2)}) copy-start(bf16[4,2,32,1024]{3,2,1,0:T(8,128)(2,1)} %psfs_ref.1) | copy-start | bytes 1572868
  4.1 10.3 %copy-start.7 = (f32[128,4096]{1,0:T(8,128)S(1)}, f32[128,4096]{1,0:T(8,128)}, u32[]{:S(2)}) copy-start(f32[128,4096]{1,0:T(8,128)} %image_ref) | copy-start | bytes 6291460
  4.1 10.3 %copy-start.8 = (bf16[256,512]{1,0:T(8,128)(2,1)S(1)}, bf16[256,512]{1,0:T(8,128)(2,1)}, u32[]{:S(2)}) copy-start(bf16[256,512]{1,0:T(8,128)(2,1)} %constant.35.clone.refs_1_.tz_ref) | copy-start | bytes 786436
  4.2 10.3 %copy-start.9 = (bf16[192,128]{1,0:T(8,128)(2,1)S(1)}, bf16[192,128]{1,0:T(8,128)(2,1)}, u32[]{:S(2)}) copy-start(bf16[192,128]{1,0:T(8,128)(2,1)} %constant.36.clone.refs_2_.ty_ref) | copy-start | bytes 147460
  4.2 10.3 %copy-start.10 = (bf16[96,64]{1,0:T(8,128)(2,1)S(1)}, bf16[96,64]{1,0:T(8,128)(2,1)}, u32[]{:S(2)}) copy-start(bf16[96,64]{1,0:T(8,128)(2,1)} %constant.34.clone.refs_0_.tx_ref) | copy-start | bytes 36868
  4.2 4.9 %collective-permute-start = (bf16[1,2,32,1024]{3,2,1,0:T(8,128)(2,1)S(1)}, bf16[1,2,32,1024]{3,2,1,0:T(8,128)(2,1)S(1)}, u32[]{:S(2)}, u32[]{:S(2)}) collective-permute-start(bf16[1,2,32,1024]{3,2,1,0:T(8,128)(2,1)S(1)} %get-tuple-element.32), channel_id=1, source_target_pairs={{0,8},{8,0},{16,24},{24,16},{1,9},{9,1},{17,25},{25,17},{2,10},{10... | collective-permute-start | bytes 393224 | tf_op jit(solution)/shard_map/ppermute | solution.py:445
  9.3 8.2 %copy-start.1 = (bf16[256,1024]{1,0:T(8,128)(2,1)S(1)}, bf16[256,1024]{1,0:T(8,128)(2,1)}, u32[]{:S(2)}) copy-start(bf16[256,1024]{1,0:T(8,128)(2,1)} %constant.40.clone.refs_7_) | copy-start | bytes 1572868
  9.3 8.2 %copy-start.2 = (bf16[512,256]{1,0:T(8,128)(2,1)S(1)}, bf16[512,256]{1,0:T(8,128)(2,1)}, u32[]{:S(2)}) copy-start(bf16[512,256]{1,0:T(8,128)(2,1)} %constant.37.clone.refs_10_.tiz) | copy-start | bytes 786436
  9.3 8.2 %copy-start.3 = (bf16[192,192]{1,0:T(8,128)(2,1)S(1)}, bf16[192,192]{1,0:T(8,128)(2,1)}, u32[]{:S(2)}) copy-start(bf16[192,192]{1,0:T(8,128)(2,1)} %constant.42.clone.refs_9_) | copy-start | bytes 221188
  9.3 8.2 %copy-start.4 = (bf16[160,192]{1,0:T(8,128)(2,1)S(1)}, bf16[160,192]{1,0:T(8,128)(2,1)}, u32[]{:S(2)}) copy-start(bf16[160,192]{1,0:T(8,128)(2,1)} %constant.38.clone.refs_11_.tix) | copy-start | bytes 184324
  9.3 8.2 %copy-start.5 = (bf16[192,64]{1,0:T(8,128)(2,1)S(1)}, bf16[192,64]{1,0:T(8,128)(2,1)}, u32[]{:S(2)}) copy-start(bf16[192,64]{1,0:T(8,128)(2,1)} %constant.41.clone.refs_8_) | copy-start | bytes 73732
  9.3 8.2 %copy-start.6 = (bf16[96,128]{1,0:T(8,128)(2,1)S(1)}, bf16[96,128]{1,0:T(8,128)(2,1)}, u32[]{:S(2)}) copy-start(bf16[96,128]{1,0:T(8,128)(2,1)} %constant.39.clone.refs_6_) | copy-start | bytes 73732
  9.3 8.1 %collective-permute-start.2 = (bf16[2,32,1024]{2,1,0:T(8,128)(2,1)S(1)}, bf16[2,32,1024]{2,1,0:T(8,128)(2,1)S(1)}, u32[]{:S(2)}, u32[]{:S(2)}) collective-permute-start(bf16[2,32,1024]{2,1,0:T(8,128)(2,1)S(1)} %get-tuple-element.24.refs_3_), channel_id=1, source_target_pairs={{1,2},{2,1},{3,4},{4,3},{5,6},{6,5},{9,10},{10,9},{11,12},{12,11},... | collective-permute-start | bytes 393224 | tf_op jit(solution)/shard_map/ppermute | solution.py:451
  14.4 3.1 %collective-permute-start.3 = (bf16[2,32,1024]{2,1,0:T(8,128)(2,1)S(1)}, bf16[2,32,1024]{2,1,0:T(8,128)(2,1)S(1)}, u32[]{:S(2)}, u32[]{:S(2)}) collective-permute-start(bf16[2,32,1024]{2,1,0:T(8,128)(2,1)S(1)} %get-tuple-element.25.refs_4_), channel_id=1, source_target_pairs={{0,1},{1,0},{2,3},{3,2},{4,5},{5,4},{6,7},{7,6},{8,9},{9,8},{10,11... | collective-permute-start | bytes 393224 | tf_op jit(solution)/shard_map/ppermute | solution.py:445
  23.8 5.8 %collective-permute-start.4 = (bf16[160,1024]{1,0:T(8,128)(2,1)S(1)}, bf16[160,1024]{1,0:T(8,128)(2,1)S(1)}, u32[]{:S(2)}, u32[]{:S(2)}) collective-permute-start(bf16[160,1024]{1,0:T(8,128)(2,1)S(1)} %get-tuple-element.27), channel_id=1, source_target_pairs={{0,1},{1,0},{2,3},{3,2},{4,5},{5,4},{6,7},{7,6},{8,9},{9,8},{10,11... | collective-permute-start | bytes 983048 | tf_op jit(solution)/shard_map/ppermute | solution.py:445
  24.3 8.4 %collective-permute-start.5 = (bf16[160,1024]{1,0:T(8,128)(2,1)S(1)}, bf16[160,1024]{1,0:T(8,128)(2,1)S(1)}, u32[]{:S(2)}, u32[]{:S(2)}) collective-permute-start(bf16[160,1024]{1,0:T(8,128)(2,1)S(1)} %get-tuple-element.28), channel_id=1, source_target_pairs={{1,2},{2,1},{3,4},{4,3},{5,6},{6,5},{9,10},{10,9},{11,12},{12,11},... | collective-permute-start | bytes 983048 | tf_op jit(solution)/shard_map/ppermute | solution.py:451
  32.8 5.9 %collective-permute-start.6 = (bf16[16,4096]{1,0:T(8,128)(2,1)S(1)}, bf16[16,4096]{1,0:T(8,128)(2,1)S(1)}, u32[]{:S(2)}, u32[]{:S(2)}) collective-permute-start(bf16[16,4096]{1,0:T(8,128)(2,1)S(1)} %get-tuple-element.29), channel_id=1, source_target_pairs={{0,8},{8,0},{16,24},{24,16},{1,9},{9,1},{17,25},{25,17},{2,10},{10... | collective-permute-start | bytes 393224 | tf_op jit(solution)/shard_map/ppermute | solution.py:445
  34.8 7.6 %collective-permute-start.7 = (bf16[16,4096]{1,0:T(8,128)(2,1)S(1)}, bf16[16,4096]{1,0:T(8,128)(2,1)S(1)}, u32[]{:S(2)}, u32[]{:S(2)}) collective-permute-start(bf16[16,4096]{1,0:T(8,128)(2,1)S(1)} %get-tuple-element.30), channel_id=1, source_target_pairs={{8,16},{16,8},{9,17},{17,9},{10,18},{18,10},{11,19},{19,11},{12,20... | collective-permute-start | bytes 393224 | tf_op jit(solution)/shard_map/ppermute | solution.py:451

commit v4 on v3

--- a/solution.py
+++ b/solution.py
@@ -27,6 +27,8 @@
 OROWS = LONG // YPER
 RIM = HALF // YPER
 EDGE = 2 * RIM
+YSTEP = YROWS + 2
+XSTEP = KX + 2
 F32 = jnp.float32
 BF16 = jnp.bfloat16
 
@@ -66,8 +68,9 @@
 def y_inverse():
     block = complex_block(angle(np.arange(LONG), np.arange(LONG), LONG).T, 1.0) / LONG
     block = block.reshape(2, OROWS, YPER, 2 * LONG).transpose(2, 0, 1, 3)
-    block = np.concatenate([block[:, :, :RIM], block[:, :, -RIM:], block[:, :, RIM:-RIM]], 2)
-    return block.reshape(2 * LONG, 2 * LONG)
+    edge = np.concatenate([block[:, :, :RIM], block[:, :, -RIM:]], 2)
+    inner = block[:, :, RIM:-RIM]
+    return edge.reshape(-1, 2 * LONG), inner.reshape(-1, 2 * LONG)
 
 
 def z_inverse():
@@ -114,7 +117,7 @@
         cells = image_ref[patch * PATCH : (patch + 1) * PATCH, at].astype(BF16)
         result = dot(tx_ref[...], cells)
         for h in range(2):
-            swap[pl.ds(2 * t + h, rows, stride=YROWS), :] = result[:, h * LANES : (h + 1) * LANES]
+            swap[pl.ds(2 * t + h, rows, stride=YSTEP), :] = result[:, h * LANES : (h + 1) * LANES]
         return 0
 
     steps = PATCH * DEPTH // tile
@@ -125,18 +128,25 @@
             ready(t, steps)
             along_x(t, 0)
 
-    half = KX * YROWS
-    chunk = 8 * YROWS
-
-    def along_z(t, _):
-        start = pl.multiple_of(t * chunk, chunk)
-        left = jnp.concatenate(
-            [swap[pl.ds(start, chunk), :], swap[pl.ds(half + start, chunk), :]], 1
-        ).astype(BF16)
-        mid[pl.ds(start, chunk), :] = dot(left, tz_ref[...]).astype(BF16)
-        return 0
-
-    lax.fori_loop(0, half // chunk, along_z, 0, unroll=3)
+    group = 8
+
+    def along_z(t):
+        left = [
+            jnp.concatenate(
+                [
+                    swap[pl.ds((c * KX + t * group + k) * YSTEP, YROWS), :].astype(BF16)
+                    for k in range(group)
+                ],
+                0,
+            )
+            for c in range(2)
+        ]
+        chunk = group * YROWS
+        result = dot(jnp.concatenate(left, 1), tz_ref[...])
+        mid[t * chunk : (t + 1) * chunk, :] = result.astype(BF16)
+
+    for t in range(KX // group):
+        along_z(t)
 
     def along_y(t, _):
         pieces = []
@@ -152,7 +162,7 @@
             out_ref[2 * t + h] = result[:, h * LANES : (h + 1) * LANES]
         return 0
 
-    lax.fori_loop(0, KX // 2, along_y, 0, unroll=8)
+    lax.fori_loop(0, KX // 2, along_y, 0, unroll=True)
 
 
 PARTS = 4
@@ -196,7 +206,7 @@
         constant(y_forward(PATCH, YPER)),
     )
     scratch = [
-        pltpu.VMEM((2 * KX * YROWS, LANES), F32),
+        pltpu.VMEM((2 * KX * YSTEP, LANES), F32),
         pltpu.VMEM((KX * YROWS, 2 * YPER * LANES), BF16),
     ]
     common = dict(
@@ -251,13 +261,24 @@
     )(psfs, even, odd)
 
 
+def y_inverted(tiy, product, rows_ref, p, t):
+    back = dot(tiy[...], product).astype(BF16)
+    pairs = back.shape[0] // (2 * YPER)
+    for h in range(2):
+        at = pl.ds(pl.multiple_of((2 * t + h) * pairs, pairs), pairs)
+        for b in range(2 * YPER):
+            rows_ref[p, at, b * LANES : (b + 1) * LANES] = back[
+                b * pairs : (b + 1) * pairs, h * LANES : (h + 1) * LANES
+            ]
+
+
 def z_swapped(rows_ref, tiz, grid_ref, p, pairs, group):
     def along_z(t, _):
         start = pl.multiple_of(t * group * pairs, group * pairs)
         result = dot(rows_ref[p, pl.ds(start, group * pairs), :], tiz[...])
         for k in range(group):
             for c in range(2):
-                grid_ref[p, c, pl.ds(t * group + k, pairs, stride=KX), :] = result[
+                grid_ref[p, c, pl.ds(t * group + k, pairs, stride=XSTEP), :] = result[
                     k * pairs : (k + 1) * pairs, c * LANES : (c + 1) * LANES
                 ]
         return 0
@@ -271,8 +292,7 @@
         for c in range(2):
             parts = []
             for h in range(2):
-                start = pl.multiple_of((2 * t + h) * KX, KX)
-                parts.append(grid_ref[p, c, pl.ds(start, KX), :])
+                parts.append(grid_ref[p, c, pl.ds((2 * t + h) * XSTEP, KX), :])
             pieces.append(jnp.concatenate(parts, 1).astype(BF16))
     return dot(tix[...], jnp.concatenate(pieces, 0))
 
@@ -281,7 +301,7 @@
     spectra = refs[:patches]
     columns = refs[patches : patches + 4]
     tpx, tpz, tpy, tiy, tiz, tix = refs[patches + 4 : patches + 10]
-    inner_ref, to_even_ref, to_odd_ref = refs[patches + 10 : patches + 13]
+    product_ref, to_even_ref, to_odd_ref = refs[patches + 10 : patches + 13]
     pswap, pmid, edge_rows, grid_x = refs[patches + 13 :]
     tile = 2 * LANES
 
@@ -302,8 +322,6 @@
             both = jnp.concatenate([result[:, :, :LANES], result[:, :, LANES:]], 1)
             pmid[p, :, 2 * b * PROWS : 2 * (b + 1) * PROWS, :] = both.astype(BF16)
 
-    inner = OROWS - EDGE
-
     def along_y(t, _):
         for p in range(patches):
             psf = dot(tpy[...], jnp.concatenate([pmid[p, 2 * t], pmid[p, 2 * t + 1]], 1))
@@ -311,19 +329,17 @@
             are, aim = field[:LONG], field[LONG:]
             bre, bim = psf[:LONG], psf[LONG:]
             product = jnp.concatenate([are * bre - aim * bim, are * bim + aim * bre], 0)
-            back = dot(tiy[...], product.astype(BF16)).astype(BF16)
-            for h in range(2):
-                edge_at = pl.ds(pl.multiple_of((2 * t + h) * EDGE, EDGE), EDGE)
-                inner_at = pl.ds(pl.multiple_of((2 * t + h) * inner, inner), inner)
-                for b in range(2 * YPER):
-                    block = back[b * OROWS : (b + 1) * OROWS, h * LANES : (h + 1) * LANES]
-                    at = slice(b * LANES, (b + 1) * LANES)
-                    edge_rows[p, edge_at, at] = block[:EDGE]
-                    inner_ref[p, inner_at, at] = block[EDGE:]
+            product_ref[p, t] = product.astype(BF16)
         return 0
 
-    lax.fori_loop(0, KX // 2, along_y, 0, unroll=8)
-
+    lax.fori_loop(0, KX // 2, along_y, 0, unroll=True)
+
+    def back_along_y(t, _):
+        for p in range(patches):
+            y_inverted(tiy, product_ref[p, t], edge_rows, p, t)
+        return 0
+
+    lax.fori_loop(0, KX // 2, back_along_y, 0, unroll=True)
     for p in range(patches):
         z_swapped(edge_rows, tiz, grid_x, p, EDGE, KX // 2)
     flag = parity("gy")
@@ -336,23 +352,24 @@
 def respond(spectra, columns):
     patches = len(spectra)
     weighted = np.concatenate([w * x_forward(PSFW) for w in BLEND], 1)
+    edge_table, inner_table = [constant(t) for t in y_inverse()]
     z_table = constant(z_inverse())
     x_table = constant(x_inverse(patches))
     tables = (
         constant(weighted),
         constant(z_forward(PSFW, PPER)),
         constant(y_forward(PSFW, PPER)),
-        constant(y_inverse()),
+        edge_table,
         z_table,
         x_table,
     )
     rows = patches * PATCH + PSFW
     rim = (rows, HALF * DEPTH)
     inner = OROWS - EDGE
-    inner_rows, out_even, out_odd = pl.pallas_call(
+    product, out_even, out_odd = pl.pallas_call(
         functools.partial(respond_kernel, patches),
         out_shape=(
-            jax.ShapeDtypeStruct((patches, KX * inner, 2 * YPER * LANES), BF16),
+            jax.ShapeDtypeStruct((patches, KX // 2, 2 * LONG, 2 * LANES), BF16),
             jax.ShapeDtypeStruct(rim, BF16),
             jax.ShapeDtypeStruct(rim, BF16),
         ),
@@ -360,7 +377,7 @@
             pltpu.VMEM((patches, 2 * KX * PROWS, LANES), F32),
             pltpu.VMEM((patches, KX, 2 * PSFW, LANES), BF16),
             pltpu.VMEM((patches, KX * EDGE, 2 * YPER * LANES), BF16),
-            pltpu.VMEM((patches, 2, EDGE * KX, LANES), F32),
+            pltpu.VMEM((patches, 2, EDGE * XSTEP, LANES), F32),
         ],
         compiler_params=pltpu.CompilerParams(vmem_limit_bytes=24 << 20),
         name="respond",
@@ -370,28 +387,35 @@
         return pl.pallas_call(
             middle_kernel,
             out_shape=jax.ShapeDtypeStruct((rows, PATCH * DEPTH), F32),
-            scratch_shapes=[pltpu.VMEM((patches, 2, inner * KX, LANES), F32)],
+            scratch_shapes=[
+                pltpu.VMEM((patches, KX * inner, 2 * YPER * LANES), BF16),
+                pltpu.VMEM((patches, 2, inner * XSTEP, LANES), F32),
+            ],
             compiler_params=pltpu.CompilerParams(vmem_limit_bytes=24 << 20),
             cost_estimate=pl.CostEstimate(
                 flops=3_000_000_000, bytes_accessed=6_000_000, transcendentals=0
             ),
             name="middle",
-        )(inner_rows, z_table, x_table)
+        )(product, inner_table, z_table, x_table)
 
     return middle, out_even, out_odd
 
 
-def middle_kernel(rows_ref, tiz, tix, out_ref, grid_x):
+def middle_kernel(product_ref, tiy, tiz, tix, out_ref, rows_ref, grid_x):
     tile = 2 * LANES
+    patches = product_ref.shape[0]
     inner = OROWS - EDGE
-    for p in range(rows_ref.shape[0]):
-        z_swapped(rows_ref, tiz, grid_x, p, inner, KX // 4)
-
-    def along_x(t, _):
-        out_ref[:, pl.ds(pl.multiple_of(t * tile, tile), tile)] = x_inverted(grid_x, tix, t)
+
+    def along_y(t, _):
+        for p in range(patches):
+            y_inverted(tiy, product_ref[p, t], rows_ref, p, t)
         return 0
 
-    lax.fori_loop(0, inner // 2, along_x, 0, unroll=4)
+    lax.fori_loop(0, KX // 2, along_y, 0, unroll=True)
+    for p in range(patches):
+        z_swapped(rows_ref, tiz, grid_x, p, inner, 8)
+    for t in range(inner // 2):
+        out_ref[:, t * tile : (t + 1) * tile] = x_inverted(grid_x, tix, t)
 
 
 def rim_kernel(mid_ref, even_ref, odd_ref, to_even_ref, to_odd_ref):
@@ -417,27 +441,65 @@
     )(mid, even, odd)
 
 
-def fold_kernel(mid_ref, even_y_ref, odd_y_ref, even_x_ref, odd_x_ref, out_ref):
+def fold_kernel(mid_ref, even_ref, odd_ref, out_ref, rims_ref):
     rows, columns = out_ref.shape
-    band = even_y_ref.shape[1]
-    gx, gy = parity("gx"), parity("gy")
+    band = even_ref.shape[1]
+    gy = parity("gy")
     out_ref[...] = mid_ref[:rows, :]
-    for ref, side in ((even_y_ref, 1 - gy), (odd_y_ref, gy)):
+    for ref, side in ((even_ref, 1 - gy), (odd_ref, gy)):
         at = pl.ds(pl.multiple_of(side * (columns - band), band), band)
         out_ref[:, at] += ref[:rows, :].astype(F32)
-    for ref, side in ((even_x_ref, 1 - gx), (odd_x_ref, gx)):
-        at = pl.ds(pl.multiple_of(side * (rows - HALF), HALF), HALF)
-        out_ref[at, :] += ref[...].astype(F32)
-
-
-def fold(mid, *received):
+    rims_ref[:HALF, :] = out_ref[:HALF, :]
+    rims_ref[HALF:, :] = out_ref[rows - HALF :, :]
+
+
+def fold(mid, even, odd):
     rows = mid.shape[0] - PSFW
     return pl.pallas_call(
         fold_kernel,
-        out_shape=jax.ShapeDtypeStruct((rows, mid.shape[1]), F32),
+        out_shape=(
+            jax.ShapeDtypeStruct((rows, mid.shape[1]), F32),
+            jax.ShapeDtypeStruct((2 * HALF, mid.shape[1]), F32),
+        ),
         compiler_params=pltpu.CompilerParams(vmem_limit_bytes=16 << 20),
+        cost_estimate=pl.CostEstimate(
+            flops=10_000_000, bytes_accessed=8_000_000, transcendentals=0
+        ),
         name="fold",
-    )(mid, *received)
+    )(mid, even, odd)
+
+
+def close_kernel(out_in, rims_ref, even_ref, odd_ref, out_ref, total, sems):
+    del out_in
+    gx = parity("gx")
+    copies = []
+    for k, (ref, side) in enumerate(((even_ref, 1 - gx), (odd_ref, gx))):
+        at = pl.ds(pl.multiple_of(side * HALF, HALF), HALF)
+        total[k] = rims_ref[at, :] + ref[...].astype(F32)
+        first = pl.multiple_of(side * (out_ref.shape[0] - HALF), HALF)
+        copies.append(
+            pltpu.make_async_copy(total.at[k], out_ref.at[pl.ds(first, HALF), :], sems.at[k])
+        )
+        copies[-1].start()
+    for copy in copies:
+        copy.wait()
+
+
+def close(out, rims, even, odd):
+    vmem = pl.BlockSpec(memory_space=pltpu.VMEM)
+    return pl.pallas_call(
+        close_kernel,
+        in_specs=[pl.BlockSpec(memory_space=pl.ANY), vmem, vmem, vmem],
+        out_specs=pl.BlockSpec(memory_space=pl.ANY),
+        out_shape=jax.ShapeDtypeStruct(out.shape, F32),
+        scratch_shapes=[
+            pltpu.VMEM((2, HALF, out.shape[1]), F32),
+            pltpu.SemaphoreType.DMA((2,)),
+        ],
+        input_output_aliases={0: 0},
+        compiler_params=pltpu.CompilerParams(vmem_limit_bytes=16 << 20),
+        name="close",
+    )(out, rims, even, odd)
 
 
 def swap_even(value, axis):
@@ -473,7 +535,8 @@
     out_even, out_odd = x_rims(mid, even_y, odd_y)
     even_x = swap_even(out_even, "gx")
     odd_x = swap_odd(out_odd, "gx")
-    return fold(mid, even_y, odd_y, even_x, odd_x)
+    out, rims = fold(mid, even_y, odd_y)
+    return close(out, rims, even_x, odd_x)
 
 
 def solution(mesh):

time: 44.6 us -> 41.7 us (0.935)
  Pallas kernels: 18.2 us -> 14.4 us
  waiting for transfers between devices: 7.82 us -> 8.27 us
    pallas_call x1, Pallas kernels: 6.25 us -> 4.52 us  [respond(): pl.pallas_call(functools.partial(respond_kernel, patches), out_shape=(jax...]
    pallas_call x1, Pallas kernels: 4.56 us -> 3.21 us  [image_forward(): pl.pallas_call(functools.partial(fetching_kernel, patch), in_specs=[pl.Bl...]
    pallas_call x1, Pallas kernels: 2.98 us -> 1.67 us  [image_forward(): pl.pallas_call(functools.partial(image_kernel, patch), scratch_shapes=scr...]
    pallas_call x1 -> x2, Pallas kernels: 1.61 us -> 2.46 us  [the longest x1 1.62 us: fold(): pl.pallas_call(fold_kernel, out_shape=(jax.ShapeDtypeStruct((rows, mid.sh...]
    ppermute x4, waiting for transfers between devices: 6.8 us -> 7.34 us  [swap_odd(): return lax.ppermute(value, axis, pairs)]
  transfers between devices with their start and end apart: 8 -> 8, of which waited for: 4 -> 5; matrix products, arithmetic and copies ran while one was open for 0% -> 0% of each run, Pallas kernels for 23% -> 22%
where the time goes in v4:
time: 41.7 us; the launch traced here: 40.9 us
  starting transfers between devices  16.9 us (41%)
  Pallas kernels  14.4 us (35%)
  waiting for transfers between devices  8.27 us (20%)
  local copies, waits for them, and re-layouts  1.07 us (3%)
    ppermute x4, starting transfers between devices, swap_odd(): return lax.ppermute(value, axis, pairs)  14.3 us
    ppermute x4, waiting for transfers between devices, swap_odd(): return lax.ppermute(value, axis, pairs)  7.34 us
    pallas_call x1, Pallas kernels, respond(): pl.pallas_call(functools.partial(respond_kernel, patches), out_shape=(jax...  4.52 us
    pallas_call x1, Pallas kernels, image_forward(): pl.pallas_call(functools.partial(fetching_kernel, patch), in_specs=[pl.Bl...  3.21 us
    ppermute x4, starting transfers between devices, swap_even(): lax.ppermute(value, axis, [(i, i ^ 1) for i in range(count) if i ^ 1 < co...  2.64 us
    pallas_call x1, Pallas kernels, middle(): pl.pallas_call(middle_kernel, out_shape=jax.ShapeDtypeStruct((rows, PATCH...  2.3 us
    pallas_call x1, Pallas kernels, image_forward(): pl.pallas_call(functools.partial(image_kernel, patch), scratch_shapes=scr...  1.67 us
    pallas_call x1, Pallas kernels, fold(): pl.pallas_call(fold_kernel, out_shape=(jax.ShapeDtypeStruct((rows, mid.sh...  1.62 us
  transfers between devices with their start and end apart: 8, of which 5 were waited for; matrix products, arithmetic and copies ran while one was open for 0% of the time, Pallas kernels for 22%

profile of v4, /device:TPU:19, one launch (start us, length us, event | category | flops | bytes accessed | tf_op | source)
XLA Modules:
  0.0 40.9 jit_solution(14488580335637007250)
XLA Ops:
  0.0 1.0 %constant_dynamic-slice_fusion = (bf16[1,2,32,1024]{3,2,1,0:T(8,128)(2,1)S(1)}, bf16[1,2,32,1024]{3,2,1,0:T(8,128)(2,1)S(1)}) fusion(bf16[4,2,32,1024]{3,2,1,0:T(8,128)(2,1)} %psfs_ref.1, s32[]{:T(128)S(6)} %select_n.7, s32[]{:T(128)S(6)} %select_n.6), kind=kLoop, calls=%fused_computation | loop fusion | bytes 524296 | tf_op jit(solution)/shard_map/dynamic_slice | solution.py:520
  1.0 3.1 %collective-permute-start.1 = (bf16[1,2,32,1024]{3,2,1,0:T(8,128)(2,1)S(1)}, bf16[1,2,32,1024]{3,2,1,0:T(8,128)(2,1)S(1)}, u32[]{:S(2)}, u32[]{:S(2)}) collective-permute-start(bf16[1,2,32,1024]{3,2,1,0:T(8,128)(2,1)S(1)} %get-tuple-element.35), channel_id=1, source_target_pairs={{8,16},{16,8},{9,17},{17,9},{10,18},{18,10},{11,19},{19,11},{12,20... | collective-permute-start | bytes 393224 | tf_op jit(solution)/shard_map/ppermute | solution.py:513
  4.1 0.0 copy-start.7
  4.1 0.0 copy-start.8
  4.2 0.0 copy-start.10
  4.2 0.0 copy-start.11
  4.2 0.1 collective-permute-start
  4.3 3.2 %image_first.1.refs_0_ = bf16[48,192,128]{2,1,0:T(8,128)(2,1)S(1)} custom-call(f32[128,4096]{1,0:T(8,128)} %image_ref, bf16[96,64]{1,0:T(8,128)(2,1)} %constant.36.clone.refs_0_.tx_ref, bf16[256,512]{1,0:T(8,128)(2,1)} %constant.37.clone.refs_1_.tz_ref, bf16[192,128]{1,0:T(8,128)(2,1)} %constant.38.clone.refs_2_.ty_ref), custom_call_target="tpu_custom_call" | custom-call | flops 4000000000 | bytes 4000000 | tf_op jit(solution)/shard_map/image_first/pallas_call | solution.py:226
  7.5 0.7 %collective-permute-done.1.odd_ref = bf16[1,2,32,1024]{3,2,1,0:T(8,128)(2,1)S(1)} collective-permute-done((bf16[1,2,32,1024]{3,2,1,0:T(8,128)(2,1)S(1)}, bf16[1,2,32,1024]{3,2,1,0:T(8,128)(2,1)S(1)}, u32[]{:S(2)}, u32[]{:S(2)}) %collective-permute-start.1) | collective-permute-done | bytes 131104 | tf_op jit(solution)/shard_map/ppermute | solution.py:513
  8.1 0.9 %collective-permute-done.even_ref = bf16[1,2,32,1024]{3,2,1,0:T(8,128)(2,1)S(1)} collective-permute-done((bf16[1,2,32,1024]{3,2,1,0:T(8,128)(2,1)S(1)}, bf16[1,2,32,1024]{3,2,1,0:T(8,128)(2,1)S(1)}, u32[]{:S(2)}, u32[]{:S(2)}) %collective-permute-start) | collective-permute-done | bytes 131104 | tf_op jit(solution)/shard_map/ppermute | solution.py:507
  9.1 0.2 blend_x.1
  9.3 0.0 copy-start.1
  9.3 0.0 copy-start.2
  9.3 0.0 copy-start.3
  9.3 0.0 copy-start.4
  9.3 0.0 copy-start.5
  9.3 0.0 copy-start.6
  9.3 5.0 %collective-permute-start.2 = (bf16[2,32,1024]{2,1,0:T(8,128)(2,1)S(1)}, bf16[2,32,1024]{2,1,0:T(8,128)(2,1)S(1)}, u32[]{:S(2)}, u32[]{:S(2)}) collective-permute-start(bf16[2,32,1024]{2,1,0:T(8,128)(2,1)S(1)} %get-tuple-element.26.refs_3_), channel_id=1, source_target_pairs={{1,2},{2,1},{3,4},{4,3},{5,6},{6,5},{9,10},{10,9},{11,12},{12,11},... | collective-permute-start | bytes 393224 | tf_op jit(solution)/shard_map/ppermute | solution.py:513
  14.4 0.1 collective-permute-start.3
  14.5 1.7 %image_forward.1.refs_1_ = bf16[48,192,128]{2,1,0:T(8,128)(2,1)S(1)} custom-call(f32[128,4096]{1,0:T(8,128)S(1)} %copy-done.7, bf16[96,64]{1,0:T(8,128)(2,1)S(1)} %copy-done.11, bf16[256,512]{1,0:T(8,128)(2,1)S(1)} %copy-done.8, bf16[192,128]{1,0:T(8,128)(2,1)S(1)} %copy-done.10), custom_call_target="tpu_custom_call" | custom-call | flops 4000000000 | bytes 4000000 | tf_op jit(solution)/shard_map/image_forward/pallas_call | solution.py:220
  16.1 0.0 copy-start.9
  16.2 1.0 %collective-permute-done.2.refs_2_ = bf16[2,32,1024]{2,1,0:T(8,128)(2,1)S(1)} collective-permute-done((bf16[2,32,1024]{2,1,0:T(8,128)(2,1)S(1)}, bf16[2,32,1024]{2,1,0:T(8,128)(2,1)S(1)}, u32[]{:S(2)}, u32[]{:S(2)}) %collective-permute-start.2) | collective-permute-done | bytes 131104 | tf_op jit(solution)/shard_map/ppermute | solution.py:513
  17.2 4.5 %respond.1 = (bf16[2,24,192,256]{3,2,1,0:T(8,128)(2,1)S(1)}, bf16[160,1024]{1,0:T(8,128)(2,1)S(1)}, bf16[160,1024]{1,0:T(8,128)(2,1)S(1)}) custom-call(bf16[48,192,128]{2,1,0:T(8,128)(2,1)S(1)} %image_first.1.refs_0_, bf16[48,192,128]{2,1,0:T(8,128)(2,1)S(1)} %image_forward.1.refs_1_, bf16[2,32,1024]{2,1,0:T(8,128)(2,1)S(1)} %collective-permute-done.2.refs_2_, ...), custom_call_target="tpu_custom_call" | custom-call | tf_op jit(solution)/shard_map/respond/pallas_call | solution.py:369
  21.7 0.5 %collective-permute-start.4 = (bf16[160,1024]{1,0:T(8,128)(2,1)S(1)}, bf16[160,1024]{1,0:T(8,128)(2,1)S(1)}, u32[]{:S(2)}, u32[]{:S(2)}) collective-permute-start(bf16[160,1024]{1,0:T(8,128)(2,1)S(1)} %get-tuple-element.29), channel_id=1, source_target_pairs={{0,1},{1,0},{2,3},{3,2},{4,5},{5,4},{6,7},{7,6},{8,9},{9,8},{10,11... | collective-permute-start | bytes 983048 | tf_op jit(solution)/shard_map/ppermute | solution.py:507
  22.2 3.1 %collective-permute-start.5 = (bf16[160,1024]{1,0:T(8,128)(2,1)S(1)}, bf16[160,1024]{1,0:T(8,128)(2,1)S(1)}, u32[]{:S(2)}, u32[]{:S(2)}) collective-permute-start(bf16[160,1024]{1,0:T(8,128)(2,1)S(1)} %get-tuple-element.30), channel_id=1, source_target_pairs={{1,2},{2,1},{3,4},{4,3},{5,6},{6,5},{9,10},{10,9},{11,12},{12,11},... | collective-permute-start | bytes 983048 | tf_op jit(solution)/shard_map/ppermute | solution.py:513
  25.3 2.3 %middle.1.mid_ref = f32[160,4096]{1,0:T(8,128)S(1)} custom-call(bf16[2,24,192,256]{3,2,1,0:T(8,128)(2,1)S(1)} %get-tuple-element.28.product_ref, bf16[128,192]{1,0:T(8,128)(2,1)S(1)} %copy-done.9, bf16[512,256]{1,0:T(8,128)(2,1)S(1)} %copy-done.2, bf16[160,192]{1,0:T(8,128)(2,1)S(1)} %copy-done.3), custom_call_target="tpu_custom_call" | custom-call | flops 3000000000 | bytes 6000000 | tf_op jit(solution)/shard_map/middle/pallas_call | solution.py:387
  27.6 2.9 %collective-permute-done.5.odd_ref = bf16[160,1024]{1,0:T(8,128)(2,1)S(1)} collective-permute-done((bf16[160,1024]{1,0:T(8,128)(2,1)S(1)}, bf16[160,1024]{1,0:T(8,128)(2,1)S(1)}, u32[]{:S(2)}, u32[]{:S(2)}) %collective-permute-start.5) | collective-permute-done | bytes 327712 | tf_op jit(solution)/shard_map/ppermute | solution.py:513
  30.6 2.0 %collective-permute-start.6 = (bf16[16,4096]{1,0:T(8,128)(2,1)S(1)}, bf16[16,4096]{1,0:T(8,128)(2,1)S(1)}, u32[]{:S(2)}, u32[]{:S(2)}) collective-permute-start(bf16[16,4096]{1,0:T(8,128)(2,1)S(1)} %get-tuple-element.33), channel_id=1, source_target_pairs={{0,8},{8,0},{16,24},{24,16},{1,9},{9,1},{17,25},{25,17},{2,10},{10... | collective-permute-start | bytes 393224 | tf_op jit(solution)/shard_map/ppermute | solution.py:507
  32.6 3.0 %collective-permute-start.7 = (bf16[16,4096]{1,0:T(8,128)(2,1)S(1)}, bf16[16,4096]{1,0:T(8,128)(2,1)S(1)}, u32[]{:S(2)}, u32[]{:S(2)}) collective-permute-start(bf16[16,4096]{1,0:T(8,128)(2,1)S(1)} %get-tuple-element.34), channel_id=1, source_target_pairs={{8,16},{16,8},{9,17},{17,9},{10,18},{18,10},{11,19},{19,11},{12,20... | collective-permute-start | bytes 393224 | tf_op jit(solution)/shard_map/ppermute | solution.py:513
  35.7 1.6 %fold.1 = (f32[128,4096]{1,0:T(8,128)}, f32[32,4096]{1,0:T(8,128)S(1)}) custom-call(f32[160,4096]{1,0:T(8,128)S(1)} %middle.1.mid_ref, bf16[160,1024]{1,0:T(8,128)(2,1)S(1)} %collective-permute-done.4.even_ref, bf16[160,1024]{1,0:T(8,128)(2,1)S(1)} %collective-permute-done.5.odd_ref), custom_call_target="tpu_custom_call" | custom-call | flops 10000000 | bytes 8000000 | tf_op jit(solution)/shard_map/fold/pallas_call | solution.py:458
  37.3 2.7 %collective-permute-done.7.odd_ref = bf16[16,4096]{1,0:T(8,128)(2,1)S(1)} collective-permute-done((bf16[16,4096]{1,0:T(8,128)(2,1)S(1)}, bf16[16,4096]{1,0:T(8,128)(2,1)S(1)}, u32[]{:S(2)}, u32[]{:S(2)}) %collective-permute-start.7) | collective-permute-done | bytes 131104 | tf_op jit(solution)/shard_map/ppermute | solution.py:513
  40.1 0.8 %close.1 = f32[128,4096]{1,0:T(8,128)} custom-call(f32[128,4096]{1,0:T(8,128)} %get-tuple-element.31.out_in, f32[32,4096]{1,0:T(8,128)S(1)} %get-tuple-element.32.rims_ref, bf16[16,4096]{1,0:T(8,128)(2,1)S(1)} %collective-permute-done.6.even_ref, bf16[16,4096]{1,0:T(8,128)(2,1)S(1)} %collective-permute-done.7.odd_ref), custom_call_target="tpu_custom_call", output_to_operand_aliasing={{}: (0, {})} | custom-call | tf_op jit(solution)/shard_map/close/pallas_call | solution.py:490
  (17 shorter events, 0.1 us)
Async XLA Ops:
  1.0 7.2 %collective-permute-start.1 = (bf16[1,2,32,1024]{3,2,1,0:T(8,128)(2,1)S(1)}, bf16[1,2,32,1024]{3,2,1,0:T(8,128)(2,1)S(1)}, u32[]{:S(2)}, u32[]{:S(2)}) collective-permute-start(bf16[1,2,32,1024]{3,2,1,0:T(8,128)(2,1)S(1)} %get-tuple-element.35), channel_id=1, source_target_pairs={{8,16},{16,8},{9,17},{17,9},{10,18},{18,10},{11,19},{19,11},{12,20... | collective-permute-start | bytes 393224 | tf_op jit(solution)/shard_map/ppermute | solution.py:513
  4.1 5.0 %copy-start = (bf16[4,2,32,1024]{3,2,1,0:T(8,128)(2,1)S(1)}, bf16[4,2,32,1024]{3,2,1,0:T(8,128)(2,1)}, u32[]{:S(2)}) copy-start(bf16[4,2,32,1024]{3,2,1,0:T(8,128)(2,1)} %psfs_ref.1) | copy-start | bytes 1572868
  4.1 10.3 %copy-start.7 = (f32[128,4096]{1,0:T(8,128)S(1)}, f32[128,4096]{1,0:T(8,128)}, u32[]{:S(2)}) copy-start(f32[128,4096]{1,0:T(8,128)} %image_ref) | copy-start | bytes 6291460
  4.1 10.3 %copy-start.8 = (bf16[256,512]{1,0:T(8,128)(2,1)S(1)}, bf16[256,512]{1,0:T(8,128)(2,1)}, u32[]{:S(2)}) copy-start(bf16[256,512]{1,0:T(8,128)(2,1)} %constant.37.clone.refs_1_.tz_ref) | copy-start | bytes 786436
  4.2 10.3 %copy-start.10 = (bf16[192,128]{1,0:T(8,128)(2,1)S(1)}, bf16[192,128]{1,0:T(8,128)(2,1)}, u32[]{:S(2)}) copy-start(bf16[192,128]{1,0:T(8,128)(2,1)} %constant.38.clone.refs_2_.ty_ref) | copy-start | bytes 147460
  4.2 10.3 %copy-start.11 = (bf16[96,64]{1,0:T(8,128)(2,1)S(1)}, bf16[96,64]{1,0:T(8,128)(2,1)}, u32[]{:S(2)}) copy-start(bf16[96,64]{1,0:T(8,128)(2,1)} %constant.36.clone.refs_0_.tx_ref) | copy-start | bytes 36868
  4.2 4.9 %collective-permute-start = (bf16[1,2,32,1024]{3,2,1,0:T(8,128)(2,1)S(1)}, bf16[1,2,32,1024]{3,2,1,0:T(8,128)(2,1)S(1)}, u32[]{:S(2)}, u32[]{:S(2)}) collective-permute-start(bf16[1,2,32,1024]{3,2,1,0:T(8,128)(2,1)S(1)} %get-tuple-element.36), channel_id=1, source_target_pairs={{0,8},{8,0},{16,24},{24,16},{1,9},{9,1},{17,25},{25,17},{2,10},{10... | collective-permute-start | bytes 393224 | tf_op jit(solution)/shard_map/ppermute | solution.py:507
  9.3 7.9 %copy-start.1 = (bf16[256,1024]{1,0:T(8,128)(2,1)S(1)}, bf16[256,1024]{1,0:T(8,128)(2,1)}, u32[]{:S(2)}) copy-start(bf16[256,1024]{1,0:T(8,128)(2,1)} %constant.44.clone.refs_7_) | copy-start | bytes 1572868
  9.3 7.9 %copy-start.2 = (bf16[512,256]{1,0:T(8,128)(2,1)S(1)}, bf16[512,256]{1,0:T(8,128)(2,1)}, u32[]{:S(2)}) copy-start(bf16[512,256]{1,0:T(8,128)(2,1)} %constant.41.clone.refs_10_.tiz) | copy-start | bytes 786436
  9.3 7.9 %copy-start.3 = (bf16[160,192]{1,0:T(8,128)(2,1)S(1)}, bf16[160,192]{1,0:T(8,128)(2,1)}, u32[]{:S(2)}) copy-start(bf16[160,192]{1,0:T(8,128)(2,1)} %constant.42.clone.refs_11_.tix) | copy-start | bytes 184324
  9.3 7.9 %copy-start.4 = (bf16[192,64]{1,0:T(8,128)(2,1)S(1)}, bf16[192,64]{1,0:T(8,128)(2,1)}, u32[]{:S(2)}) copy-start(bf16[192,64]{1,0:T(8,128)(2,1)} %constant.45.clone.refs_8_) | copy-start | bytes 73732
  9.3 7.9 %copy-start.5 = (bf16[64,192]{1,0:T(8,128)(2,1)S(1)}, bf16[64,192]{1,0:T(8,128)(2,1)}, u32[]{:S(2)}) copy-start(bf16[64,192]{1,0:T(8,128)(2,1)} %constant.39.clone.refs_9_) | copy-start | bytes 73732
  9.3 7.9 %copy-start.6 = (bf16[96,128]{1,0:T(8,128)(2,1)S(1)}, bf16[96,128]{1,0:T(8,128)(2,1)}, u32[]{:S(2)}) copy-start(bf16[96,128]{1,0:T(8,128)(2,1)} %constant.43.clone.refs_6_) | copy-start | bytes 73732
  9.3 7.8 %collective-permute-start.2 = (bf16[2,32,1024]{2,1,0:T(8,128)(2,1)S(1)}, bf16[2,32,1024]{2,1,0:T(8,128)(2,1)S(1)}, u32[]{:S(2)}, u32[]{:S(2)}) collective-permute-start(bf16[2,32,1024]{2,1,0:T(8,128)(2,1)S(1)} %get-tuple-element.26.refs_3_), channel_id=1, source_target_pairs={{1,2},{2,1},{3,4},{4,3},{5,6},{6,5},{9,10},{10,9},{11,12},{12,11},... | collective-permute-start | bytes 393224 | tf_op jit(solution)/shard_map/ppermute | solution.py:513
  14.4 2.8 %collective-permute-start.3 = (bf16[2,32,1024]{2,1,0:T(8,128)(2,1)S(1)}, bf16[2,32,1024]{2,1,0:T(8,128)(2,1)S(1)}, u32[]{:S(2)}, u32[]{:S(2)}) collective-permute-start(bf16[2,32,1024]{2,1,0:T(8,128)(2,1)S(1)} %get-tuple-element.27.refs_4_), channel_id=1, source_target_pairs={{0,1},{1,0},{2,3},{3,2},{4,5},{5,4},{6,7},{7,6},{8,9},{9,8},{10,11... | collective-permute-start | bytes 393224 | tf_op jit(solution)/shard_map/ppermute | solution.py:507
  16.1 9.2 %copy-start.9 = (bf16[128,192]{1,0:T(8,128)(2,1)S(1)}, bf16[128,192]{1,0:T(8,128)(2,1)}, u32[]{:S(2)}) copy-start(bf16[128,192]{1,0:T(8,128)(2,1)} %constant.40.clone.tiy) | copy-start | bytes 147460
  21.7 5.9 %collective-permute-start.4 = (bf16[160,1024]{1,0:T(8,128)(2,1)S(1)}, bf16[160,1024]{1,0:T(8,128)(2,1)S(1)}, u32[]{:S(2)}, u32[]{:S(2)}) collective-permute-start(bf16[160,1024]{1,0:T(8,128)(2,1)S(1)} %get-tuple-element.29), channel_id=1, source_target_pairs={{0,1},{1,0},{2,3},{3,2},{4,5},{5,4},{6,7},{7,6},{8,9},{9,8},{10,11... | collective-permute-start | bytes 983048 | tf_op jit(solution)/shard_map/ppermute | solution.py:507
  22.2 8.4 %collective-permute-start.5 = (bf16[160,1024]{1,0:T(8,128)(2,1)S(1)}, bf16[160,1024]{1,0:T(8,128)(2,1)S(1)}, u32[]{:S(2)}, u32[]{:S(2)}) collective-permute-start(bf16[160,1024]{1,0:T(8,128)(2,1)S(1)} %get-tuple-element.30), channel_id=1, source_target_pairs={{1,2},{2,1},{3,4},{4,3},{5,6},{6,5},{9,10},{10,9},{11,12},{12,11},... | collective-permute-start | bytes 983048 | tf_op jit(solution)/shard_map/ppermute | solution.py:513
  30.6 6.7 %collective-permute-start.6 = (bf16[16,4096]{1,0:T(8,128)(2,1)S(1)}, bf16[16,4096]{1,0:T(8,128)(2,1)S(1)}, u32[]{:S(2)}, u32[]{:S(2)}) collective-permute-start(bf16[16,4096]{1,0:T(8,128)(2,1)S(1)} %get-tuple-element.33), channel_id=1, source_target_pairs={{0,8},{8,0},{16,24},{24,16},{1,9},{9,1},{17,25},{25,17},{2,10},{10... | collective-permute-start | bytes 393224 | tf_op jit(solution)/shard_map/ppermute | solution.py:507
  32.6 7.4 %collective-permute-start.7 = (bf16[16,4096]{1,0:T(8,128)(2,1)S(1)}, bf16[16,4096]{1,0:T(8,128)(2,1)S(1)}, u32[]{:S(2)}, u32[]{:S(2)}) collective-permute-start(bf16[16,4096]{1,0:T(8,128)(2,1)S(1)} %get-tuple-element.34), channel_id=1, source_target_pairs={{8,16},{16,8},{9,17},{17,9},{10,18},{18,10},{11,19},{19,11},{12,20... | collective-permute-start | bytes 393224 | tf_op jit(solution)/shard_map/ppermute | solution.py:513

commit v5 on v4

--- a/solution.py
+++ b/solution.py
@@ -236,7 +236,7 @@
     )(*[pltpu.with_memory_space_constraint(x, pltpu.HBM) for x in (image, *tables)])
 
 
-def blend_kernel(psfs_ref, even_ref, odd_ref, to_even_ref, to_odd_ref):
+def blend_kernel(psfs_ref, odd_ref, even_ref, to_even_ref, to_odd_ref):
     count = psfs_ref.shape[0]
     gx, gy = parity("gx"), parity("gy")
     for out, column in ((to_even_ref, 1 - gy), (to_odd_ref, gy)):
@@ -251,14 +251,14 @@
             out[p] = total.astype(BF16)
 
 
-def blend_x(psfs, even, odd):
+def blend_x(psfs, odd, even):
     shape = (psfs.shape[0] // 2,) + psfs.shape[2:]
     return pl.pallas_call(
         blend_kernel,
         out_shape=(jax.ShapeDtypeStruct(shape, BF16),) * 2,
         compiler_params=pltpu.CompilerParams(vmem_limit_bytes=16 << 20),
         name="blend_x",
-    )(psfs, even, odd)
+    )(psfs, odd, even)
 
 
 def y_inverted(tiy, product, rows_ref, p, t):
@@ -522,13 +522,13 @@
     even = swap_even(to_even, "gx")
     odd = swap_odd(to_odd, "gx")
     spectra = [image_forward(image, 0)]
-    spectra[0], even, odd = lax.optimization_barrier((spectra[0], even, odd))
-    to_even, to_odd = blend_x(psfs, even, odd)
+    spectra[0], odd, even = lax.optimization_barrier((spectra[0], odd, even))
+    to_even, to_odd = blend_x(psfs, odd, even)
     image, to_even, to_odd = lax.optimization_barrier((image, to_even, to_odd))
     even = swap_even(to_even, "gy")
     odd = swap_odd(to_odd, "gy")
     spectra += [image_forward(image, p) for p in range(1, patches)]
-    middle, out_even, out_odd = respond(spectra, (odd, to_odd, to_even, even))
+    middle, out_even, out_odd = respond(spectra, (even, to_even, to_odd, odd))
     odd_y = swap_odd(out_odd, "gy")
     even_y = swap_even(out_even, "gy")
     mid = middle()

time: 41.7 us -> 40.3 us (0.966)
  waiting for transfers between devices: 8.27 us -> 7.61 us
    ppermute x4, waiting for transfers between devices: 0.93 us -> 0.01 us  [swap_even(): lax.ppermute(value, axis, [(i, i ^ 1) for i in range(count) if i ^ 1 < co...]
    ppermute x4, starting transfers between devices: 2.64 us -> 2.12 us  [swap_even(): lax.ppermute(value, axis, [(i, i ^ 1) for i in range(count) if i ^ 1 < co...]
  transfers between devices with their start and end apart: 8 -> 8, of which waited for: 5 -> 4; matrix products, arithmetic and copies ran while one was open for 0% -> 0% of each run, Pallas kernels for 22% -> 22%
where the time goes in v5:
time: 40.3 us; the launch traced here: 39.6 us
  starting transfers between devices  16.5 us (41%)
  Pallas kernels  14.2 us (35%)
  waiting for transfers between devices  7.61 us (19%)
  local copies, waits for them, and re-layouts  1.05 us (3%)
    ppermute x4, starting transfers between devices, swap_odd(): return lax.ppermute(value, axis, pairs)  14.3 us
    ppermute x4, waiting for transfers between devices, swap_odd(): return lax.ppermute(value, axis, pairs)  7.6 us
    pallas_call x1, Pallas kernels, respond(): pl.pallas_call(functools.partial(respond_kernel, patches), out_shape=(jax...  4.52 us
    pallas_call x1, Pallas kernels, image_forward(): pl.pallas_call(functools.partial(fetching_kernel, patch), in_specs=[pl.Bl...  3.06 us
    pallas_call x1, Pallas kernels, middle(): pl.pallas_call(middle_kernel, out_shape=jax.ShapeDtypeStruct((rows, PATCH...  2.3 us
    ppermute x4, starting transfers between devices, swap_even(): lax.ppermute(value, axis, [(i, i ^ 1) for i in range(count) if i ^ 1 < co...  2.12 us
    pallas_call x1, Pallas kernels, image_forward(): pl.pallas_call(functools.partial(image_kernel, patch), scratch_shapes=scr...  1.66 us
    pallas_call x1, Pallas kernels, fold(): pl.pallas_call(fold_kernel, out_shape=(jax.ShapeDtypeStruct((rows, mid.sh...  1.62 us
  transfers between devices with their start and end apart: 8, of which 4 were waited for; matrix products, arithmetic and copies ran while one was open for 0% of the time, Pallas kernels for 22%

profile of v5, /device:TPU:19, one launch (start us, length us, event | category | flops | bytes accessed | tf_op | source)
XLA Modules:
  0.0 39.6 jit_solution(15596235217278387094)
XLA Ops:
  0.0 1.0 %constant_dynamic-slice_fusion = (bf16[1,2,32,1024]{3,2,1,0:T(8,128)(2,1)S(1)}, bf16[1,2,32,1024]{3,2,1,0:T(8,128)(2,1)S(1)}) fusion(bf16[4,2,32,1024]{3,2,1,0:T(8,128)(2,1)} %psfs_ref.1, s32[]{:T(128)S(6)} %select_n.7, s32[]{:T(128)S(6)} %select_n.6), kind=kLoop, calls=%fused_computation | loop fusion | bytes 524296 | tf_op jit(solution)/shard_map/dynamic_slice | solution.py:521
  1.0 0.3 collective-permute-start.1
  1.3 0.0 copy-start.11
  1.3 4.3 %collective-permute-start = (bf16[1,2,32,1024]{3,2,1,0:T(8,128)(2,1)S(1)}, bf16[1,2,32,1024]{3,2,1,0:T(8,128)(2,1)S(1)}, u32[]{:S(2)}, u32[]{:S(2)}) collective-permute-start(bf16[1,2,32,1024]{3,2,1,0:T(8,128)(2,1)S(1)} %get-tuple-element.36), channel_id=1, source_target_pairs={{8,16},{16,8},{9,17},{17,9},{10,18},{18,10},{11,19},{19,11},{12,20... | collective-permute-start | bytes 393224 | tf_op jit(solution)/shard_map/ppermute | solution.py:513
  5.7 3.1 %image_first.1.refs_0_ = bf16[48,192,128]{2,1,0:T(8,128)(2,1)S(1)} custom-call(f32[128,4096]{1,0:T(8,128)} %image_ref, bf16[96,64]{1,0:T(8,128)(2,1)} %constant.36.clone.refs_0_.tx_ref, bf16[256,512]{1,0:T(8,128)(2,1)} %constant.37.clone.refs_1_.tz_ref, bf16[192,128]{1,0:T(8,128)(2,1)} %constant.38.clone.refs_2_.ty_ref), custom_call_target="tpu_custom_call" | custom-call | flops 4000000000 | bytes 4000000 | tf_op jit(solution)/shard_map/image_first/pallas_call | solution.py:226
  8.8 0.0 collective-permute-done.1.even_ref
  8.8 0.5 %collective-permute-done.odd_ref = bf16[1,2,32,1024]{3,2,1,0:T(8,128)(2,1)S(1)} collective-permute-done((bf16[1,2,32,1024]{3,2,1,0:T(8,128)(2,1)S(1)}, bf16[1,2,32,1024]{3,2,1,0:T(8,128)(2,1)S(1)}, u32[]{:S(2)}, u32[]{:S(2)}) %collective-permute-start) | collective-permute-done | bytes 131104 | tf_op jit(solution)/shard_map/ppermute | solution.py:513
  9.3 0.2 blend_x.1
  9.5 0.0 copy-start.1
  9.5 0.0 copy-start.2
  9.5 0.0 copy-start.3
  9.5 0.0 copy-start.4
  9.5 0.0 copy-start.5
  9.6 0.0 copy-start.6
  9.6 1.5 %collective-permute-start.2 = (bf16[2,32,1024]{2,1,0:T(8,128)(2,1)S(1)}, bf16[2,32,1024]{2,1,0:T(8,128)(2,1)S(1)}, u32[]{:S(2)}, u32[]{:S(2)}) collective-permute-start(bf16[2,32,1024]{2,1,0:T(8,128)(2,1)S(1)} %get-tuple-element.26.refs_3_), channel_id=1, source_target_pairs={{0,1},{1,0},{2,3},{3,2},{4,5},{5,4},{6,7},{7,6},{8,9},{9,8},{10,11... | collective-permute-start | bytes 393224 | tf_op jit(solution)/shard_map/ppermute | solution.py:507
  11.1 3.2 %collective-permute-start.3 = (bf16[2,32,1024]{2,1,0:T(8,128)(2,1)S(1)}, bf16[2,32,1024]{2,1,0:T(8,128)(2,1)S(1)}, u32[]{:S(2)}, u32[]{:S(2)}) collective-permute-start(bf16[2,32,1024]{2,1,0:T(8,128)(2,1)S(1)} %get-tuple-element.27.refs_4_), channel_id=1, source_target_pairs={{1,2},{2,1},{3,4},{4,3},{5,6},{6,5},{9,10},{10,9},{11,12},{12,11},... | collective-permute-start | bytes 393224 | tf_op jit(solution)/shard_map/ppermute | solution.py:513
  14.4 1.7 %image_forward.1.refs_1_ = bf16[48,192,128]{2,1,0:T(8,128)(2,1)S(1)} custom-call(f32[128,4096]{1,0:T(8,128)S(1)} %copy-done.7, bf16[96,64]{1,0:T(8,128)(2,1)S(1)} %copy-done.11, bf16[256,512]{1,0:T(8,128)(2,1)S(1)} %copy-done.8, bf16[192,128]{1,0:T(8,128)(2,1)S(1)} %copy-done.10), custom_call_target="tpu_custom_call" | custom-call | flops 4000000000 | bytes 4000000 | tf_op jit(solution)/shard_map/image_forward/pallas_call | solution.py:220
  16.0 0.0 copy-start.9
  16.0 0.0 collective-permute-done.2.refs_2_
  16.1 1.3 %collective-permute-done.3.refs_5_ = bf16[2,32,1024]{2,1,0:T(8,128)(2,1)S(1)} collective-permute-done((bf16[2,32,1024]{2,1,0:T(8,128)(2,1)S(1)}, bf16[2,32,1024]{2,1,0:T(8,128)(2,1)S(1)}, u32[]{:S(2)}, u32[]{:S(2)}) %collective-permute-start.3) | collective-permute-done | bytes 131104 | tf_op jit(solution)/shard_map/ppermute | solution.py:513
  17.4 4.5 %respond.1 = (bf16[2,24,192,256]{3,2,1,0:T(8,128)(2,1)S(1)}, bf16[160,1024]{1,0:T(8,128)(2,1)S(1)}, bf16[160,1024]{1,0:T(8,128)(2,1)S(1)}) custom-call(bf16[48,192,128]{2,1,0:T(8,128)(2,1)S(1)} %image_first.1.refs_0_, bf16[48,192,128]{2,1,0:T(8,128)(2,1)S(1)} %image_forward.1.refs_1_, bf16[2,32,1024]{2,1,0:T(8,128)(2,1)S(1)} %collective-permute-done.2.refs_2_, ...), custom_call_target="tpu_custom_call" | custom-call | tf_op jit(solution)/shard_map/respond/pallas_call | solution.py:369
  21.9 0.2 collective-permute-start.4
  22.1 3.1 %collective-permute-start.5 = (bf16[160,1024]{1,0:T(8,128)(2,1)S(1)}, bf16[160,1024]{1,0:T(8,128)(2,1)S(1)}, u32[]{:S(2)}, u32[]{:S(2)}) collective-permute-start(bf16[160,1024]{1,0:T(8,128)(2,1)S(1)} %get-tuple-element.30), channel_id=1, source_target_pairs={{1,2},{2,1},{3,4},{4,3},{5,6},{6,5},{9,10},{10,9},{11,12},{12,11},... | collective-permute-start | bytes 983048 | tf_op jit(solution)/shard_map/ppermute | solution.py:513
  25.3 2.3 %middle.1.mid_ref = f32[160,4096]{1,0:T(8,128)S(1)} custom-call(bf16[2,24,192,256]{3,2,1,0:T(8,128)(2,1)S(1)} %get-tuple-element.28.product_ref, bf16[128,192]{1,0:T(8,128)(2,1)S(1)} %copy-done.9, bf16[512,256]{1,0:T(8,128)(2,1)S(1)} %copy-done.2, bf16[160,192]{1,0:T(8,128)(2,1)S(1)} %copy-done.3), custom_call_target="tpu_custom_call" | custom-call | flops 3000000000 | bytes 6000000 | tf_op jit(solution)/shard_map/middle/pallas_call | solution.py:387
  27.6 0.0 collective-permute-done.4.even_ref
  27.6 2.9 %collective-permute-done.5.odd_ref = bf16[160,1024]{1,0:T(8,128)(2,1)S(1)} collective-permute-done((bf16[160,1024]{1,0:T(8,128)(2,1)S(1)}, bf16[160,1024]{1,0:T(8,128)(2,1)S(1)}, u32[]{:S(2)}, u32[]{:S(2)}) %collective-permute-start.5) | collective-permute-done | bytes 327712 | tf_op jit(solution)/shard_map/ppermute | solution.py:513
  30.6 0.1 collective-permute-start.6
  30.6 3.7 %collective-permute-start.7 = (bf16[16,4096]{1,0:T(8,128)(2,1)S(1)}, bf16[16,4096]{1,0:T(8,128)(2,1)S(1)}, u32[]{:S(2)}, u32[]{:S(2)}) collective-permute-start(bf16[16,4096]{1,0:T(8,128)(2,1)S(1)} %get-tuple-element.34), channel_id=1, source_target_pairs={{8,16},{16,8},{9,17},{17,9},{10,18},{18,10},{11,19},{19,11},{12,20... | collective-permute-start | bytes 393224 | tf_op jit(solution)/shard_map/ppermute | solution.py:513
  34.3 1.6 %fold.1 = (f32[128,4096]{1,0:T(8,128)}, f32[32,4096]{1,0:T(8,128)S(1)}) custom-call(f32[160,4096]{1,0:T(8,128)S(1)} %middle.1.mid_ref, bf16[160,1024]{1,0:T(8,128)(2,1)S(1)} %collective-permute-done.4.even_ref, bf16[160,1024]{1,0:T(8,128)(2,1)S(1)} %collective-permute-done.5.odd_ref), custom_call_target="tpu_custom_call" | custom-call | flops 10000000 | bytes 8000000 | tf_op jit(solution)/shard_map/fold/pallas_call | solution.py:458
  35.9 0.0 collective-permute-done.6.even_ref
  35.9 2.8 %collective-permute-done.7.odd_ref = bf16[16,4096]{1,0:T(8,128)(2,1)S(1)} collective-permute-done((bf16[16,4096]{1,0:T(8,128)(2,1)S(1)}, bf16[16,4096]{1,0:T(8,128)(2,1)S(1)}, u32[]{:S(2)}, u32[]{:S(2)}) %collective-permute-start.7) | collective-permute-done | bytes 131104 | tf_op jit(solution)/shard_map/ppermute | solution.py:513
  38.8 0.8 %close.1 = f32[128,4096]{1,0:T(8,128)} custom-call(f32[128,4096]{1,0:T(8,128)} %get-tuple-element.31.out_in, f32[32,4096]{1,0:T(8,128)S(1)} %get-tuple-element.32.rims_ref, bf16[16,4096]{1,0:T(8,128)(2,1)S(1)} %collective-permute-done.6.even_ref, bf16[16,4096]{1,0:T(8,128)(2,1)S(1)} %collective-permute-done.7.odd_ref), custom_call_target="tpu_custom_call", output_to_operand_aliasing={{}: (0, {})} | custom-call | tf_op jit(solution)/shard_map/close/pallas_call | solution.py:490
  (17 shorter events, 0.1 us)
Async XLA Ops:
  1.0 7.8 %collective-permute-start.1 = (bf16[1,2,32,1024]{3,2,1,0:T(8,128)(2,1)S(1)}, bf16[1,2,32,1024]{3,2,1,0:T(8,128)(2,1)S(1)}, u32[]{:S(2)}, u32[]{:S(2)}) collective-permute-start(bf16[1,2,32,1024]{3,2,1,0:T(8,128)(2,1)S(1)} %get-tuple-element.35), channel_id=1, source_target_pairs={{0,8},{8,0},{16,24},{24,16},{1,9},{9,1},{17,25},{25,17},{2,10},{10... | collective-permute-start | bytes 393224 | tf_op jit(solution)/shard_map/ppermute | solution.py:507
  1.3 8.0 %copy-start = (bf16[4,2,32,1024]{3,2,1,0:T(8,128)(2,1)S(1)}, bf16[4,2,32,1024]{3,2,1,0:T(8,128)(2,1)}, u32[]{:S(2)}) copy-start(bf16[4,2,32,1024]{3,2,1,0:T(8,128)(2,1)} %psfs_ref.1) | copy-start | bytes 1572868
  1.3 13.0 %copy-start.7 = (f32[128,4096]{1,0:T(8,128)S(1)}, f32[128,4096]{1,0:T(8,128)}, u32[]{:S(2)}) copy-start(f32[128,4096]{1,0:T(8,128)} %image_ref) | copy-start | bytes 6291460
  1.3 13.0 %copy-start.8 = (bf16[256,512]{1,0:T(8,128)(2,1)S(1)}, bf16[256,512]{1,0:T(8,128)(2,1)}, u32[]{:S(2)}) copy-start(bf16[256,512]{1,0:T(8,128)(2,1)} %constant.37.clone.refs_1_.tz_ref) | copy-start | bytes 786436
  1.3 13.0 %copy-start.10 = (bf16[192,128]{1,0:T(8,128)(2,1)S(1)}, bf16[192,128]{1,0:T(8,128)(2,1)}, u32[]{:S(2)}) copy-start(bf16[192,128]{1,0:T(8,128)(2,1)} %constant.38.clone.refs_2_.ty_ref) | copy-start | bytes 147460
  1.3 13.0 %copy-start.11 = (bf16[96,64]{1,0:T(8,128)(2,1)S(1)}, bf16[96,64]{1,0:T(8,128)(2,1)}, u32[]{:S(2)}) copy-start(bf16[96,64]{1,0:T(8,128)(2,1)} %constant.36.clone.refs_0_.tx_ref) | copy-start | bytes 36868
  1.3 8.0 %collective-permute-start = (bf16[1,2,32,1024]{3,2,1,0:T(8,128)(2,1)S(1)}, bf16[1,2,32,1024]{3,2,1,0:T(8,128)(2,1)S(1)}, u32[]{:S(2)}, u32[]{:S(2)}) collective-permute-start(bf16[1,2,32,1024]{3,2,1,0:T(8,128)(2,1)S(1)} %get-tuple-element.36), channel_id=1, source_target_pairs={{8,16},{16,8},{9,17},{17,9},{10,18},{18,10},{11,19},{19,11},{12,20... | collective-permute-start | bytes 393224 | tf_op jit(solution)/shard_map/ppermute | solution.py:513
  9.5 7.9 %copy-start.1 = (bf16[256,1024]{1,0:T(8,128)(2,1)S(1)}, bf16[256,1024]{1,0:T(8,128)(2,1)}, u32[]{:S(2)}) copy-start(bf16[256,1024]{1,0:T(8,128)(2,1)} %constant.44.clone.refs_7_) | copy-start | bytes 1572868
  9.5 7.8 %copy-start.2 = (bf16[512,256]{1,0:T(8,128)(2,1)S(1)}, bf16[512,256]{1,0:T(8,128)(2,1)}, u32[]{:S(2)}) copy-start(bf16[512,256]{1,0:T(8,128)(2,1)} %constant.41.clone.refs_10_.tiz) | copy-start | bytes 786436
  9.5 7.8 %copy-start.3 = (bf16[160,192]{1,0:T(8,128)(2,1)S(1)}, bf16[160,192]{1,0:T(8,128)(2,1)}, u32[]{:S(2)}) copy-start(bf16[160,192]{1,0:T(8,128)(2,1)} %constant.42.clone.refs_11_.tix) | copy-start | bytes 184324
  9.5 7.8 %copy-start.4 = (bf16[192,64]{1,0:T(8,128)(2,1)S(1)}, bf16[192,64]{1,0:T(8,128)(2,1)}, u32[]{:S(2)}) copy-start(bf16[192,64]{1,0:T(8,128)(2,1)} %constant.45.clone.refs_8_) | copy-start | bytes 73732
  9.5 7.8 %copy-start.5 = (bf16[64,192]{1,0:T(8,128)(2,1)S(1)}, bf16[64,192]{1,0:T(8,128)(2,1)}, u32[]{:S(2)}) copy-start(bf16[64,192]{1,0:T(8,128)(2,1)} %constant.39.clone.refs_9_) | copy-start | bytes 73732
  9.6 7.8 %copy-start.6 = (bf16[96,128]{1,0:T(8,128)(2,1)S(1)}, bf16[96,128]{1,0:T(8,128)(2,1)}, u32[]{:S(2)}) copy-start(bf16[96,128]{1,0:T(8,128)(2,1)} %constant.43.clone.refs_6_) | copy-start | bytes 73732
  9.6 6.5 %collective-permute-start.2 = (bf16[2,32,1024]{2,1,0:T(8,128)(2,1)S(1)}, bf16[2,32,1024]{2,1,0:T(8,128)(2,1)S(1)}, u32[]{:S(2)}, u32[]{:S(2)}) collective-permute-start(bf16[2,32,1024]{2,1,0:T(8,128)(2,1)S(1)} %get-tuple-element.26.refs_3_), channel_id=1, source_target_pairs={{0,1},{1,0},{2,3},{3,2},{4,5},{5,4},{6,7},{7,6},{8,9},{9,8},{10,11... | collective-permute-start | bytes 393224 | tf_op jit(solution)/shard_map/ppermute | solution.py:507
  11.1 6.3 %collective-permute-start.3 = (bf16[2,32,1024]{2,1,0:T(8,128)(2,1)S(1)}, bf16[2,32,1024]{2,1,0:T(8,128)(2,1)S(1)}, u32[]{:S(2)}, u32[]{:S(2)}) collective-permute-start(bf16[2,32,1024]{2,1,0:T(8,128)(2,1)S(1)} %get-tuple-element.27.refs_4_), channel_id=1, source_target_pairs={{1,2},{2,1},{3,4},{4,3},{5,6},{6,5},{9,10},{10,9},{11,12},{12,11},... | collective-permute-start | bytes 393224 | tf_op jit(solution)/shard_map/ppermute | solution.py:513
  16.0 9.2 %copy-start.9 = (bf16[128,192]{1,0:T(8,128)(2,1)S(1)}, bf16[128,192]{1,0:T(8,128)(2,1)}, u32[]{:S(2)}) copy-start(bf16[128,192]{1,0:T(8,128)(2,1)} %constant.40.clone.tiy) | copy-start | bytes 147460
  21.9 5.7 %collective-permute-start.4 = (bf16[160,1024]{1,0:T(8,128)(2,1)S(1)}, bf16[160,1024]{1,0:T(8,128)(2,1)S(1)}, u32[]{:S(2)}, u32[]{:S(2)}) collective-permute-start(bf16[160,1024]{1,0:T(8,128)(2,1)S(1)} %get-tuple-element.29), channel_id=1, source_target_pairs={{0,1},{1,0},{2,3},{3,2},{4,5},{5,4},{6,7},{7,6},{8,9},{9,8},{10,11... | collective-permute-start | bytes 983048 | tf_op jit(solution)/shard_map/ppermute | solution.py:507
  22.1 8.4 %collective-permute-start.5 = (bf16[160,1024]{1,0:T(8,128)(2,1)S(1)}, bf16[160,1024]{1,0:T(8,128)(2,1)S(1)}, u32[]{:S(2)}, u32[]{:S(2)}) collective-permute-start(bf16[160,1024]{1,0:T(8,128)(2,1)S(1)} %get-tuple-element.30), channel_id=1, source_target_pairs={{1,2},{2,1},{3,4},{4,3},{5,6},{6,5},{9,10},{10,9},{11,12},{12,11},... | collective-permute-start | bytes 983048 | tf_op jit(solution)/shard_map/ppermute | solution.py:513
  30.6 5.4 %collective-permute-start.6 = (bf16[16,4096]{1,0:T(8,128)(2,1)S(1)}, bf16[16,4096]{1,0:T(8,128)(2,1)S(1)}, u32[]{:S(2)}, u32[]{:S(2)}) collective-permute-start(bf16[16,4096]{1,0:T(8,128)(2,1)S(1)} %get-tuple-element.33), channel_id=1, source_target_pairs={{0,8},{8,0},{16,24},{24,16},{1,9},{9,1},{17,25},{25,17},{2,10},{10... | collective-permute-start | bytes 393224 | tf_op jit(solution)/shard_map/ppermute | solution.py:507
  30.6 8.1 %collective-permute-start.7 = (bf16[16,4096]{1,0:T(8,128)(2,1)S(1)}, bf16[16,4096]{1,0:T(8,128)(2,1)S(1)}, u32[]{:S(2)}, u32[]{:S(2)}) collective-permute-start(bf16[16,4096]{1,0:T(8,128)(2,1)S(1)} %get-tuple-element.34), channel_id=1, source_target_pairs={{8,16},{16,8},{9,17},{17,9},{10,18},{18,10},{11,19},{19,11},{12,20... | collective-permute-start | bytes 393224 | tf_op jit(solution)/shard_map/ppermute | solution.py:513

commit v6 on v5

--- a/solution.py
+++ b/solution.py
@@ -325,11 +325,12 @@
     def along_y(t, _):
         for p in range(patches):
             psf = dot(tpy[...], jnp.concatenate([pmid[p, 2 * t], pmid[p, 2 * t + 1]], 1))
-            field = jnp.concatenate([spectra[p][2 * t], spectra[p][2 * t + 1]], 1).astype(F32)
+            psf = psf.astype(BF16)
+            field = jnp.concatenate([spectra[p][2 * t], spectra[p][2 * t + 1]], 1)
             are, aim = field[:LONG], field[LONG:]
             bre, bim = psf[:LONG], psf[LONG:]
             product = jnp.concatenate([are * bre - aim * bim, are * bim + aim * bre], 0)
-            product_ref[p, t] = product.astype(BF16)
+            product_ref[p, t] = product
         return 0
 
     lax.fori_loop(0, KX // 2, along_y, 0, unroll=True)

time: 40.3 us -> 39.4 us (0.978)
  Pallas kernels: 14.2 us -> 13.4 us
    pallas_call x1, Pallas kernels: 4.52 us -> 3.66 us  [respond(): pl.pallas_call(functools.partial(respond_kernel, patches), out_shape=(jax...]
where the time goes in v6:
time: 39.4 us; the launch traced here: 38.7 us
  starting transfers between devices  16.4 us (42%)
  Pallas kernels  13.4 us (34%)
  waiting for transfers between devices  7.61 us (19%)
  local copies, waits for them, and re-layouts  1.05 us (3%)
    ppermute x4, starting transfers between devices, swap_odd(): return lax.ppermute(value, axis, pairs)  14.3 us
    ppermute x4, waiting for transfers between devices, swap_odd(): return lax.ppermute(value, axis, pairs)  7.6 us
    pallas_call x1, Pallas kernels, respond(): pl.pallas_call(functools.partial(respond_kernel, patches), out_shape=(jax...  3.66 us
    pallas_call x1, Pallas kernels, image_forward(): pl.pallas_call(functools.partial(fetching_kernel, patch), in_specs=[pl.Bl...  3.06 us
    pallas_call x1, Pallas kernels, middle(): pl.pallas_call(middle_kernel, out_shape=jax.ShapeDtypeStruct((rows, PATCH...  2.3 us
    ppermute x4, starting transfers between devices, swap_even(): lax.ppermute(value, axis, [(i, i ^ 1) for i in range(count) if i ^ 1 < co...  2.12 us
    pallas_call x1, Pallas kernels, image_forward(): pl.pallas_call(functools.partial(image_kernel, patch), scratch_shapes=scr...  1.66 us
    pallas_call x1, Pallas kernels, fold(): pl.pallas_call(fold_kernel, out_shape=(jax.ShapeDtypeStruct((rows, mid.sh...  1.62 us
  transfers between devices with their start and end apart: 8, of which 4 were waited for; matrix products, arithmetic and copies ran while one was open for 0% of the time, Pallas kernels for 22%

profile of v6, /device:TPU:19, one launch (start us, length us, event | category | flops | bytes accessed | tf_op | source)
XLA Modules:
  0.0 38.7 jit_solution(12302370364115628514)
XLA Ops:
  0.0 1.0 %constant_dynamic-slice_fusion = (bf16[1,2,32,1024]{3,2,1,0:T(8,128)(2,1)S(1)}, bf16[1,2,32,1024]{3,2,1,0:T(8,128)(2,1)S(1)}) fusion(bf16[4,2,32,1024]{3,2,1,0:T(8,128)(2,1)} %psfs_ref.1, s32[]{:T(128)S(6)} %select_n.7, s32[]{:T(128)S(6)} %select_n.6), kind=kLoop, calls=%fused_computation | loop fusion | bytes 524296 | tf_op jit(solution)/shard_map/dynamic_slice | solution.py:522
  1.0 0.3 collective-permute-start.1
  1.3 0.0 copy-start.11
  1.3 4.3 %collective-permute-start = (bf16[1,2,32,1024]{3,2,1,0:T(8,128)(2,1)S(1)}, bf16[1,2,32,1024]{3,2,1,0:T(8,128)(2,1)S(1)}, u32[]{:S(2)}, u32[]{:S(2)}) collective-permute-start(bf16[1,2,32,1024]{3,2,1,0:T(8,128)(2,1)S(1)} %get-tuple-element.36), channel_id=1, source_target_pairs={{8,16},{16,8},{9,17},{17,9},{10,18},{18,10},{11,19},{19,11},{12,20... | collective-permute-start | bytes 393224 | tf_op jit(solution)/shard_map/ppermute | solution.py:514
  5.7 3.1 %image_first.1.refs_0_ = bf16[48,192,128]{2,1,0:T(8,128)(2,1)S(1)} custom-call(f32[128,4096]{1,0:T(8,128)} %image_ref, bf16[96,64]{1,0:T(8,128)(2,1)} %constant.36.clone.refs_0_.tx_ref, bf16[256,512]{1,0:T(8,128)(2,1)} %constant.37.clone.refs_1_.tz_ref, bf16[192,128]{1,0:T(8,128)(2,1)} %constant.38.clone.refs_2_.ty_ref), custom_call_target="tpu_custom_call" | custom-call | flops 4000000000 | bytes 4000000 | tf_op jit(solution)/shard_map/image_first/pallas_call | solution.py:226
  8.8 0.0 collective-permute-done.1.even_ref
  8.8 0.5 %collective-permute-done.odd_ref = bf16[1,2,32,1024]{3,2,1,0:T(8,128)(2,1)S(1)} collective-permute-done((bf16[1,2,32,1024]{3,2,1,0:T(8,128)(2,1)S(1)}, bf16[1,2,32,1024]{3,2,1,0:T(8,128)(2,1)S(1)}, u32[]{:S(2)}, u32[]{:S(2)}) %collective-permute-start) | collective-permute-done | bytes 131104 | tf_op jit(solution)/shard_map/ppermute | solution.py:514
  9.3 0.2 blend_x.1
  9.5 0.0 copy-start.1
  9.5 0.0 copy-start.2
  9.5 0.0 copy-start.3
  9.5 0.0 copy-start.4
  9.5 0.0 copy-start.5
  9.6 0.0 copy-start.6
  9.6 1.5 %collective-permute-start.2 = (bf16[2,32,1024]{2,1,0:T(8,128)(2,1)S(1)}, bf16[2,32,1024]{2,1,0:T(8,128)(2,1)S(1)}, u32[]{:S(2)}, u32[]{:S(2)}) collective-permute-start(bf16[2,32,1024]{2,1,0:T(8,128)(2,1)S(1)} %get-tuple-element.26.refs_3_), channel_id=1, source_target_pairs={{0,1},{1,0},{2,3},{3,2},{4,5},{5,4},{6,7},{7,6},{8,9},{9,8},{10,11... | collective-permute-start | bytes 393224 | tf_op jit(solution)/shard_map/ppermute | solution.py:508
  11.1 3.2 %collective-permute-start.3 = (bf16[2,32,1024]{2,1,0:T(8,128)(2,1)S(1)}, bf16[2,32,1024]{2,1,0:T(8,128)(2,1)S(1)}, u32[]{:S(2)}, u32[]{:S(2)}) collective-permute-start(bf16[2,32,1024]{2,1,0:T(8,128)(2,1)S(1)} %get-tuple-element.27.refs_4_), channel_id=1, source_target_pairs={{1,2},{2,1},{3,4},{4,3},{5,6},{6,5},{9,10},{10,9},{11,12},{12,11},... | collective-permute-start | bytes 393224 | tf_op jit(solution)/shard_map/ppermute | solution.py:514
  14.4 1.7 %image_forward.1.refs_1_ = bf16[48,192,128]{2,1,0:T(8,128)(2,1)S(1)} custom-call(f32[128,4096]{1,0:T(8,128)S(1)} %copy-done.7, bf16[96,64]{1,0:T(8,128)(2,1)S(1)} %copy-done.11, bf16[256,512]{1,0:T(8,128)(2,1)S(1)} %copy-done.8, bf16[192,128]{1,0:T(8,128)(2,1)S(1)} %copy-done.10), custom_call_target="tpu_custom_call" | custom-call | flops 4000000000 | bytes 4000000 | tf_op jit(solution)/shard_map/image_forward/pallas_call | solution.py:220
  16.0 0.0 copy-start.9
  16.0 0.0 collective-permute-done.2.refs_2_
  16.1 1.3 %collective-permute-done.3.refs_5_ = bf16[2,32,1024]{2,1,0:T(8,128)(2,1)S(1)} collective-permute-done((bf16[2,32,1024]{2,1,0:T(8,128)(2,1)S(1)}, bf16[2,32,1024]{2,1,0:T(8,128)(2,1)S(1)}, u32[]{:S(2)}, u32[]{:S(2)}) %collective-permute-start.3) | collective-permute-done | bytes 131104 | tf_op jit(solution)/shard_map/ppermute | solution.py:514
  17.4 3.7 %respond.1 = (bf16[2,24,192,256]{3,2,1,0:T(8,128)(2,1)S(1)}, bf16[160,1024]{1,0:T(8,128)(2,1)S(1)}, bf16[160,1024]{1,0:T(8,128)(2,1)S(1)}) custom-call(bf16[48,192,128]{2,1,0:T(8,128)(2,1)S(1)} %image_first.1.refs_0_, bf16[48,192,128]{2,1,0:T(8,128)(2,1)S(1)} %image_forward.1.refs_1_, bf16[2,32,1024]{2,1,0:T(8,128)(2,1)S(1)} %collective-permute-done.2.refs_2_, ...), custom_call_target="tpu_custom_call" | custom-call | tf_op jit(solution)/shard_map/respond/pallas_call | solution.py:370
  21.1 0.2 collective-permute-start.4
  21.3 3.1 %collective-permute-start.5 = (bf16[160,1024]{1,0:T(8,128)(2,1)S(1)}, bf16[160,1024]{1,0:T(8,128)(2,1)S(1)}, u32[]{:S(2)}, u32[]{:S(2)}) collective-permute-start(bf16[160,1024]{1,0:T(8,128)(2,1)S(1)} %get-tuple-element.30), channel_id=1, source_target_pairs={{1,2},{2,1},{3,4},{4,3},{5,6},{6,5},{9,10},{10,9},{11,12},{12,11},... | collective-permute-start | bytes 983048 | tf_op jit(solution)/shard_map/ppermute | solution.py:514
  24.4 2.3 %middle.1.mid_ref = f32[160,4096]{1,0:T(8,128)S(1)} custom-call(bf16[2,24,192,256]{3,2,1,0:T(8,128)(2,1)S(1)} %get-tuple-element.28.product_ref, bf16[128,192]{1,0:T(8,128)(2,1)S(1)} %copy-done.9, bf16[512,256]{1,0:T(8,128)(2,1)S(1)} %copy-done.2, bf16[160,192]{1,0:T(8,128)(2,1)S(1)} %copy-done.3), custom_call_target="tpu_custom_call" | custom-call | flops 3000000000 | bytes 6000000 | tf_op jit(solution)/shard_map/middle/pallas_call | solution.py:388
  26.7 0.0 collective-permute-done.4.even_ref
  26.7 3.0 %collective-permute-done.5.odd_ref = bf16[160,1024]{1,0:T(8,128)(2,1)S(1)} collective-permute-done((bf16[160,1024]{1,0:T(8,128)(2,1)S(1)}, bf16[160,1024]{1,0:T(8,128)(2,1)S(1)}, u32[]{:S(2)}, u32[]{:S(2)}) %collective-permute-start.5) | collective-permute-done | bytes 327712 | tf_op jit(solution)/shard_map/ppermute | solution.py:514
  29.7 0.1 collective-permute-start.6
  29.8 3.7 %collective-permute-start.7 = (bf16[16,4096]{1,0:T(8,128)(2,1)S(1)}, bf16[16,4096]{1,0:T(8,128)(2,1)S(1)}, u32[]{:S(2)}, u32[]{:S(2)}) collective-permute-start(bf16[16,4096]{1,0:T(8,128)(2,1)S(1)} %get-tuple-element.34), channel_id=1, source_target_pairs={{8,16},{16,8},{9,17},{17,9},{10,18},{18,10},{11,19},{19,11},{12,20... | collective-permute-start | bytes 393224 | tf_op jit(solution)/shard_map/ppermute | solution.py:514
  33.5 1.6 %fold.1 = (f32[128,4096]{1,0:T(8,128)}, f32[32,4096]{1,0:T(8,128)S(1)}) custom-call(f32[160,4096]{1,0:T(8,128)S(1)} %middle.1.mid_ref, bf16[160,1024]{1,0:T(8,128)(2,1)S(1)} %collective-permute-done.4.even_ref, bf16[160,1024]{1,0:T(8,128)(2,1)S(1)} %collective-permute-done.5.odd_ref), custom_call_target="tpu_custom_call" | custom-call | flops 10000000 | bytes 8000000 | tf_op jit(solution)/shard_map/fold/pallas_call | solution.py:459
  35.1 0.0 collective-permute-done.6.even_ref
  35.1 2.8 %collective-permute-done.7.odd_ref = bf16[16,4096]{1,0:T(8,128)(2,1)S(1)} collective-permute-done((bf16[16,4096]{1,0:T(8,128)(2,1)S(1)}, bf16[16,4096]{1,0:T(8,128)(2,1)S(1)}, u32[]{:S(2)}, u32[]{:S(2)}) %collective-permute-start.7) | collective-permute-done | bytes 131104 | tf_op jit(solution)/shard_map/ppermute | solution.py:514
  37.9 0.8 %close.1 = f32[128,4096]{1,0:T(8,128)} custom-call(f32[128,4096]{1,0:T(8,128)} %get-tuple-element.31.out_in, f32[32,4096]{1,0:T(8,128)S(1)} %get-tuple-element.32.rims_ref, bf16[16,4096]{1,0:T(8,128)(2,1)S(1)} %collective-permute-done.6.even_ref, bf16[16,4096]{1,0:T(8,128)(2,1)S(1)} %collective-permute-done.7.odd_ref), custom_call_target="tpu_custom_call", output_to_operand_aliasing={{}: (0, {})} | custom-call | tf_op jit(solution)/shard_map/close/pallas_call | solution.py:491
  (17 shorter events, 0.1 us)
Async XLA Ops:
  1.0 7.8 %collective-permute-start.1 = (bf16[1,2,32,1024]{3,2,1,0:T(8,128)(2,1)S(1)}, bf16[1,2,32,1024]{3,2,1,0:T(8,128)(2,1)S(1)}, u32[]{:S(2)}, u32[]{:S(2)}) collective-permute-start(bf16[1,2,32,1024]{3,2,1,0:T(8,128)(2,1)S(1)} %get-tuple-element.35), channel_id=1, source_target_pairs={{0,8},{8,0},{16,24},{24,16},{1,9},{9,1},{17,25},{25,17},{2,10},{10... | collective-permute-start | bytes 393224 | tf_op jit(solution)/shard_map/ppermute | solution.py:508
  1.3 8.0 %copy-start = (bf16[4,2,32,1024]{3,2,1,0:T(8,128)(2,1)S(1)}, bf16[4,2,32,1024]{3,2,1,0:T(8,128)(2,1)}, u32[]{:S(2)}) copy-start(bf16[4,2,32,1024]{3,2,1,0:T(8,128)(2,1)} %psfs_ref.1) | copy-start | bytes 1572868
  1.3 13.0 %copy-start.7 = (f32[128,4096]{1,0:T(8,128)S(1)}, f32[128,4096]{1,0:T(8,128)}, u32[]{:S(2)}) copy-start(f32[128,4096]{1,0:T(8,128)} %image_ref) | copy-start | bytes 6291460
  1.3 13.0 %copy-start.8 = (bf16[256,512]{1,0:T(8,128)(2,1)S(1)}, bf16[256,512]{1,0:T(8,128)(2,1)}, u32[]{:S(2)}) copy-start(bf16[256,512]{1,0:T(8,128)(2,1)} %constant.37.clone.refs_1_.tz_ref) | copy-start | bytes 786436
  1.3 13.0 %copy-start.10 = (bf16[192,128]{1,0:T(8,128)(2,1)S(1)}, bf16[192,128]{1,0:T(8,128)(2,1)}, u32[]{:S(2)}) copy-start(bf16[192,128]{1,0:T(8,128)(2,1)} %constant.38.clone.refs_2_.ty_ref) | copy-start | bytes 147460
  1.3 13.0 %copy-start.11 = (bf16[96,64]{1,0:T(8,128)(2,1)S(1)}, bf16[96,64]{1,0:T(8,128)(2,1)}, u32[]{:S(2)}) copy-start(bf16[96,64]{1,0:T(8,128)(2,1)} %constant.36.clone.refs_0_.tx_ref) | copy-start | bytes 36868
  1.3 8.0 %collective-permute-start = (bf16[1,2,32,1024]{3,2,1,0:T(8,128)(2,1)S(1)}, bf16[1,2,32,1024]{3,2,1,0:T(8,128)(2,1)S(1)}, u32[]{:S(2)}, u32[]{:S(2)}) collective-permute-start(bf16[1,2,32,1024]{3,2,1,0:T(8,128)(2,1)S(1)} %get-tuple-element.36), channel_id=1, source_target_pairs={{8,16},{16,8},{9,17},{17,9},{10,18},{18,10},{11,19},{19,11},{12,20... | collective-permute-start | bytes 393224 | tf_op jit(solution)/shard_map/ppermute | solution.py:514
  9.5 7.9 %copy-start.1 = (bf16[256,1024]{1,0:T(8,128)(2,1)S(1)}, bf16[256,1024]{1,0:T(8,128)(2,1)}, u32[]{:S(2)}) copy-start(bf16[256,1024]{1,0:T(8,128)(2,1)} %constant.44.clone.refs_7_) | copy-start | bytes 1572868
  9.5 7.8 %copy-start.2 = (bf16[512,256]{1,0:T(8,128)(2,1)S(1)}, bf16[512,256]{1,0:T(8,128)(2,1)}, u32[]{:S(2)}) copy-start(bf16[512,256]{1,0:T(8,128)(2,1)} %constant.41.clone.refs_10_.tiz) | copy-start | bytes 786436
  9.5 7.8 %copy-start.3 = (bf16[160,192]{1,0:T(8,128)(2,1)S(1)}, bf16[160,192]{1,0:T(8,128)(2,1)}, u32[]{:S(2)}) copy-start(bf16[160,192]{1,0:T(8,128)(2,1)} %constant.42.clone.refs_11_.tix) | copy-start | bytes 184324
  9.5 7.8 %copy-start.4 = (bf16[192,64]{1,0:T(8,128)(2,1)S(1)}, bf16[192,64]{1,0:T(8,128)(2,1)}, u32[]{:S(2)}) copy-start(bf16[192,64]{1,0:T(8,128)(2,1)} %constant.45.clone.refs_8_) | copy-start | bytes 73732
  9.5 7.8 %copy-start.5 = (bf16[64,192]{1,0:T(8,128)(2,1)S(1)}, bf16[64,192]{1,0:T(8,128)(2,1)}, u32[]{:S(2)}) copy-start(bf16[64,192]{1,0:T(8,128)(2,1)} %constant.39.clone.refs_9_) | copy-start | bytes 73732
  9.6 7.8 %copy-start.6 = (bf16[96,128]{1,0:T(8,128)(2,1)S(1)}, bf16[96,128]{1,0:T(8,128)(2,1)}, u32[]{:S(2)}) copy-start(bf16[96,128]{1,0:T(8,128)(2,1)} %constant.43.clone.refs_6_) | copy-start | bytes 73732
  9.6 6.5 %collective-permute-start.2 = (bf16[2,32,1024]{2,1,0:T(8,128)(2,1)S(1)}, bf16[2,32,1024]{2,1,0:T(8,128)(2,1)S(1)}, u32[]{:S(2)}, u32[]{:S(2)}) collective-permute-start(bf16[2,32,1024]{2,1,0:T(8,128)(2,1)S(1)} %get-tuple-element.26.refs_3_), channel_id=1, source_target_pairs={{0,1},{1,0},{2,3},{3,2},{4,5},{5,4},{6,7},{7,6},{8,9},{9,8},{10,11... | collective-permute-start | bytes 393224 | tf_op jit(solution)/shard_map/ppermute | solution.py:508
  11.1 6.3 %collective-permute-start.3 = (bf16[2,32,1024]{2,1,0:T(8,128)(2,1)S(1)}, bf16[2,32,1024]{2,1,0:T(8,128)(2,1)S(1)}, u32[]{:S(2)}, u32[]{:S(2)}) collective-permute-start(bf16[2,32,1024]{2,1,0:T(8,128)(2,1)S(1)} %get-tuple-element.27.refs_4_), channel_id=1, source_target_pairs={{1,2},{2,1},{3,4},{4,3},{5,6},{6,5},{9,10},{10,9},{11,12},{12,11},... | collective-permute-start | bytes 393224 | tf_op jit(solution)/shard_map/ppermute | solution.py:514
  16.0 8.4 %copy-start.9 = (bf16[128,192]{1,0:T(8,128)(2,1)S(1)}, bf16[128,192]{1,0:T(8,128)(2,1)}, u32[]{:S(2)}) copy-start(bf16[128,192]{1,0:T(8,128)(2,1)} %constant.40.clone.tiy) | copy-start | bytes 147460
  21.1 5.6 %collective-permute-start.4 = (bf16[160,1024]{1,0:T(8,128)(2,1)S(1)}, bf16[160,1024]{1,0:T(8,128)(2,1)S(1)}, u32[]{:S(2)}, u32[]{:S(2)}) collective-permute-start(bf16[160,1024]{1,0:T(8,128)(2,1)S(1)} %get-tuple-element.29), channel_id=1, source_target_pairs={{0,1},{1,0},{2,3},{3,2},{4,5},{5,4},{6,7},{7,6},{8,9},{9,8},{10,11... | collective-permute-start | bytes 983048 | tf_op jit(solution)/shard_map/ppermute | solution.py:508
  21.3 8.4 %collective-permute-start.5 = (bf16[160,1024]{1,0:T(8,128)(2,1)S(1)}, bf16[160,1024]{1,0:T(8,128)(2,1)S(1)}, u32[]{:S(2)}, u32[]{:S(2)}) collective-permute-start(bf16[160,1024]{1,0:T(8,128)(2,1)S(1)} %get-tuple-element.30), channel_id=1, source_target_pairs={{1,2},{2,1},{3,4},{4,3},{5,6},{6,5},{9,10},{10,9},{11,12},{12,11},... | collective-permute-start | bytes 983048 | tf_op jit(solution)/shard_map/ppermute | solution.py:514
  29.7 5.4 %collective-permute-start.6 = (bf16[16,4096]{1,0:T(8,128)(2,1)S(1)}, bf16[16,4096]{1,0:T(8,128)(2,1)S(1)}, u32[]{:S(2)}, u32[]{:S(2)}) collective-permute-start(bf16[16,4096]{1,0:T(8,128)(2,1)S(1)} %get-tuple-element.33), channel_id=1, source_target_pairs={{0,8},{8,0},{16,24},{24,16},{1,9},{9,1},{17,25},{25,17},{2,10},{10... | collective-permute-start | bytes 393224 | tf_op jit(solution)/shard_map/ppermute | solution.py:508
  29.8 8.1 %collective-permute-start.7 = (bf16[16,4096]{1,0:T(8,128)(2,1)S(1)}, bf16[16,4096]{1,0:T(8,128)(2,1)S(1)}, u32[]{:S(2)}, u32[]{:S(2)}) collective-permute-start(bf16[16,4096]{1,0:T(8,128)(2,1)S(1)} %get-tuple-element.34), channel_id=1, source_target_pairs={{8,16},{16,8},{9,17},{17,9},{10,18},{18,10},{11,19},{19,11},{12,20... | collective-permute-start | bytes 393224 | tf_op jit(solution)/shard_map/ppermute | solution.py:514

commit v7 on v6

--- a/solution.py
+++ b/solution.py
@@ -419,27 +419,42 @@
         out_ref[:, t * tile : (t + 1) * tile] = x_inverted(grid_x, tix, t)
 
 
-def rim_kernel(mid_ref, even_ref, odd_ref, to_even_ref, to_odd_ref):
+def rim_kernel(mid_ref, even_ref, to_odd_ref, to_even_ref):
     band = even_ref.shape[1]
-    rows = mid_ref.shape[0] - PSFW
+    rows, columns = mid_ref.shape[0] - PSFW, mid_ref.shape[1]
     gx, gy = parity("gx"), parity("gy")
-    for out, side in ((to_even_ref, 1 - gx), (to_odd_ref, gx)):
+    corner = pl.ds(pl.multiple_of((1 - gy) * (columns - band), band), band)
+    for out, side in ((to_odd_ref, gx), (to_even_ref, 1 - gx)):
         at = pl.ds(pl.multiple_of(rows + side * HALF, HALF), HALF)
-        low = pick(gy, odd_ref[at, :], even_ref[at, :]).astype(F32)
-        high = pick(gy, even_ref[at, :], odd_ref[at, :]).astype(F32)
-        out[:, band:-band] = mid_ref[at, band:-band].astype(BF16)
-        out[:, :band] = (mid_ref[at, :band] + low).astype(BF16)
-        out[:, -band:] = (mid_ref[at, -band:] + high).astype(BF16)
-
-
-def x_rims(mid, even, odd):
+        out[...] = mid_ref[at, :].astype(BF16)
+        out[:, corner] = (mid_ref[at, corner] + even_ref[at, :].astype(F32)).astype(BF16)
+
+
+def x_rims(mid, even):
     shape = jax.ShapeDtypeStruct((HALF, mid.shape[1]), BF16)
     return pl.pallas_call(
         rim_kernel,
         out_shape=(shape,) * 2,
         compiler_params=pltpu.CompilerParams(vmem_limit_bytes=16 << 20),
         name="x_rims",
-    )(mid, even, odd)
+    )(mid, even)
+
+
+def corner_kernel(odd_ref, to_odd_ref, to_even_ref):
+    rows = odd_ref.shape[0] - PSFW
+    gx = parity("gx")
+    for out, side in ((to_odd_ref, gx), (to_even_ref, 1 - gx)):
+        out[...] = odd_ref[pl.ds(pl.multiple_of(rows + side * HALF, HALF), HALF), :]
+
+
+def x_corners(odd):
+    shape = jax.ShapeDtypeStruct((HALF, odd.shape[1]), BF16)
+    return pl.pallas_call(
+        corner_kernel,
+        out_shape=(shape,) * 2,
+        compiler_params=pltpu.CompilerParams(vmem_limit_bytes=16 << 20),
+        name="x_corners",
+    )(odd)
 
 
 def fold_kernel(mid_ref, even_ref, odd_ref, out_ref, rims_ref):
@@ -470,13 +485,19 @@
     )(mid, even, odd)
 
 
-def close_kernel(out_in, rims_ref, even_ref, odd_ref, out_ref, total, sems):
+def close_kernel(
+    out_in, rims_ref, even_ref, odd_ref, even_corner, odd_corner, out_ref, total, sems
+):
     del out_in
-    gx = parity("gx")
+    gx, gy = parity("gx"), parity("gy")
+    band = even_corner.shape[1]
+    far = pl.ds(pl.multiple_of(gy * (out_ref.shape[1] - band), band), band)
     copies = []
-    for k, (ref, side) in enumerate(((even_ref, 1 - gx), (odd_ref, gx))):
+    sides = ((even_ref, even_corner, 1 - gx), (odd_ref, odd_corner, gx))
+    for k, (ref, corner, side) in enumerate(sides):
         at = pl.ds(pl.multiple_of(side * HALF, HALF), HALF)
         total[k] = rims_ref[at, :] + ref[...].astype(F32)
+        total[k, :, far] += corner[...].astype(F32)
         first = pl.multiple_of(side * (out_ref.shape[0] - HALF), HALF)
         copies.append(
             pltpu.make_async_copy(total.at[k], out_ref.at[pl.ds(first, HALF), :], sems.at[k])
@@ -486,11 +507,11 @@
         copy.wait()
 
 
-def close(out, rims, even, odd):
+def close(out, rims, *received):
     vmem = pl.BlockSpec(memory_space=pltpu.VMEM)
     return pl.pallas_call(
         close_kernel,
-        in_specs=[pl.BlockSpec(memory_space=pl.ANY), vmem, vmem, vmem],
+        in_specs=[pl.BlockSpec(memory_space=pl.ANY)] + [vmem] * 5,
         out_specs=pl.BlockSpec(memory_space=pl.ANY),
         out_shape=jax.ShapeDtypeStruct(out.shape, F32),
         scratch_shapes=[
@@ -500,7 +521,7 @@
         input_output_aliases={0: 0},
         compiler_params=pltpu.CompilerParams(vmem_limit_bytes=16 << 20),
         name="close",
-    )(out, rims, even, odd)
+    )(out, rims, *received)
 
 
 def swap_even(value, axis):
@@ -533,11 +554,14 @@
     odd_y = swap_odd(out_odd, "gy")
     even_y = swap_even(out_even, "gy")
     mid = middle()
-    out_even, out_odd = x_rims(mid, even_y, odd_y)
+    out_odd, out_even = x_rims(mid, even_y)
     even_x = swap_even(out_even, "gx")
     odd_x = swap_odd(out_odd, "gx")
+    out_odd, out_even = x_corners(odd_y)
+    even_corner = swap_even(out_even, "gx")
+    odd_corner = swap_odd(out_odd, "gx")
     out, rims = fold(mid, even_y, odd_y)
-    return close(out, rims, even_x, odd_x)
+    return close(out, rims, even_x, odd_x, even_corner, odd_corner)
 
 
 def solution(mesh):

time: 39.4 us -> 37.9 us (0.962)
  waiting for transfers between devices: 7.61 us -> 3.33 us
  starting transfers between devices: 16.4 us -> 19.5 us
    ppermute x4 -> x5, waiting for transfers between devices: 7.6 us -> 3.32 us  [swap_odd(): return lax.ppermute(value, axis, pairs)]
    ppermute x4 -> x5, starting transfers between devices: 14.3 us -> 17.3 us  [swap_odd(): return lax.ppermute(value, axis, pairs)]
    ppermute x4 -> x5, starting transfers between devices: 2.12 us -> 2.19 us  [swap_even(): lax.ppermute(value, axis, [(i, i ^ 1) for i in range(count) if i ^ 1 < co...]
    pallas_call x1 -> x2, Pallas kernels: 0.84 us -> 0.87 us  [the longest x1 0.85 us: close(): pl.pallas_call(close_kernel, in_specs=[pl.BlockSpec(memory_space=pl.ANY)]...]
  transfers between devices with their start and end apart: 8 -> 10, of which waited for: 4 -> 3; matrix products, arithmetic and copies ran while one was open for 0% -> 0% of each run, Pallas kernels for 22% -> 23%
where the time goes in v7:
time: 37.9 us; the launch traced here: 37.6 us
  starting transfers between devices  19.5 us (51%)
  Pallas kernels  13.4 us (35%)
  waiting for transfers between devices  3.33 us (9%)
  local copies, waits for them, and re-layouts  1.05 us (3%)
    ppermute x5, starting transfers between devices, swap_odd(): return lax.ppermute(value, axis, pairs)  17.3 us
    pallas_call x1, Pallas kernels, respond(): pl.pallas_call(functools.partial(respond_kernel, patches), out_shape=(jax...  3.66 us
    ppermute x5, waiting for transfers between devices, swap_odd(): return lax.ppermute(value, axis, pairs)  3.32 us
    pallas_call x1, Pallas kernels, image_forward(): pl.pallas_call(functools.partial(fetching_kernel, patch), in_specs=[pl.Bl...  3.06 us
    pallas_call x1, Pallas kernels, middle(): pl.pallas_call(middle_kernel, out_shape=jax.ShapeDtypeStruct((rows, PATCH...  2.3 us
    ppermute x5, starting transfers between devices, swap_even(): lax.ppermute(value, axis, [(i, i ^ 1) for i in range(count) if i ^ 1 < co...  2.19 us
    pallas_call x1, Pallas kernels, image_forward(): pl.pallas_call(functools.partial(image_kernel, patch), scratch_shapes=scr...  1.66 us
    pallas_call x1, Pallas kernels, fold(): pl.pallas_call(fold_kernel, out_shape=(jax.ShapeDtypeStruct((rows, mid.sh...  1.62 us
  transfers between devices with their start and end apart: 10, of which 3 were waited for; matrix products, arithmetic and copies ran while one was open for 0% of the time, Pallas kernels for 23%

profile of v7, /device:TPU:19, one launch (start us, length us, event | category | flops | bytes accessed | tf_op | source)
XLA Modules:
  0.0 37.6 jit_solution(6928995996738744493)
XLA Ops:
  0.0 1.0 %constant_dynamic-slice_fusion = (bf16[1,2,32,1024]{3,2,1,0:T(8,128)(2,1)S(1)}, bf16[1,2,32,1024]{3,2,1,0:T(8,128)(2,1)S(1)}) fusion(bf16[4,2,32,1024]{3,2,1,0:T(8,128)(2,1)} %psfs_ref.1, s32[]{:T(128)S(6)} %select_n.7, s32[]{:T(128)S(6)} %select_n.6), kind=kLoop, calls=%fused_computation | loop fusion | bytes 524296 | tf_op jit(solution)/shard_map/dynamic_slice | solution.py:543
  1.0 0.3 collective-permute-start.1
  1.3 0.0 copy-start.11
  1.3 4.3 %collective-permute-start = (bf16[1,2,32,1024]{3,2,1,0:T(8,128)(2,1)S(1)}, bf16[1,2,32,1024]{3,2,1,0:T(8,128)(2,1)S(1)}, u32[]{:S(2)}, u32[]{:S(2)}) collective-permute-start(bf16[1,2,32,1024]{3,2,1,0:T(8,128)(2,1)S(1)} %get-tuple-element.40), channel_id=1, source_target_pairs={{8,16},{16,8},{9,17},{17,9},{10,18},{18,10},{11,19},{19,11},{12,20... | collective-permute-start | bytes 393224 | tf_op jit(solution)/shard_map/ppermute | solution.py:535
  5.7 3.1 %image_first.1.refs_0_ = bf16[48,192,128]{2,1,0:T(8,128)(2,1)S(1)} custom-call(f32[128,4096]{1,0:T(8,128)} %image_ref, bf16[96,64]{1,0:T(8,128)(2,1)} %constant.36.clone.refs_0_.tx_ref, bf16[256,512]{1,0:T(8,128)(2,1)} %constant.37.clone.refs_1_.tz_ref, bf16[192,128]{1,0:T(8,128)(2,1)} %constant.38.clone.refs_2_.ty_ref), custom_call_target="tpu_custom_call" | custom-call | flops 4000000000 | bytes 4000000 | tf_op jit(solution)/shard_map/image_first/pallas_call | solution.py:226
  8.8 0.5 %collective-permute-done.odd_ref = bf16[1,2,32,1024]{3,2,1,0:T(8,128)(2,1)S(1)} collective-permute-done((bf16[1,2,32,1024]{3,2,1,0:T(8,128)(2,1)S(1)}, bf16[1,2,32,1024]{3,2,1,0:T(8,128)(2,1)S(1)}, u32[]{:S(2)}, u32[]{:S(2)}) %collective-permute-start) | collective-permute-done | bytes 131104 | tf_op jit(solution)/shard_map/ppermute | solution.py:535
  9.3 0.2 blend_x.1
  9.5 0.0 copy-start.1
  9.5 0.0 copy-start.2
  9.5 0.0 copy-start.3
  9.5 0.0 copy-start.4
  9.5 0.0 copy-start.5
  9.6 0.0 copy-start.6
  9.6 1.5 %collective-permute-start.2 = (bf16[2,32,1024]{2,1,0:T(8,128)(2,1)S(1)}, bf16[2,32,1024]{2,1,0:T(8,128)(2,1)S(1)}, u32[]{:S(2)}, u32[]{:S(2)}) collective-permute-start(bf16[2,32,1024]{2,1,0:T(8,128)(2,1)S(1)} %get-tuple-element.28.refs_3_), channel_id=1, source_target_pairs={{0,1},{1,0},{2,3},{3,2},{4,5},{5,4},{6,7},{7,6},{8,9},{9,8},{10,11... | collective-permute-start | bytes 393224 | tf_op jit(solution)/shard_map/ppermute | solution.py:529
  11.1 3.2 %collective-permute-start.3 = (bf16[2,32,1024]{2,1,0:T(8,128)(2,1)S(1)}, bf16[2,32,1024]{2,1,0:T(8,128)(2,1)S(1)}, u32[]{:S(2)}, u32[]{:S(2)}) collective-permute-start(bf16[2,32,1024]{2,1,0:T(8,128)(2,1)S(1)} %get-tuple-element.29.refs_4_), channel_id=1, source_target_pairs={{1,2},{2,1},{3,4},{4,3},{5,6},{6,5},{9,10},{10,9},{11,12},{12,11},... | collective-permute-start | bytes 393224 | tf_op jit(solution)/shard_map/ppermute | solution.py:535
  14.4 1.7 %image_forward.1.refs_1_ = bf16[48,192,128]{2,1,0:T(8,128)(2,1)S(1)} custom-call(f32[128,4096]{1,0:T(8,128)S(1)} %copy-done.7, bf16[96,64]{1,0:T(8,128)(2,1)S(1)} %copy-done.11, bf16[256,512]{1,0:T(8,128)(2,1)S(1)} %copy-done.8, bf16[192,128]{1,0:T(8,128)(2,1)S(1)} %copy-done.10), custom_call_target="tpu_custom_call" | custom-call | flops 4000000000 | bytes 4000000 | tf_op jit(solution)/shard_map/image_forward/pallas_call | solution.py:220
  16.0 0.0 copy-start.9
  16.1 1.3 %collective-permute-done.3.refs_5_ = bf16[2,32,1024]{2,1,0:T(8,128)(2,1)S(1)} collective-permute-done((bf16[2,32,1024]{2,1,0:T(8,128)(2,1)S(1)}, bf16[2,32,1024]{2,1,0:T(8,128)(2,1)S(1)}, u32[]{:S(2)}, u32[]{:S(2)}) %collective-permute-start.3) | collective-permute-done | bytes 131104 | tf_op jit(solution)/shard_map/ppermute | solution.py:535
  17.4 3.7 %respond.1 = (bf16[2,24,192,256]{3,2,1,0:T(8,128)(2,1)S(1)}, bf16[160,1024]{1,0:T(8,128)(2,1)S(1)}, bf16[160,1024]{1,0:T(8,128)(2,1)S(1)}) custom-call(bf16[48,192,128]{2,1,0:T(8,128)(2,1)S(1)} %image_first.1.refs_0_, bf16[48,192,128]{2,1,0:T(8,128)(2,1)S(1)} %image_forward.1.refs_1_, bf16[2,32,1024]{2,1,0:T(8,128)(2,1)S(1)} %collective-permute-done.2.refs_2_, ...), custom_call_target="tpu_custom_call" | custom-call | tf_op jit(solution)/shard_map/respond/pallas_call | solution.py:370
  21.1 0.2 collective-permute-start.4
  21.3 3.1 %collective-permute-start.5 = (bf16[160,1024]{1,0:T(8,128)(2,1)S(1)}, bf16[160,1024]{1,0:T(8,128)(2,1)S(1)}, u32[]{:S(2)}, u32[]{:S(2)}) collective-permute-start(bf16[160,1024]{1,0:T(8,128)(2,1)S(1)} %get-tuple-element.32), channel_id=1, source_target_pairs={{1,2},{2,1},{3,4},{4,3},{5,6},{6,5},{9,10},{10,9},{11,12},{12,11},... | collective-permute-start | bytes 983048 | tf_op jit(solution)/shard_map/ppermute | solution.py:535
  24.4 2.3 %middle.1.mid_ref = f32[160,4096]{1,0:T(8,128)S(1)} custom-call(bf16[2,24,192,256]{3,2,1,0:T(8,128)(2,1)S(1)} %get-tuple-element.30.product_ref, bf16[128,192]{1,0:T(8,128)(2,1)S(1)} %copy-done.9, bf16[512,256]{1,0:T(8,128)(2,1)S(1)} %copy-done.2, bf16[160,192]{1,0:T(8,128)(2,1)S(1)} %copy-done.3), custom_call_target="tpu_custom_call" | custom-call | flops 3000000000 | bytes 6000000 | tf_op jit(solution)/shard_map/middle/pallas_call | solution.py:388
  26.7 0.0 collective-permute-done.4.even_ref
  26.7 0.1 x_rims.1
  26.8 0.1 collective-permute-start.6
  26.9 3.7 %collective-permute-start.7 = (bf16[16,4096]{1,0:T(8,128)(2,1)S(1)}, bf16[16,4096]{1,0:T(8,128)(2,1)S(1)}, u32[]{:S(2)}, u32[]{:S(2)}) collective-permute-start(bf16[16,4096]{1,0:T(8,128)(2,1)S(1)} %get-tuple-element.36), channel_id=1, source_target_pairs={{8,16},{16,8},{9,17},{17,9},{10,18},{18,10},{11,19},{19,11},{12,20... | collective-permute-start | bytes 393224 | tf_op jit(solution)/shard_map/ppermute | solution.py:535
  30.5 0.0 collective-permute-done.5.odd_ref
  30.6 0.1 collective-permute-start.8
  30.6 3.0 %collective-permute-start.9 = (bf16[16,1024]{1,0:T(8,128)(2,1)S(1)}, bf16[16,1024]{1,0:T(8,128)(2,1)S(1)}, u32[]{:S(2)}, u32[]{:S(2)}) collective-permute-start(bf16[16,1024]{1,0:T(8,128)(2,1)S(1)} %get-tuple-element.38), channel_id=1, source_target_pairs={{8,16},{16,8},{9,17},{17,9},{10,18},{18,10},{11,19},{19,11},{12,20... | collective-permute-start | bytes 98312 | tf_op jit(solution)/shard_map/ppermute | solution.py:535
  33.6 1.6 %fold.1 = (f32[128,4096]{1,0:T(8,128)}, f32[32,4096]{1,0:T(8,128)S(1)}) custom-call(f32[160,4096]{1,0:T(8,128)S(1)} %middle.1.mid_ref, bf16[160,1024]{1,0:T(8,128)(2,1)S(1)} %collective-permute-done.4.even_ref, bf16[160,1024]{1,0:T(8,128)(2,1)S(1)} %collective-permute-done.5.odd_ref), custom_call_target="tpu_custom_call" | custom-call | flops 10000000 | bytes 8000000 | tf_op jit(solution)/shard_map/fold/pallas_call | solution.py:474
  35.3 1.5 %collective-permute-done.9.odd_corner = bf16[16,1024]{1,0:T(8,128)(2,1)S(1)} collective-permute-done((bf16[16,1024]{1,0:T(8,128)(2,1)S(1)}, bf16[16,1024]{1,0:T(8,128)(2,1)S(1)}, u32[]{:S(2)}, u32[]{:S(2)}) %collective-permute-start.9) | collective-permute-done | bytes 32800 | tf_op jit(solution)/shard_map/ppermute | solution.py:535
  36.8 0.9 %close.1 = f32[128,4096]{1,0:T(8,128)} custom-call(f32[128,4096]{1,0:T(8,128)} %get-tuple-element.33.out_in, f32[32,4096]{1,0:T(8,128)S(1)} %get-tuple-element.34.rims_ref, bf16[16,4096]{1,0:T(8,128)(2,1)S(1)} %collective-permute-done.6.even_ref, bf16[16,4096]{1,0:T(8,128)(2,1)S(1)} %collective-permute-done.7.odd_ref, ...), custom_call_target="tpu_custom_call", output_to_operand_aliasing={{}: (0, {})} | custom-call | tf_op jit(solution)/shard_map/close/pallas_call | solution.py:512
  (22 shorter events, 0.1 us)
Async XLA Ops:
  1.0 7.8 %collective-permute-start.1 = (bf16[1,2,32,1024]{3,2,1,0:T(8,128)(2,1)S(1)}, bf16[1,2,32,1024]{3,2,1,0:T(8,128)(2,1)S(1)}, u32[]{:S(2)}, u32[]{:S(2)}) collective-permute-start(bf16[1,2,32,1024]{3,2,1,0:T(8,128)(2,1)S(1)} %get-tuple-element.39), channel_id=1, source_target_pairs={{0,8},{8,0},{16,24},{24,16},{1,9},{9,1},{17,25},{25,17},{2,10},{10... | collective-permute-start | bytes 393224 | tf_op jit(solution)/shard_map/ppermute | solution.py:529
  1.3 8.0 %copy-start = (bf16[4,2,32,1024]{3,2,1,0:T(8,128)(2,1)S(1)}, bf16[4,2,32,1024]{3,2,1,0:T(8,128)(2,1)}, u32[]{:S(2)}) copy-start(bf16[4,2,32,1024]{3,2,1,0:T(8,128)(2,1)} %psfs_ref.1) | copy-start | bytes 1572868
  1.3 13.0 %copy-start.7 = (f32[128,4096]{1,0:T(8,128)S(1)}, f32[128,4096]{1,0:T(8,128)}, u32[]{:S(2)}) copy-start(f32[128,4096]{1,0:T(8,128)} %image_ref) | copy-start | bytes 6291460
  1.3 13.0 %copy-start.8 = (bf16[256,512]{1,0:T(8,128)(2,1)S(1)}, bf16[256,512]{1,0:T(8,128)(2,1)}, u32[]{:S(2)}) copy-start(bf16[256,512]{1,0:T(8,128)(2,1)} %constant.37.clone.refs_1_.tz_ref) | copy-start | bytes 786436
  1.3 13.0 %copy-start.10 = (bf16[192,128]{1,0:T(8,128)(2,1)S(1)}, bf16[192,128]{1,0:T(8,128)(2,1)}, u32[]{:S(2)}) copy-start(bf16[192,128]{1,0:T(8,128)(2,1)} %constant.38.clone.refs_2_.ty_ref) | copy-start | bytes 147460
  1.3 13.0 %copy-start.11 = (bf16[96,64]{1,0:T(8,128)(2,1)S(1)}, bf16[96,64]{1,0:T(8,128)(2,1)}, u32[]{:S(2)}) copy-start(bf16[96,64]{1,0:T(8,128)(2,1)} %constant.36.clone.refs_0_.tx_ref) | copy-start | bytes 36868
  1.3 8.0 %collective-permute-start = (bf16[1,2,32,1024]{3,2,1,0:T(8,128)(2,1)S(1)}, bf16[1,2,32,1024]{3,2,1,0:T(8,128)(2,1)S(1)}, u32[]{:S(2)}, u32[]{:S(2)}) collective-permute-start(bf16[1,2,32,1024]{3,2,1,0:T(8,128)(2,1)S(1)} %get-tuple-element.40), channel_id=1, source_target_pairs={{8,16},{16,8},{9,17},{17,9},{10,18},{18,10},{11,19},{19,11},{12,20... | collective-permute-start | bytes 393224 | tf_op jit(solution)/shard_map/ppermute | solution.py:535
  9.5 7.9 %copy-start.1 = (bf16[256,1024]{1,0:T(8,128)(2,1)S(1)}, bf16[256,1024]{1,0:T(8,128)(2,1)}, u32[]{:S(2)}) copy-start(bf16[256,1024]{1,0:T(8,128)(2,1)} %constant.44.clone.refs_7_) | copy-start | bytes 1572868
  9.5 7.8 %copy-start.2 = (bf16[512,256]{1,0:T(8,128)(2,1)S(1)}, bf16[512,256]{1,0:T(8,128)(2,1)}, u32[]{:S(2)}) copy-start(bf16[512,256]{1,0:T(8,128)(2,1)} %constant.41.clone.refs_10_.tiz) | copy-start | bytes 786436
  9.5 7.8 %copy-start.3 = (bf16[160,192]{1,0:T(8,128)(2,1)S(1)}, bf16[160,192]{1,0:T(8,128)(2,1)}, u32[]{:S(2)}) copy-start(bf16[160,192]{1,0:T(8,128)(2,1)} %constant.42.clone.refs_11_.tix) | copy-start | bytes 184324
  9.5 7.8 %copy-start.4 = (bf16[192,64]{1,0:T(8,128)(2,1)S(1)}, bf16[192,64]{1,0:T(8,128)(2,1)}, u32[]{:S(2)}) copy-start(bf16[192,64]{1,0:T(8,128)(2,1)} %constant.45.clone.refs_8_) | copy-start | bytes 73732
  9.5 7.8 %copy-start.5 = (bf16[64,192]{1,0:T(8,128)(2,1)S(1)}, bf16[64,192]{1,0:T(8,128)(2,1)}, u32[]{:S(2)}) copy-start(bf16[64,192]{1,0:T(8,128)(2,1)} %constant.39.clone.refs_9_) | copy-start | bytes 73732
  9.6 7.8 %copy-start.6 = (bf16[96,128]{1,0:T(8,128)(2,1)S(1)}, bf16[96,128]{1,0:T(8,128)(2,1)}, u32[]{:S(2)}) copy-start(bf16[96,128]{1,0:T(8,128)(2,1)} %constant.43.clone.refs_6_) | copy-start | bytes 73732
  9.6 6.5 %collective-permute-start.2 = (bf16[2,32,1024]{2,1,0:T(8,128)(2,1)S(1)}, bf16[2,32,1024]{2,1,0:T(8,128)(2,1)S(1)}, u32[]{:S(2)}, u32[]{:S(2)}) collective-permute-start(bf16[2,32,1024]{2,1,0:T(8,128)(2,1)S(1)} %get-tuple-element.28.refs_3_), channel_id=1, source_target_pairs={{0,1},{1,0},{2,3},{3,2},{4,5},{5,4},{6,7},{7,6},{8,9},{9,8},{10,11... | collective-permute-start | bytes 393224 | tf_op jit(solution)/shard_map/ppermute | solution.py:529
  11.1 6.3 %collective-permute-start.3 = (bf16[2,32,1024]{2,1,0:T(8,128)(2,1)S(1)}, bf16[2,32,1024]{2,1,0:T(8,128)(2,1)S(1)}, u32[]{:S(2)}, u32[]{:S(2)}) collective-permute-start(bf16[2,32,1024]{2,1,0:T(8,128)(2,1)S(1)} %get-tuple-element.29.refs_4_), channel_id=1, source_target_pairs={{1,2},{2,1},{3,4},{4,3},{5,6},{6,5},{9,10},{10,9},{11,12},{12,11},... | collective-permute-start | bytes 393224 | tf_op jit(solution)/shard_map/ppermute | solution.py:535
  16.0 8.4 %copy-start.9 = (bf16[128,192]{1,0:T(8,128)(2,1)S(1)}, bf16[128,192]{1,0:T(8,128)(2,1)}, u32[]{:S(2)}) copy-start(bf16[128,192]{1,0:T(8,128)(2,1)} %constant.40.clone.tiy) | copy-start | bytes 147460
  21.1 5.6 %collective-permute-start.4 = (bf16[160,1024]{1,0:T(8,128)(2,1)S(1)}, bf16[160,1024]{1,0:T(8,128)(2,1)S(1)}, u32[]{:S(2)}, u32[]{:S(2)}) collective-permute-start(bf16[160,1024]{1,0:T(8,128)(2,1)S(1)} %get-tuple-element.31), channel_id=1, source_target_pairs={{0,1},{1,0},{2,3},{3,2},{4,5},{5,4},{6,7},{7,6},{8,9},{9,8},{10,11... | collective-permute-start | bytes 983048 | tf_op jit(solution)/shard_map/ppermute | solution.py:529
  21.3 9.2 %collective-permute-start.5 = (bf16[160,1024]{1,0:T(8,128)(2,1)S(1)}, bf16[160,1024]{1,0:T(8,128)(2,1)S(1)}, u32[]{:S(2)}, u32[]{:S(2)}) collective-permute-start(bf16[160,1024]{1,0:T(8,128)(2,1)S(1)} %get-tuple-element.32), channel_id=1, source_target_pairs={{1,2},{2,1},{3,4},{4,3},{5,6},{6,5},{9,10},{10,9},{11,12},{12,11},... | collective-permute-start | bytes 983048 | tf_op jit(solution)/shard_map/ppermute | solution.py:535
  26.8 10.0 %collective-permute-start.6 = (bf16[16,4096]{1,0:T(8,128)(2,1)S(1)}, bf16[16,4096]{1,0:T(8,128)(2,1)S(1)}, u32[]{:S(2)}, u32[]{:S(2)}) collective-permute-start(bf16[16,4096]{1,0:T(8,128)(2,1)S(1)} %get-tuple-element.35), channel_id=1, source_target_pairs={{0,8},{8,0},{16,24},{24,16},{1,9},{9,1},{17,25},{25,17},{2,10},{10... | collective-permute-start | bytes 393224 | tf_op jit(solution)/shard_map/ppermute | solution.py:529
  26.9 9.9 %collective-permute-start.7 = (bf16[16,4096]{1,0:T(8,128)(2,1)S(1)}, bf16[16,4096]{1,0:T(8,128)(2,1)S(1)}, u32[]{:S(2)}, u32[]{:S(2)}) collective-permute-start(bf16[16,4096]{1,0:T(8,128)(2,1)S(1)} %get-tuple-element.36), channel_id=1, source_target_pairs={{8,16},{16,8},{9,17},{17,9},{10,18},{18,10},{11,19},{19,11},{12,20... | collective-permute-start | bytes 393224 | tf_op jit(solution)/shard_map/ppermute | solution.py:535
  30.6 4.7 %collective-permute-start.8 = (bf16[16,1024]{1,0:T(8,128)(2,1)S(1)}, bf16[16,1024]{1,0:T(8,128)(2,1)S(1)}, u32[]{:S(2)}, u32[]{:S(2)}) collective-permute-start(bf16[16,1024]{1,0:T(8,128)(2,1)S(1)} %get-tuple-element.37), channel_id=1, source_target_pairs={{0,8},{8,0},{16,24},{24,16},{1,9},{9,1},{17,25},{25,17},{2,10},{10... | collective-permute-start | bytes 98312 | tf_op jit(solution)/shard_map/ppermute | solution.py:529
  30.6 6.1 %collective-permute-start.9 = (bf16[16,1024]{1,0:T(8,128)(2,1)S(1)}, bf16[16,1024]{1,0:T(8,128)(2,1)S(1)}, u32[]{:S(2)}, u32[]{:S(2)}) collective-permute-start(bf16[16,1024]{1,0:T(8,128)(2,1)S(1)} %get-tuple-element.38), channel_id=1, source_target_pairs={{8,16},{16,8},{9,17},{17,9},{10,18},{18,10},{11,19},{19,11},{12,20... | collective-permute-start | bytes 98312 | tf_op jit(solution)/shard_map/ppermute | solution.py:535

commit v8 on v7

--- a/solution.py
+++ b/solution.py
@@ -485,43 +485,60 @@
     )(mid, even, odd)
 
 
-def close_kernel(
-    out_in, rims_ref, even_ref, odd_ref, even_corner, odd_corner, out_ref, total, sems
-):
+def edges_kernel(out_in, rims_ref, even_ref, odd_ref, out_ref, corners_ref, total, sems):
     del out_in
     gx, gy = parity("gx"), parity("gy")
-    band = even_corner.shape[1]
-    far = pl.ds(pl.multiple_of(gy * (out_ref.shape[1] - band), band), band)
+    rows, columns = out_ref.shape
+    band = corners_ref.shape[2]
+    far = pl.ds(pl.multiple_of(gy * (columns - band), band), band)
     copies = []
-    sides = ((even_ref, even_corner, 1 - gx), (odd_ref, odd_corner, gx))
-    for k, (ref, corner, side) in enumerate(sides):
+    for k, (ref, side) in enumerate(((even_ref, 1 - gx), (odd_ref, gx))):
         at = pl.ds(pl.multiple_of(side * HALF, HALF), HALF)
         total[k] = rims_ref[at, :] + ref[...].astype(F32)
-        total[k, :, far] += corner[...].astype(F32)
-        first = pl.multiple_of(side * (out_ref.shape[0] - HALF), HALF)
+        first = pl.multiple_of(side * (rows - HALF), HALF)
         copies.append(
             pltpu.make_async_copy(total.at[k], out_ref.at[pl.ds(first, HALF), :], sems.at[k])
         )
         copies[-1].start()
+        corners_ref[k] = total[k, :, far]
     for copy in copies:
         copy.wait()
 
 
-def close(out, rims, *received):
-    vmem = pl.BlockSpec(memory_space=pltpu.VMEM)
+def close_kernel(out_in, corners_ref, even_ref, odd_ref, out_ref, total, sems):
+    del out_in
+    gx, gy = parity("gx"), parity("gy")
+    rows, columns = out_ref.shape
+    band = even_ref.shape[1]
+    far = pl.ds(pl.multiple_of(gy * (columns - band), band), band)
+    copies = []
+    for k, (ref, side) in enumerate(((even_ref, 1 - gx), (odd_ref, gx))):
+        total[k] = corners_ref[k] + ref[...].astype(F32)
+        at = pl.ds(pl.multiple_of(side * (rows - HALF), HALF), HALF)
+        copies.append(pltpu.make_async_copy(total.at[k], out_ref.at[at, far], sems.at[k]))
+        copies[-1].start()
+    for copy in copies:
+        copy.wait()
+
+
+def close(kernel, name, width, out, kept, even, odd):
+    vmem, anywhere = pl.BlockSpec(memory_space=pltpu.VMEM), pl.BlockSpec(memory_space=pl.ANY)
+    corners = jax.ShapeDtypeStruct((2, HALF, HALF * DEPTH), F32)
+    first = kernel is edges_kernel
+    shape = jax.ShapeDtypeStruct(out.shape, F32)
     return pl.pallas_call(
-        close_kernel,
-        in_specs=[pl.BlockSpec(memory_space=pl.ANY)] + [vmem] * 5,
-        out_specs=pl.BlockSpec(memory_space=pl.ANY),
-        out_shape=jax.ShapeDtypeStruct(out.shape, F32),
+        kernel,
+        in_specs=[anywhere, vmem, vmem, vmem],
+        out_specs=(anywhere, vmem) if first else anywhere,
+        out_shape=(shape, corners) if first else shape,
         scratch_shapes=[
-            pltpu.VMEM((2, HALF, out.shape[1]), F32),
+            pltpu.VMEM((2, HALF, width), F32),
             pltpu.SemaphoreType.DMA((2,)),
         ],
         input_output_aliases={0: 0},
         compiler_params=pltpu.CompilerParams(vmem_limit_bytes=16 << 20),
-        name="close",
-    )(out, rims, *received)
+        name=name,
+    )(out, kept, even, odd)
 
 
 def swap_even(value, axis):
@@ -561,7 +578,8 @@
     even_corner = swap_even(out_even, "gx")
     odd_corner = swap_odd(out_odd, "gx")
     out, rims = fold(mid, even_y, odd_y)
-    return close(out, rims, even_x, odd_x, even_corner, odd_corner)
+    out, corners = close(edges_kernel, "edges", out.shape[1], out, rims, even_x, odd_x)
+    return close(close_kernel, "corners", HALF * DEPTH, out, corners, even_corner, odd_corner)
 
 
 def solution(mesh):

time: 37.9 us -> 37.7 us (level)
  waiting for transfers between devices: 3.33 us -> 2.47 us
  Pallas kernels: 13.4 us -> 14.1 us
    ppermute x5, waiting for transfers between devices: 3.32 us -> 2.45 us  [swap_odd(): return lax.ppermute(value, axis, pairs)]
    pallas_call x1 -> x2, Pallas kernels: 0.85 us -> 1.52 us  [close(): pl.pallas_call(kernel, in_specs=[anywhere, vmem, vmem, vmem], out_specs=(...]
  transfers between devices with their start and end apart: 10 -> 10, of which waited for: 3 -> 3; matrix products, arithmetic and copies ran while one was open for 0% -> 0% of each run, Pallas kernels for 23% -> 26%
where the time goes in v8:
time: 37.7 us; the launch traced here: 37.4 us
  starting transfers between devices  19.5 us (52%)
  Pallas kernels  14.1 us (37%)
  waiting for transfers between devices  2.47 us (7%)
  local copies, waits for them, and re-layouts  1.05 us (3%)
    ppermute x5, starting transfers between devices, swap_odd(): return lax.ppermute(value, axis, pairs)  17.3 us
    pallas_call x1, Pallas kernels, respond(): pl.pallas_call(functools.partial(respond_kernel, patches), out_shape=(jax...  3.66 us
    pallas_call x1, Pallas kernels, image_forward(): pl.pallas_call(functools.partial(fetching_kernel, patch), in_specs=[pl.Bl...  3.06 us
    ppermute x5, waiting for transfers between devices, swap_odd(): return lax.ppermute(value, axis, pairs)  2.45 us
    pallas_call x1, Pallas kernels, middle(): pl.pallas_call(middle_kernel, out_shape=jax.ShapeDtypeStruct((rows, PATCH...  2.3 us
    ppermute x5, starting transfers between devices, swap_even(): lax.ppermute(value, axis, [(i, i ^ 1) for i in range(count) if i ^ 1 < co...  2.19 us
    pallas_call x1, Pallas kernels, image_forward(): pl.pallas_call(functools.partial(image_kernel, patch), scratch_shapes=scr...  1.66 us
    pallas_call x1, Pallas kernels, fold(): pl.pallas_call(fold_kernel, out_shape=(jax.ShapeDtypeStruct((rows, mid.sh...  1.62 us
  transfers between devices with their start and end apart: 10, of which 3 were waited for; matrix products, arithmetic and copies ran while one was open for 0% of the time, Pallas kernels for 26%

profile of v8, /device:TPU:19, one launch (start us, length us, event | category | flops | bytes accessed | tf_op | source)
XLA Modules:
  0.0 37.4 jit_solution(5791944375826551863)
XLA Ops:
  0.0 1.0 %constant_dynamic-slice_fusion = (bf16[1,2,32,1024]{3,2,1,0:T(8,128)(2,1)S(1)}, bf16[1,2,32,1024]{3,2,1,0:T(8,128)(2,1)S(1)}) fusion(bf16[4,2,32,1024]{3,2,1,0:T(8,128)(2,1)} %psfs_ref.1, s32[]{:T(128)S(6)} %select_n.7, s32[]{:T(128)S(6)} %select_n.6), kind=kLoop, calls=%fused_computation | loop fusion | bytes 524296 | tf_op jit(solution)/shard_map/dynamic_slice | solution.py:560
  1.0 0.3 collective-permute-start.1
  1.3 0.0 copy-start.11
  1.3 4.3 %collective-permute-start = (bf16[1,2,32,1024]{3,2,1,0:T(8,128)(2,1)S(1)}, bf16[1,2,32,1024]{3,2,1,0:T(8,128)(2,1)S(1)}, u32[]{:S(2)}, u32[]{:S(2)}) collective-permute-start(bf16[1,2,32,1024]{3,2,1,0:T(8,128)(2,1)S(1)} %get-tuple-element.44), channel_id=1, source_target_pairs={{8,16},{16,8},{9,17},{17,9},{10,18},{18,10},{11,19},{19,11},{12,20... | collective-permute-start | bytes 393224 | tf_op jit(solution)/shard_map/ppermute | solution.py:552
  5.7 3.1 %image_first.1.refs_0_ = bf16[48,192,128]{2,1,0:T(8,128)(2,1)S(1)} custom-call(f32[128,4096]{1,0:T(8,128)} %image_ref, bf16[96,64]{1,0:T(8,128)(2,1)} %constant.36.clone.refs_0_.tx_ref, bf16[256,512]{1,0:T(8,128)(2,1)} %constant.37.clone.refs_1_.tz_ref, bf16[192,128]{1,0:T(8,128)(2,1)} %constant.38.clone.refs_2_.ty_ref), custom_call_target="tpu_custom_call" | custom-call | flops 4000000000 | bytes 4000000 | tf_op jit(solution)/shard_map/image_first/pallas_call | solution.py:226
  8.8 0.0 collective-permute-done.1.even_ref
  8.8 0.5 %collective-permute-done.odd_ref = bf16[1,2,32,1024]{3,2,1,0:T(8,128)(2,1)S(1)} collective-permute-done((bf16[1,2,32,1024]{3,2,1,0:T(8,128)(2,1)S(1)}, bf16[1,2,32,1024]{3,2,1,0:T(8,128)(2,1)S(1)}, u32[]{:S(2)}, u32[]{:S(2)}) %collective-permute-start) | collective-permute-done | bytes 131104 | tf_op jit(solution)/shard_map/ppermute | solution.py:552
  9.3 0.2 blend_x.1
  9.5 0.0 copy-start.1
  9.5 0.0 copy-start.2
  9.5 0.0 copy-start.3
  9.5 0.0 copy-start.4
  9.5 0.0 copy-start.5
  9.6 0.0 copy-start.6
  9.6 1.5 %collective-permute-start.2 = (bf16[2,32,1024]{2,1,0:T(8,128)(2,1)S(1)}, bf16[2,32,1024]{2,1,0:T(8,128)(2,1)S(1)}, u32[]{:S(2)}, u32[]{:S(2)}) collective-permute-start(bf16[2,32,1024]{2,1,0:T(8,128)(2,1)S(1)} %get-tuple-element.30.refs_3_), channel_id=1, source_target_pairs={{0,1},{1,0},{2,3},{3,2},{4,5},{5,4},{6,7},{7,6},{8,9},{9,8},{10,11... | collective-permute-start | bytes 393224 | tf_op jit(solution)/shard_map/ppermute | solution.py:546
  11.1 3.2 %collective-permute-start.3 = (bf16[2,32,1024]{2,1,0:T(8,128)(2,1)S(1)}, bf16[2,32,1024]{2,1,0:T(8,128)(2,1)S(1)}, u32[]{:S(2)}, u32[]{:S(2)}) collective-permute-start(bf16[2,32,1024]{2,1,0:T(8,128)(2,1)S(1)} %get-tuple-element.31.refs_4_), channel_id=1, source_target_pairs={{1,2},{2,1},{3,4},{4,3},{5,6},{6,5},{9,10},{10,9},{11,12},{12,11},... | collective-permute-start | bytes 393224 | tf_op jit(solution)/shard_map/ppermute | solution.py:552
  14.4 1.7 %image_forward.1.refs_1_ = bf16[48,192,128]{2,1,0:T(8,128)(2,1)S(1)} custom-call(f32[128,4096]{1,0:T(8,128)S(1)} %copy-done.7, bf16[96,64]{1,0:T(8,128)(2,1)S(1)} %copy-done.11, bf16[256,512]{1,0:T(8,128)(2,1)S(1)} %copy-done.8, bf16[192,128]{1,0:T(8,128)(2,1)S(1)} %copy-done.10), custom_call_target="tpu_custom_call" | custom-call | flops 4000000000 | bytes 4000000 | tf_op jit(solution)/shard_map/image_forward/pallas_call | solution.py:220
  16.0 0.0 copy-start.9
  16.1 1.3 %collective-permute-done.3.refs_5_ = bf16[2,32,1024]{2,1,0:T(8,128)(2,1)S(1)} collective-permute-done((bf16[2,32,1024]{2,1,0:T(8,128)(2,1)S(1)}, bf16[2,32,1024]{2,1,0:T(8,128)(2,1)S(1)}, u32[]{:S(2)}, u32[]{:S(2)}) %collective-permute-start.3) | collective-permute-done | bytes 131104 | tf_op jit(solution)/shard_map/ppermute | solution.py:552
  17.4 3.7 %respond.1 = (bf16[2,24,192,256]{3,2,1,0:T(8,128)(2,1)S(1)}, bf16[160,1024]{1,0:T(8,128)(2,1)S(1)}, bf16[160,1024]{1,0:T(8,128)(2,1)S(1)}) custom-call(bf16[48,192,128]{2,1,0:T(8,128)(2,1)S(1)} %image_first.1.refs_0_, bf16[48,192,128]{2,1,0:T(8,128)(2,1)S(1)} %image_forward.1.refs_1_, bf16[2,32,1024]{2,1,0:T(8,128)(2,1)S(1)} %collective-permute-done.2.refs_2_, ...), custom_call_target="tpu_custom_call" | custom-call | tf_op jit(solution)/shard_map/respond/pallas_call | solution.py:370
  21.1 0.2 collective-permute-start.4
  21.3 3.1 %collective-permute-start.5 = (bf16[160,1024]{1,0:T(8,128)(2,1)S(1)}, bf16[160,1024]{1,0:T(8,128)(2,1)S(1)}, u32[]{:S(2)}, u32[]{:S(2)}) collective-permute-start(bf16[160,1024]{1,0:T(8,128)(2,1)S(1)} %get-tuple-element.34), channel_id=1, source_target_pairs={{1,2},{2,1},{3,4},{4,3},{5,6},{6,5},{9,10},{10,9},{11,12},{12,11},... | collective-permute-start | bytes 983048 | tf_op jit(solution)/shard_map/ppermute | solution.py:552
  24.4 2.3 %middle.1.mid_ref = f32[160,4096]{1,0:T(8,128)S(1)} custom-call(bf16[2,24,192,256]{3,2,1,0:T(8,128)(2,1)S(1)} %get-tuple-element.32.product_ref, bf16[128,192]{1,0:T(8,128)(2,1)S(1)} %copy-done.9, bf16[512,256]{1,0:T(8,128)(2,1)S(1)} %copy-done.2, bf16[160,192]{1,0:T(8,128)(2,1)S(1)} %copy-done.3), custom_call_target="tpu_custom_call" | custom-call | flops 3000000000 | bytes 6000000 | tf_op jit(solution)/shard_map/middle/pallas_call | solution.py:388
  26.7 0.1 x_rims.1
  26.8 0.1 collective-permute-start.6
  26.9 3.7 %collective-permute-start.7 = (bf16[16,4096]{1,0:T(8,128)(2,1)S(1)}, bf16[16,4096]{1,0:T(8,128)(2,1)S(1)}, u32[]{:S(2)}, u32[]{:S(2)}) collective-permute-start(bf16[16,4096]{1,0:T(8,128)(2,1)S(1)} %get-tuple-element.38), channel_id=1, source_target_pairs={{8,16},{16,8},{9,17},{17,9},{10,18},{18,10},{11,19},{19,11},{12,20... | collective-permute-start | bytes 393224 | tf_op jit(solution)/shard_map/ppermute | solution.py:552
  30.6 0.1 collective-permute-start.8
  30.6 3.0 %collective-permute-start.9 = (bf16[16,1024]{1,0:T(8,128)(2,1)S(1)}, bf16[16,1024]{1,0:T(8,128)(2,1)S(1)}, u32[]{:S(2)}, u32[]{:S(2)}) collective-permute-start(bf16[16,1024]{1,0:T(8,128)(2,1)S(1)} %get-tuple-element.42), channel_id=1, source_target_pairs={{8,16},{16,8},{9,17},{17,9},{10,18},{18,10},{11,19},{19,11},{12,20... | collective-permute-start | bytes 98312 | tf_op jit(solution)/shard_map/ppermute | solution.py:552
  33.6 1.6 %fold.1 = (f32[128,4096]{1,0:T(8,128)}, f32[32,4096]{1,0:T(8,128)S(1)}) custom-call(f32[160,4096]{1,0:T(8,128)S(1)} %middle.1.mid_ref, bf16[160,1024]{1,0:T(8,128)(2,1)S(1)} %collective-permute-done.4.even_ref, bf16[160,1024]{1,0:T(8,128)(2,1)S(1)} %collective-permute-done.5.odd_ref), custom_call_target="tpu_custom_call" | custom-call | flops 10000000 | bytes 8000000 | tf_op jit(solution)/shard_map/fold/pallas_call | solution.py:474
  35.3 0.8 %edges.1 = (f32[128,4096]{1,0:T(8,128)}, f32[2,16,1024]{2,1,0:T(8,128)S(1)}) custom-call(f32[128,4096]{1,0:T(8,128)} %get-tuple-element.35.out_in, f32[32,4096]{1,0:T(8,128)S(1)} %get-tuple-element.36.rims_ref, bf16[16,4096]{1,0:T(8,128)(2,1)S(1)} %collective-permute-done.6.even_ref, ...), custom_call_target="tpu_custom_call", output_to_operand_aliasing={{0}: (0, {})} | custom-call | tf_op jit(solution)/shard_map/edges/pallas_call | solution.py:529
  36.1 0.6 %collective-permute-done.9.odd_ref = bf16[16,1024]{1,0:T(8,128)(2,1)S(1)} collective-permute-done((bf16[16,1024]{1,0:T(8,128)(2,1)S(1)}, bf16[16,1024]{1,0:T(8,128)(2,1)S(1)}, u32[]{:S(2)}, u32[]{:S(2)}) %collective-permute-start.9) | collective-permute-done | bytes 32800 | tf_op jit(solution)/shard_map/ppermute | solution.py:552
  36.8 0.7 %corners.1 = f32[128,4096]{1,0:T(8,128)} custom-call(f32[128,4096]{1,0:T(8,128)} %get-tuple-element.39.out_in, f32[2,16,1024]{2,1,0:T(8,128)S(1)} %get-tuple-element.40.corners_ref, bf16[16,1024]{1,0:T(8,128)(2,1)S(1)} %collective-permute-done.8.even_ref, bf16[16,1024]{1,0:T(8,128)(2,1)S(1)} %collective-permute-done.9.odd_ref), custom_call_target="tpu_custom_call", output_to_operand_aliasing={{}: (0, {})} | custom-call | tf_op jit(solution)/shard_map/corners/pallas_call | solution.py:529
  (23 shorter events, 0.1 us)
Async XLA Ops:
  1.0 7.8 %collective-permute-start.1 = (bf16[1,2,32,1024]{3,2,1,0:T(8,128)(2,1)S(1)}, bf16[1,2,32,1024]{3,2,1,0:T(8,128)(2,1)S(1)}, u32[]{:S(2)}, u32[]{:S(2)}) collective-permute-start(bf16[1,2,32,1024]{3,2,1,0:T(8,128)(2,1)S(1)} %get-tuple-element.43), channel_id=1, source_target_pairs={{0,8},{8,0},{16,24},{24,16},{1,9},{9,1},{17,25},{25,17},{2,10},{10... | collective-permute-start | bytes 393224 | tf_op jit(solution)/shard_map/ppermute | solution.py:546
  1.3 8.0 %copy-start = (bf16[4,2,32,1024]{3,2,1,0:T(8,128)(2,1)S(1)}, bf16[4,2,32,1024]{3,2,1,0:T(8,128)(2,1)}, u32[]{:S(2)}) copy-start(bf16[4,2,32,1024]{3,2,1,0:T(8,128)(2,1)} %psfs_ref.1) | copy-start | bytes 1572868
  1.3 13.0 %copy-start.7 = (f32[128,4096]{1,0:T(8,128)S(1)}, f32[128,4096]{1,0:T(8,128)}, u32[]{:S(2)}) copy-start(f32[128,4096]{1,0:T(8,128)} %image_ref) | copy-start | bytes 6291460
  1.3 13.0 %copy-start.8 = (bf16[256,512]{1,0:T(8,128)(2,1)S(1)}, bf16[256,512]{1,0:T(8,128)(2,1)}, u32[]{:S(2)}) copy-start(bf16[256,512]{1,0:T(8,128)(2,1)} %constant.37.clone.refs_1_.tz_ref) | copy-start | bytes 786436
  1.3 13.0 %copy-start.10 = (bf16[192,128]{1,0:T(8,128)(2,1)S(1)}, bf16[192,128]{1,0:T(8,128)(2,1)}, u32[]{:S(2)}) copy-start(bf16[192,128]{1,0:T(8,128)(2,1)} %constant.38.clone.refs_2_.ty_ref) | copy-start | bytes 147460
  1.3 13.0 %copy-start.11 = (bf16[96,64]{1,0:T(8,128)(2,1)S(1)}, bf16[96,64]{1,0:T(8,128)(2,1)}, u32[]{:S(2)}) copy-start(bf16[96,64]{1,0:T(8,128)(2,1)} %constant.36.clone.refs_0_.tx_ref) | copy-start | bytes 36868
  1.3 8.0 %collective-permute-start = (bf16[1,2,32,1024]{3,2,1,0:T(8,128)(2,1)S(1)}, bf16[1,2,32,1024]{3,2,1,0:T(8,128)(2,1)S(1)}, u32[]{:S(2)}, u32[]{:S(2)}) collective-permute-start(bf16[1,2,32,1024]{3,2,1,0:T(8,128)(2,1)S(1)} %get-tuple-element.44), channel_id=1, source_target_pairs={{8,16},{16,8},{9,17},{17,9},{10,18},{18,10},{11,19},{19,11},{12,20... | collective-permute-start | bytes 393224 | tf_op jit(solution)/shard_map/ppermute | solution.py:552
  9.5 7.9 %copy-start.1 = (bf16[256,1024]{1,0:T(8,128)(2,1)S(1)}, bf16[256,1024]{1,0:T(8,128)(2,1)}, u32[]{:S(2)}) copy-start(bf16[256,1024]{1,0:T(8,128)(2,1)} %constant.44.clone.refs_7_) | copy-start | bytes 1572868
  9.5 7.8 %copy-start.2 = (bf16[512,256]{1,0:T(8,128)(2,1)S(1)}, bf16[512,256]{1,0:T(8,128)(2,1)}, u32[]{:S(2)}) copy-start(bf16[512,256]{1,0:T(8,128)(2,1)} %constant.41.clone.refs_10_.tiz) | copy-start | bytes 786436
  9.5 7.8 %copy-start.3 = (bf16[160,192]{1,0:T(8,128)(2,1)S(1)}, bf16[160,192]{1,0:T(8,128)(2,1)}, u32[]{:S(2)}) copy-start(bf16[160,192]{1,0:T(8,128)(2,1)} %constant.42.clone.refs_11_.tix) | copy-start | bytes 184324
  9.5 7.8 %copy-start.4 = (bf16[192,64]{1,0:T(8,128)(2,1)S(1)}, bf16[192,64]{1,0:T(8,128)(2,1)}, u32[]{:S(2)}) copy-start(bf16[192,64]{1,0:T(8,128)(2,1)} %constant.45.clone.refs_8_) | copy-start | bytes 73732
  9.5 7.8 %copy-start.5 = (bf16[64,192]{1,0:T(8,128)(2,1)S(1)}, bf16[64,192]{1,0:T(8,128)(2,1)}, u32[]{:S(2)}) copy-start(bf16[64,192]{1,0:T(8,128)(2,1)} %constant.39.clone.refs_9_) | copy-start | bytes 73732
  9.6 7.8 %copy-start.6 = (bf16[96,128]{1,0:T(8,128)(2,1)S(1)}, bf16[96,128]{1,0:T(8,128)(2,1)}, u32[]{:S(2)}) copy-start(bf16[96,128]{1,0:T(8,128)(2,1)} %constant.43.clone.refs_6_) | copy-start | bytes 73732
  9.6 6.5 %collective-permute-start.2 = (bf16[2,32,1024]{2,1,0:T(8,128)(2,1)S(1)}, bf16[2,32,1024]{2,1,0:T(8,128)(2,1)S(1)}, u32[]{:S(2)}, u32[]{:S(2)}) collective-permute-start(bf16[2,32,1024]{2,1,0:T(8,128)(2,1)S(1)} %get-tuple-element.30.refs_3_), channel_id=1, source_target_pairs={{0,1},{1,0},{2,3},{3,2},{4,5},{5,4},{6,7},{7,6},{8,9},{9,8},{10,11... | collective-permute-start | bytes 393224 | tf_op jit(solution)/shard_map/ppermute | solution.py:546
  11.1 6.3 %collective-permute-start.3 = (bf16[2,32,1024]{2,1,0:T(8,128)(2,1)S(1)}, bf16[2,32,1024]{2,1,0:T(8,128)(2,1)S(1)}, u32[]{:S(2)}, u32[]{:S(2)}) collective-permute-start(bf16[2,32,1024]{2,1,0:T(8,128)(2,1)S(1)} %get-tuple-element.31.refs_4_), channel_id=1, source_target_pairs={{1,2},{2,1},{3,4},{4,3},{5,6},{6,5},{9,10},{10,9},{11,12},{12,11},... | collective-permute-start | bytes 393224 | tf_op jit(solution)/shard_map/ppermute | solution.py:552
  16.0 8.4 %copy-start.9 = (bf16[128,192]{1,0:T(8,128)(2,1)S(1)}, bf16[128,192]{1,0:T(8,128)(2,1)}, u32[]{:S(2)}) copy-start(bf16[128,192]{1,0:T(8,128)(2,1)} %constant.40.clone.tiy) | copy-start | bytes 147460
  21.1 5.6 %collective-permute-start.4 = (bf16[160,1024]{1,0:T(8,128)(2,1)S(1)}, bf16[160,1024]{1,0:T(8,128)(2,1)S(1)}, u32[]{:S(2)}, u32[]{:S(2)}) collective-permute-start(bf16[160,1024]{1,0:T(8,128)(2,1)S(1)} %get-tuple-element.33), channel_id=1, source_target_pairs={{0,1},{1,0},{2,3},{3,2},{4,5},{5,4},{6,7},{7,6},{8,9},{9,8},{10,11... | collective-permute-start | bytes 983048 | tf_op jit(solution)/shard_map/ppermute | solution.py:546
  21.3 9.2 %collective-permute-start.5 = (bf16[160,1024]{1,0:T(8,128)(2,1)S(1)}, bf16[160,1024]{1,0:T(8,128)(2,1)S(1)}, u32[]{:S(2)}, u32[]{:S(2)}) collective-permute-start(bf16[160,1024]{1,0:T(8,128)(2,1)S(1)} %get-tuple-element.34), channel_id=1, source_target_pairs={{1,2},{2,1},{3,4},{4,3},{5,6},{6,5},{9,10},{10,9},{11,12},{12,11},... | collective-permute-start | bytes 983048 | tf_op jit(solution)/shard_map/ppermute | solution.py:552
  26.8 8.5 %collective-permute-start.6 = (bf16[16,4096]{1,0:T(8,128)(2,1)S(1)}, bf16[16,4096]{1,0:T(8,128)(2,1)S(1)}, u32[]{:S(2)}, u32[]{:S(2)}) collective-permute-start(bf16[16,4096]{1,0:T(8,128)(2,1)S(1)} %get-tuple-element.37), channel_id=1, source_target_pairs={{0,8},{8,0},{16,24},{24,16},{1,9},{9,1},{17,25},{25,17},{2,10},{10... | collective-permute-start | bytes 393224 | tf_op jit(solution)/shard_map/ppermute | solution.py:546
  26.9 8.4 %collective-permute-start.7 = (bf16[16,4096]{1,0:T(8,128)(2,1)S(1)}, bf16[16,4096]{1,0:T(8,128)(2,1)S(1)}, u32[]{:S(2)}, u32[]{:S(2)}) collective-permute-start(bf16[16,4096]{1,0:T(8,128)(2,1)S(1)} %get-tuple-element.38), channel_id=1, source_target_pairs={{8,16},{16,8},{9,17},{17,9},{10,18},{18,10},{11,19},{19,11},{12,20... | collective-permute-start | bytes 393224 | tf_op jit(solution)/shard_map/ppermute | solution.py:552
  30.6 5.6 %collective-permute-start.8 = (bf16[16,1024]{1,0:T(8,128)(2,1)S(1)}, bf16[16,1024]{1,0:T(8,128)(2,1)S(1)}, u32[]{:S(2)}, u32[]{:S(2)}) collective-permute-start(bf16[16,1024]{1,0:T(8,128)(2,1)S(1)} %get-tuple-element.41), channel_id=1, source_target_pairs={{0,8},{8,0},{16,24},{24,16},{1,9},{9,1},{17,25},{25,17},{2,10},{10... | collective-permute-start | bytes 98312 | tf_op jit(solution)/shard_map/ppermute | solution.py:546
  30.6 6.1 %collective-permute-start.9 = (bf16[16,1024]{1,0:T(8,128)(2,1)S(1)}, bf16[16,1024]{1,0:T(8,128)(2,1)S(1)}, u32[]{:S(2)}, u32[]{:S(2)}) collective-permute-start(bf16[16,1024]{1,0:T(8,128)(2,1)S(1)} %get-tuple-element.42), channel_id=1, source_target_pairs={{8,16},{16,8},{9,17},{17,9},{10,18},{18,10},{11,19},{19,11},{12,20... | collective-permute-start | bytes 98312 | tf_op jit(solution)/shard_map/ppermute | solution.py:552

commit v9 on v8

--- a/solution.py
+++ b/solution.py
@@ -384,10 +384,14 @@
         name="respond",
     )(*spectra, *columns, *tables)
 
-    def middle():
+    def middle(even):
         return pl.pallas_call(
             middle_kernel,
-            out_shape=jax.ShapeDtypeStruct((rows, PATCH * DEPTH), F32),
+            out_shape=(
+                jax.ShapeDtypeStruct((rows, PATCH * DEPTH), F32),
+                jax.ShapeDtypeStruct((HALF, PATCH * DEPTH), BF16),
+                jax.ShapeDtypeStruct((HALF, PATCH * DEPTH), BF16),
+            ),
             scratch_shapes=[
                 pltpu.VMEM((patches, KX * inner, 2 * YPER * LANES), BF16),
                 pltpu.VMEM((patches, 2, inner * XSTEP, LANES), F32),
@@ -397,12 +401,14 @@
                 flops=3_000_000_000, bytes_accessed=6_000_000, transcendentals=0
             ),
             name="middle",
-        )(product, inner_table, z_table, x_table)
+        )(product, even, inner_table, z_table, x_table)
 
     return middle, out_even, out_odd
 
 
-def middle_kernel(product_ref, tiy, tiz, tix, out_ref, rows_ref, grid_x):
+def middle_kernel(
+    product_ref, even_ref, tiy, tiz, tix, out_ref, to_odd_ref, to_even_ref, rows_ref, grid_x
+):
     tile = 2 * LANES
     patches = product_ref.shape[0]
     inner = OROWS - EDGE
@@ -417,9 +423,10 @@
         z_swapped(rows_ref, tiz, grid_x, p, inner, 8)
     for t in range(inner // 2):
         out_ref[:, t * tile : (t + 1) * tile] = x_inverted(grid_x, tix, t)
-
-
-def rim_kernel(mid_ref, even_ref, to_odd_ref, to_even_ref):
+    x_rims(out_ref, even_ref, to_odd_ref, to_even_ref)
+
+
+def x_rims(mid_ref, even_ref, to_odd_ref, to_even_ref):
     band = even_ref.shape[1]
     rows, columns = mid_ref.shape[0] - PSFW, mid_ref.shape[1]
     gx, gy = parity("gx"), parity("gy")
@@ -428,16 +435,6 @@
         at = pl.ds(pl.multiple_of(rows + side * HALF, HALF), HALF)
         out[...] = mid_ref[at, :].astype(BF16)
         out[:, corner] = (mid_ref[at, corner] + even_ref[at, :].astype(F32)).astype(BF16)
-
-
-def x_rims(mid, even):
-    shape = jax.ShapeDtypeStruct((HALF, mid.shape[1]), BF16)
-    return pl.pallas_call(
-        rim_kernel,
-        out_shape=(shape,) * 2,
-        compiler_params=pltpu.CompilerParams(vmem_limit_bytes=16 << 20),
-        name="x_rims",
-    )(mid, even)
 
 
 def corner_kernel(odd_ref, to_odd_ref, to_even_ref):
@@ -570,8 +567,7 @@
     middle, out_even, out_odd = respond(spectra, (even, to_even, to_odd, odd))
     odd_y = swap_odd(out_odd, "gy")
     even_y = swap_even(out_even, "gy")
-    mid = middle()
-    out_odd, out_even = x_rims(mid, even_y)
+    mid, out_odd, out_even = middle(even_y)
     even_x = swap_even(out_even, "gx")
     odd_x = swap_odd(out_odd, "gx")
     out_odd, out_even = x_corners(odd_y)

time: 37.7 us -> 37.6 us (level)
    pallas_call x2 -> x1, Pallas kernels: 2.36 us -> 2.31 us  [middle(): pl.pallas_call(middle_kernel, out_shape=(jax.ShapeDtypeStruct((rows, PATC...]
  transfers between devices with their start and end apart: 10 -> 10, of which waited for: 3 -> 3; matrix products, arithmetic and copies ran while one was open for 0% -> 0% of each run, Pallas kernels for 26% -> 25%
where the time goes in v9:
time: 37.6 us; the launch traced here: 37.4 us
  starting transfers between devices  19.6 us (52%)
  Pallas kernels  14.1 us (38%)
  waiting for transfers between devices  2.4 us (6%)
  local copies, waits for them, and re-layouts  1.05 us (3%)
    ppermute x5, starting transfers between devices, swap_odd(): return lax.ppermute(value, axis, pairs)  17.4 us
    pallas_call x1, Pallas kernels, respond(): pl.pallas_call(functools.partial(respond_kernel, patches), out_shape=(jax...  3.65 us
    pallas_call x1, Pallas kernels, image_forward(): pl.pallas_call(functools.partial(fetching_kernel, patch), in_specs=[pl.Bl...  3.06 us
    ppermute x5, waiting for transfers between devices, swap_odd(): return lax.ppermute(value, axis, pairs)  2.39 us
    pallas_call x1, Pallas kernels, middle(): pl.pallas_call(middle_kernel, out_shape=(jax.ShapeDtypeStruct((rows, PATC...  2.31 us
    ppermute x5, starting transfers between devices, swap_even(): lax.ppermute(value, axis, [(i, i ^ 1) for i in range(count) if i ^ 1 < co...  2.19 us
    pallas_call x1, Pallas kernels, image_forward(): pl.pallas_call(functools.partial(image_kernel, patch), scratch_shapes=scr...  1.67 us
    pallas_call x1, Pallas kernels, fold(): pl.pallas_call(fold_kernel, out_shape=(jax.ShapeDtypeStruct((rows, mid.sh...  1.62 us
  transfers between devices with their start and end apart: 10, of which 3 were waited for; matrix products, arithmetic and copies ran while one was open for 0% of the time, Pallas kernels for 25%

profile of v9, /device:TPU:19, one launch (start us, length us, event | category | flops | bytes accessed | tf_op | source)
XLA Modules:
  0.0 37.4 jit_solution(15358484466373823039)
XLA Ops:
  0.0 1.0 %constant_dynamic-slice_fusion = (bf16[1,2,32,1024]{3,2,1,0:T(8,128)(2,1)S(1)}, bf16[1,2,32,1024]{3,2,1,0:T(8,128)(2,1)S(1)}) fusion(bf16[4,2,32,1024]{3,2,1,0:T(8,128)(2,1)} %psfs_ref.1, s32[]{:T(128)S(6)} %select_n.7, s32[]{:T(128)S(6)} %select_n.6), kind=kLoop, calls=%fused_computation | loop fusion | bytes 524296 | tf_op jit(solution)/shard_map/dynamic_slice | solution.py:557
  1.0 0.3 collective-permute-start.1
  1.3 0.0 copy-start.11
  1.3 4.3 %collective-permute-start = (bf16[1,2,32,1024]{3,2,1,0:T(8,128)(2,1)S(1)}, bf16[1,2,32,1024]{3,2,1,0:T(8,128)(2,1)S(1)}, u32[]{:S(2)}, u32[]{:S(2)}) collective-permute-start(bf16[1,2,32,1024]{3,2,1,0:T(8,128)(2,1)S(1)} %get-tuple-element.46), channel_id=1, source_target_pairs={{8,16},{16,8},{9,17},{17,9},{10,18},{18,10},{11,19},{19,11},{12,20... | collective-permute-start | bytes 393224 | tf_op jit(solution)/shard_map/ppermute | solution.py:549
  5.7 3.1 %image_first.1.refs_0_ = bf16[48,192,128]{2,1,0:T(8,128)(2,1)S(1)} custom-call(f32[128,4096]{1,0:T(8,128)} %image_ref, bf16[96,64]{1,0:T(8,128)(2,1)} %constant.36.clone.refs_0_.tx_ref, bf16[256,512]{1,0:T(8,128)(2,1)} %constant.37.clone.refs_1_.tz_ref, bf16[192,128]{1,0:T(8,128)(2,1)} %constant.38.clone.refs_2_.ty_ref), custom_call_target="tpu_custom_call" | custom-call | flops 4000000000 | bytes 4000000 | tf_op jit(solution)/shard_map/image_first/pallas_call | solution.py:226
  8.8 0.0 collective-permute-done.1.even_ref
  8.8 0.5 %collective-permute-done.odd_ref = bf16[1,2,32,1024]{3,2,1,0:T(8,128)(2,1)S(1)} collective-permute-done((bf16[1,2,32,1024]{3,2,1,0:T(8,128)(2,1)S(1)}, bf16[1,2,32,1024]{3,2,1,0:T(8,128)(2,1)S(1)}, u32[]{:S(2)}, u32[]{:S(2)}) %collective-permute-start) | collective-permute-done | bytes 131104 | tf_op jit(solution)/shard_map/ppermute | solution.py:549
  9.3 0.2 blend_x.1
  9.5 0.0 copy-start.1
  9.5 0.0 copy-start.2
  9.5 0.0 copy-start.3
  9.5 0.0 copy-start.4
  9.5 0.0 copy-start.5
  9.6 0.0 copy-start.6
  9.6 1.5 %collective-permute-start.2 = (bf16[2,32,1024]{2,1,0:T(8,128)(2,1)S(1)}, bf16[2,32,1024]{2,1,0:T(8,128)(2,1)S(1)}, u32[]{:S(2)}, u32[]{:S(2)}) collective-permute-start(bf16[2,32,1024]{2,1,0:T(8,128)(2,1)S(1)} %get-tuple-element.31.refs_3_), channel_id=1, source_target_pairs={{0,1},{1,0},{2,3},{3,2},{4,5},{5,4},{6,7},{7,6},{8,9},{9,8},{10,11... | collective-permute-start | bytes 393224 | tf_op jit(solution)/shard_map/ppermute | solution.py:543
  11.1 3.2 %collective-permute-start.3 = (bf16[2,32,1024]{2,1,0:T(8,128)(2,1)S(1)}, bf16[2,32,1024]{2,1,0:T(8,128)(2,1)S(1)}, u32[]{:S(2)}, u32[]{:S(2)}) collective-permute-start(bf16[2,32,1024]{2,1,0:T(8,128)(2,1)S(1)} %get-tuple-element.32.refs_4_), channel_id=1, source_target_pairs={{1,2},{2,1},{3,4},{4,3},{5,6},{6,5},{9,10},{10,9},{11,12},{12,11},... | collective-permute-start | bytes 393224 | tf_op jit(solution)/shard_map/ppermute | solution.py:549
  14.4 1.7 %image_forward.1.refs_1_ = bf16[48,192,128]{2,1,0:T(8,128)(2,1)S(1)} custom-call(f32[128,4096]{1,0:T(8,128)S(1)} %copy-done.7, bf16[96,64]{1,0:T(8,128)(2,1)S(1)} %copy-done.11, bf16[256,512]{1,0:T(8,128)(2,1)S(1)} %copy-done.8, bf16[192,128]{1,0:T(8,128)(2,1)S(1)} %copy-done.10), custom_call_target="tpu_custom_call" | custom-call | flops 4000000000 | bytes 4000000 | tf_op jit(solution)/shard_map/image_forward/pallas_call | solution.py:220
  16.0 0.0 copy-start.9
  16.1 1.3 %collective-permute-done.3.refs_5_ = bf16[2,32,1024]{2,1,0:T(8,128)(2,1)S(1)} collective-permute-done((bf16[2,32,1024]{2,1,0:T(8,128)(2,1)S(1)}, bf16[2,32,1024]{2,1,0:T(8,128)(2,1)S(1)}, u32[]{:S(2)}, u32[]{:S(2)}) %collective-permute-start.3) | collective-permute-done | bytes 131104 | tf_op jit(solution)/shard_map/ppermute | solution.py:549
  17.4 3.7 %respond.1 = (bf16[2,24,192,256]{3,2,1,0:T(8,128)(2,1)S(1)}, bf16[160,1024]{1,0:T(8,128)(2,1)S(1)}, bf16[160,1024]{1,0:T(8,128)(2,1)S(1)}) custom-call(bf16[48,192,128]{2,1,0:T(8,128)(2,1)S(1)} %image_first.1.refs_0_, bf16[48,192,128]{2,1,0:T(8,128)(2,1)S(1)} %image_forward.1.refs_1_, bf16[2,32,1024]{2,1,0:T(8,128)(2,1)S(1)} %collective-permute-done.2.refs_2_, ...), custom_call_target="tpu_custom_call" | custom-call | tf_op jit(solution)/shard_map/respond/pallas_call | solution.py:370
  21.1 0.2 collective-permute-start.4
  21.3 3.1 %collective-permute-start.5 = (bf16[160,1024]{1,0:T(8,128)(2,1)S(1)}, bf16[160,1024]{1,0:T(8,128)(2,1)S(1)}, u32[]{:S(2)}, u32[]{:S(2)}) collective-permute-start(bf16[160,1024]{1,0:T(8,128)(2,1)S(1)} %get-tuple-element.36), channel_id=1, source_target_pairs={{1,2},{2,1},{3,4},{4,3},{5,6},{6,5},{9,10},{10,9},{11,12},{12,11},... | collective-permute-start | bytes 983048 | tf_op jit(solution)/shard_map/ppermute | solution.py:549
  24.4 2.3 %middle.1 = (f32[160,4096]{1,0:T(8,128)S(1)}, bf16[16,4096]{1,0:T(8,128)(2,1)S(1)}, bf16[16,4096]{1,0:T(8,128)(2,1)S(1)}) custom-call(bf16[2,24,192,256]{3,2,1,0:T(8,128)(2,1)S(1)} %get-tuple-element.33.product_ref, bf16[160,1024]{1,0:T(8,128)(2,1)S(1)} %collective-permute-done.4.even_ref, bf16[128,192]{1,0:T(8,128)(2,1)S(1)} %copy-done.9, ...), custom_call_target="tpu_custom_call" | custom-call | flops 3000000000 | bytes 6000000 | tf_op jit(solution)/shard_map/middle/pallas_call | solution.py:388
  26.7 0.1 collective-permute-start.6
  26.8 3.7 %collective-permute-start.7 = (bf16[16,4096]{1,0:T(8,128)(2,1)S(1)}, bf16[16,4096]{1,0:T(8,128)(2,1)S(1)}, u32[]{:S(2)}, u32[]{:S(2)}) collective-permute-start(bf16[16,4096]{1,0:T(8,128)(2,1)S(1)} %get-tuple-element.40), channel_id=1, source_target_pairs={{8,16},{16,8},{9,17},{17,9},{10,18},{18,10},{11,19},{19,11},{12,20... | collective-permute-start | bytes 393224 | tf_op jit(solution)/shard_map/ppermute | solution.py:549
  30.5 0.1 collective-permute-start.8
  30.6 3.0 %collective-permute-start.9 = (bf16[16,1024]{1,0:T(8,128)(2,1)S(1)}, bf16[16,1024]{1,0:T(8,128)(2,1)S(1)}, u32[]{:S(2)}, u32[]{:S(2)}) collective-permute-start(bf16[16,1024]{1,0:T(8,128)(2,1)S(1)} %get-tuple-element.44), channel_id=1, source_target_pairs={{8,16},{16,8},{9,17},{17,9},{10,18},{18,10},{11,19},{19,11},{12,20... | collective-permute-start | bytes 98312 | tf_op jit(solution)/shard_map/ppermute | solution.py:549
  33.6 1.6 %fold.1 = (f32[128,4096]{1,0:T(8,128)}, f32[32,4096]{1,0:T(8,128)S(1)}) custom-call(f32[160,4096]{1,0:T(8,128)S(1)} %get-tuple-element.35.mid_ref, bf16[160,1024]{1,0:T(8,128)(2,1)S(1)} %collective-permute-done.4.even_ref, bf16[160,1024]{1,0:T(8,128)(2,1)S(1)} %collective-permute-done.5.odd_ref), custom_call_target="tpu_custom_call" | custom-call | flops 10000000 | bytes 8000000 | tf_op jit(solution)/shard_map/fold/pallas_call | solution.py:471
  35.3 0.8 %edges.1 = (f32[128,4096]{1,0:T(8,128)}, f32[2,16,1024]{2,1,0:T(8,128)S(1)}) custom-call(f32[128,4096]{1,0:T(8,128)} %get-tuple-element.37.out_in, f32[32,4096]{1,0:T(8,128)S(1)} %get-tuple-element.38.rims_ref, bf16[16,4096]{1,0:T(8,128)(2,1)S(1)} %collective-permute-done.6.even_ref, ...), custom_call_target="tpu_custom_call", output_to_operand_aliasing={{0}: (0, {})} | custom-call | tf_op jit(solution)/shard_map/edges/pallas_call | solution.py:526
  36.1 0.0 collective-permute-done.8.even_ref
  36.1 0.6 %collective-permute-done.9.odd_ref = bf16[16,1024]{1,0:T(8,128)(2,1)S(1)} collective-permute-done((bf16[16,1024]{1,0:T(8,128)(2,1)S(1)}, bf16[16,1024]{1,0:T(8,128)(2,1)S(1)}, u32[]{:S(2)}, u32[]{:S(2)}) %collective-permute-start.9) | collective-permute-done | bytes 32800 | tf_op jit(solution)/shard_map/ppermute | solution.py:549
  36.7 0.7 %corners.1 = f32[128,4096]{1,0:T(8,128)} custom-call(f32[128,4096]{1,0:T(8,128)} %get-tuple-element.41.out_in, f32[2,16,1024]{2,1,0:T(8,128)S(1)} %get-tuple-element.42.corners_ref, bf16[16,1024]{1,0:T(8,128)(2,1)S(1)} %collective-permute-done.8.even_ref, bf16[16,1024]{1,0:T(8,128)(2,1)S(1)} %collective-permute-done.9.odd_ref), custom_call_target="tpu_custom_call", output_to_operand_aliasing={{}: (0, {})} | custom-call | tf_op jit(solution)/shard_map/corners/pallas_call | solution.py:526
  (22 shorter events, 0.1 us)
Async XLA Ops:
  1.0 7.8 %collective-permute-start.1 = (bf16[1,2,32,1024]{3,2,1,0:T(8,128)(2,1)S(1)}, bf16[1,2,32,1024]{3,2,1,0:T(8,128)(2,1)S(1)}, u32[]{:S(2)}, u32[]{:S(2)}) collective-permute-start(bf16[1,2,32,1024]{3,2,1,0:T(8,128)(2,1)S(1)} %get-tuple-element.45), channel_id=1, source_target_pairs={{0,8},{8,0},{16,24},{24,16},{1,9},{9,1},{17,25},{25,17},{2,10},{10... | collective-permute-start | bytes 393224 | tf_op jit(solution)/shard_map/ppermute | solution.py:543
  1.3 8.0 %copy-start = (bf16[4,2,32,1024]{3,2,1,0:T(8,128)(2,1)S(1)}, bf16[4,2,32,1024]{3,2,1,0:T(8,128)(2,1)}, u32[]{:S(2)}) copy-start(bf16[4,2,32,1024]{3,2,1,0:T(8,128)(2,1)} %psfs_ref.1) | copy-start | bytes 1572868
  1.3 13.0 %copy-start.7 = (f32[128,4096]{1,0:T(8,128)S(1)}, f32[128,4096]{1,0:T(8,128)}, u32[]{:S(2)}) copy-start(f32[128,4096]{1,0:T(8,128)} %image_ref) | copy-start | bytes 6291460
  1.3 13.0 %copy-start.8 = (bf16[256,512]{1,0:T(8,128)(2,1)S(1)}, bf16[256,512]{1,0:T(8,128)(2,1)}, u32[]{:S(2)}) copy-start(bf16[256,512]{1,0:T(8,128)(2,1)} %constant.37.clone.refs_1_.tz_ref) | copy-start | bytes 786436
  1.3 13.0 %copy-start.10 = (bf16[192,128]{1,0:T(8,128)(2,1)S(1)}, bf16[192,128]{1,0:T(8,128)(2,1)}, u32[]{:S(2)}) copy-start(bf16[192,128]{1,0:T(8,128)(2,1)} %constant.38.clone.refs_2_.ty_ref) | copy-start | bytes 147460
  1.3 13.0 %copy-start.11 = (bf16[96,64]{1,0:T(8,128)(2,1)S(1)}, bf16[96,64]{1,0:T(8,128)(2,1)}, u32[]{:S(2)}) copy-start(bf16[96,64]{1,0:T(8,128)(2,1)} %constant.36.clone.refs_0_.tx_ref) | copy-start | bytes 36868
  1.3 8.0 %collective-permute-start = (bf16[1,2,32,1024]{3,2,1,0:T(8,128)(2,1)S(1)}, bf16[1,2,32,1024]{3,2,1,0:T(8,128)(2,1)S(1)}, u32[]{:S(2)}, u32[]{:S(2)}) collective-permute-start(bf16[1,2,32,1024]{3,2,1,0:T(8,128)(2,1)S(1)} %get-tuple-element.46), channel_id=1, source_target_pairs={{8,16},{16,8},{9,17},{17,9},{10,18},{18,10},{11,19},{19,11},{12,20... | collective-permute-start | bytes 393224 | tf_op jit(solution)/shard_map/ppermute | solution.py:549
  9.5 7.9 %copy-start.1 = (bf16[256,1024]{1,0:T(8,128)(2,1)S(1)}, bf16[256,1024]{1,0:T(8,128)(2,1)}, u32[]{:S(2)}) copy-start(bf16[256,1024]{1,0:T(8,128)(2,1)} %constant.44.clone.refs_7_) | copy-start | bytes 1572868
  9.5 7.8 %copy-start.2 = (bf16[512,256]{1,0:T(8,128)(2,1)S(1)}, bf16[512,256]{1,0:T(8,128)(2,1)}, u32[]{:S(2)}) copy-start(bf16[512,256]{1,0:T(8,128)(2,1)} %constant.41.clone.refs_10_.tiz) | copy-start | bytes 786436
  9.5 7.8 %copy-start.3 = (bf16[160,192]{1,0:T(8,128)(2,1)S(1)}, bf16[160,192]{1,0:T(8,128)(2,1)}, u32[]{:S(2)}) copy-start(bf16[160,192]{1,0:T(8,128)(2,1)} %constant.42.clone.refs_11_.tix) | copy-start | bytes 184324
  9.5 7.8 %copy-start.4 = (bf16[192,64]{1,0:T(8,128)(2,1)S(1)}, bf16[192,64]{1,0:T(8,128)(2,1)}, u32[]{:S(2)}) copy-start(bf16[192,64]{1,0:T(8,128)(2,1)} %constant.45.clone.refs_8_) | copy-start | bytes 73732
  9.5 7.8 %copy-start.5 = (bf16[64,192]{1,0:T(8,128)(2,1)S(1)}, bf16[64,192]{1,0:T(8,128)(2,1)}, u32[]{:S(2)}) copy-start(bf16[64,192]{1,0:T(8,128)(2,1)} %constant.39.clone.refs_9_) | copy-start | bytes 73732
  9.6 7.8 %copy-start.6 = (bf16[96,128]{1,0:T(8,128)(2,1)S(1)}, bf16[96,128]{1,0:T(8,128)(2,1)}, u32[]{:S(2)}) copy-start(bf16[96,128]{1,0:T(8,128)(2,1)} %constant.43.clone.refs_6_) | copy-start | bytes 73732
  9.6 6.5 %collective-permute-start.2 = (bf16[2,32,1024]{2,1,0:T(8,128)(2,1)S(1)}, bf16[2,32,1024]{2,1,0:T(8,128)(2,1)S(1)}, u32[]{:S(2)}, u32[]{:S(2)}) collective-permute-start(bf16[2,32,1024]{2,1,0:T(8,128)(2,1)S(1)} %get-tuple-element.31.refs_3_), channel_id=1, source_target_pairs={{0,1},{1,0},{2,3},{3,2},{4,5},{5,4},{6,7},{7,6},{8,9},{9,8},{10,11... | collective-permute-start | bytes 393224 | tf_op jit(solution)/shard_map/ppermute | solution.py:543
  11.1 6.3 %collective-permute-start.3 = (bf16[2,32,1024]{2,1,0:T(8,128)(2,1)S(1)}, bf16[2,32,1024]{2,1,0:T(8,128)(2,1)S(1)}, u32[]{:S(2)}, u32[]{:S(2)}) collective-permute-start(bf16[2,32,1024]{2,1,0:T(8,128)(2,1)S(1)} %get-tuple-element.32.refs_4_), channel_id=1, source_target_pairs={{1,2},{2,1},{3,4},{4,3},{5,6},{6,5},{9,10},{10,9},{11,12},{12,11},... | collective-permute-start | bytes 393224 | tf_op jit(solution)/shard_map/ppermute | solution.py:549
  16.0 8.4 %copy-start.9 = (bf16[128,192]{1,0:T(8,128)(2,1)S(1)}, bf16[128,192]{1,0:T(8,128)(2,1)}, u32[]{:S(2)}) copy-start(bf16[128,192]{1,0:T(8,128)(2,1)} %constant.40.clone.tiy) | copy-start | bytes 147460
  21.1 3.3 %collective-permute-start.4 = (bf16[160,1024]{1,0:T(8,128)(2,1)S(1)}, bf16[160,1024]{1,0:T(8,128)(2,1)S(1)}, u32[]{:S(2)}, u32[]{:S(2)}) collective-permute-start(bf16[160,1024]{1,0:T(8,128)(2,1)S(1)} %get-tuple-element.34), channel_id=1, source_target_pairs={{0,1},{1,0},{2,3},{3,2},{4,5},{5,4},{6,7},{7,6},{8,9},{9,8},{10,11... | collective-permute-start | bytes 983048 | tf_op jit(solution)/shard_map/ppermute | solution.py:543
  21.3 9.2 %collective-permute-start.5 = (bf16[160,1024]{1,0:T(8,128)(2,1)S(1)}, bf16[160,1024]{1,0:T(8,128)(2,1)S(1)}, u32[]{:S(2)}, u32[]{:S(2)}) collective-permute-start(bf16[160,1024]{1,0:T(8,128)(2,1)S(1)} %get-tuple-element.36), channel_id=1, source_target_pairs={{1,2},{2,1},{3,4},{4,3},{5,6},{6,5},{9,10},{10,9},{11,12},{12,11},... | collective-permute-start | bytes 983048 | tf_op jit(solution)/shard_map/ppermute | solution.py:549
  26.7 8.5 %collective-permute-start.6 = (bf16[16,4096]{1,0:T(8,128)(2,1)S(1)}, bf16[16,4096]{1,0:T(8,128)(2,1)S(1)}, u32[]{:S(2)}, u32[]{:S(2)}) collective-permute-start(bf16[16,4096]{1,0:T(8,128)(2,1)S(1)} %get-tuple-element.39), channel_id=1, source_target_pairs={{0,8},{8,0},{16,24},{24,16},{1,9},{9,1},{17,25},{25,17},{2,10},{10... | collective-permute-start | bytes 393224 | tf_op jit(solution)/shard_map/ppermute | solution.py:543
  26.8 8.5 %collective-permute-start.7 = (bf16[16,4096]{1,0:T(8,128)(2,1)S(1)}, bf16[16,4096]{1,0:T(8,128)(2,1)S(1)}, u32[]{:S(2)}, u32[]{:S(2)}) collective-permute-start(bf16[16,4096]{1,0:T(8,128)(2,1)S(1)} %get-tuple-element.40), channel_id=1, source_target_pairs={{8,16},{16,8},{9,17},{17,9},{10,18},{18,10},{11,19},{19,11},{12,20... | collective-permute-start | bytes 393224 | tf_op jit(solution)/shard_map/ppermute | solution.py:549
  30.5 5.6 %collective-permute-start.8 = (bf16[16,1024]{1,0:T(8,128)(2,1)S(1)}, bf16[16,1024]{1,0:T(8,128)(2,1)S(1)}, u32[]{:S(2)}, u32[]{:S(2)}) collective-permute-start(bf16[16,1024]{1,0:T(8,128)(2,1)S(1)} %get-tuple-element.43), channel_id=1, source_target_pairs={{0,8},{8,0},{16,24},{24,16},{1,9},{9,1},{17,25},{25,17},{2,10},{10... | collective-permute-start | bytes 98312 | tf_op jit(solution)/shard_map/ppermute | solution.py:543
  30.6 6.1 %collective-permute-start.9 = (bf16[16,1024]{1,0:T(8,128)(2,1)S(1)}, bf16[16,1024]{1,0:T(8,128)(2,1)S(1)}, u32[]{:S(2)}, u32[]{:S(2)}) collective-permute-start(bf16[16,1024]{1,0:T(8,128)(2,1)S(1)} %get-tuple-element.44), channel_id=1, source_target_pairs={{8,16},{16,8},{9,17},{17,9},{10,18},{18,10},{11,19},{19,11},{12,20... | collective-permute-start | bytes 98312 | tf_op jit(solution)/shard_map/ppermute | solution.py:549

commit v10 on v8

--- a/solution.py
+++ b/solution.py
@@ -384,25 +384,25 @@
         name="respond",
     )(*spectra, *columns, *tables)
 
-    def middle():
+    def bands():
         return pl.pallas_call(
-            middle_kernel,
-            out_shape=jax.ShapeDtypeStruct((rows, PATCH * DEPTH), F32),
-            scratch_shapes=[
-                pltpu.VMEM((patches, KX * inner, 2 * YPER * LANES), BF16),
-                pltpu.VMEM((patches, 2, inner * XSTEP, LANES), F32),
-            ],
-            compiler_params=pltpu.CompilerParams(vmem_limit_bytes=24 << 20),
+            bands_kernel,
+            out_shape=(
+                jax.ShapeDtypeStruct((patches, 2, inner * XSTEP, LANES), F32),
+                jax.ShapeDtypeStruct((PSFW, PATCH * DEPTH), F32),
+            ),
+            scratch_shapes=[pltpu.VMEM((patches, KX * inner, 2 * YPER * LANES), BF16)],
+            compiler_params=pltpu.CompilerParams(vmem_limit_bytes=20 << 20),
             cost_estimate=pl.CostEstimate(
-                flops=3_000_000_000, bytes_accessed=6_000_000, transcendentals=0
+                flops=2_000_000_000, bytes_accessed=6_000_000, transcendentals=0
             ),
-            name="middle",
-        )(product, inner_table, z_table, x_table)
-
-    return middle, out_even, out_odd
-
-
-def middle_kernel(product_ref, tiy, tiz, tix, out_ref, rows_ref, grid_x):
+            name="bands",
+        )(product, inner_table, z_table, x_table[rows - PSFW :])
+
+    return bands, x_table[: rows - PSFW], out_even, out_odd
+
+
+def bands_kernel(product_ref, tiy, tiz, tix, grid_x, out_ref, rows_ref):
     tile = 2 * LANES
     patches = product_ref.shape[0]
     inner = OROWS - EDGE
@@ -419,25 +419,26 @@
         out_ref[:, t * tile : (t + 1) * tile] = x_inverted(grid_x, tix, t)
 
 
-def rim_kernel(mid_ref, even_ref, to_odd_ref, to_even_ref):
-    band = even_ref.shape[1]
-    rows, columns = mid_ref.shape[0] - PSFW, mid_ref.shape[1]
+def rim_kernel(band_ref, even_ref, to_odd_ref, to_even_ref):
+    width = even_ref.shape[1]
+    rows, columns = even_ref.shape[0] - PSFW, band_ref.shape[1]
     gx, gy = parity("gx"), parity("gy")
-    corner = pl.ds(pl.multiple_of((1 - gy) * (columns - band), band), band)
+    corner = pl.ds(pl.multiple_of((1 - gy) * (columns - width), width), width)
     for out, side in ((to_odd_ref, gx), (to_even_ref, 1 - gx)):
-        at = pl.ds(pl.multiple_of(rows + side * HALF, HALF), HALF)
-        out[...] = mid_ref[at, :].astype(BF16)
-        out[:, corner] = (mid_ref[at, corner] + even_ref[at, :].astype(F32)).astype(BF16)
-
-
-def x_rims(mid, even):
-    shape = jax.ShapeDtypeStruct((HALF, mid.shape[1]), BF16)
+        at = pl.ds(pl.multiple_of(side * HALF, HALF), HALF)
+        even_at = pl.ds(pl.multiple_of(rows + side * HALF, HALF), HALF)
+        out[...] = band_ref[at, :].astype(BF16)
+        out[:, corner] = (band_ref[at, corner] + even_ref[even_at, :].astype(F32)).astype(BF16)
+
+
+def x_rims(band, even):
+    shape = jax.ShapeDtypeStruct((HALF, band.shape[1]), BF16)
     return pl.pallas_call(
         rim_kernel,
         out_shape=(shape,) * 2,
         compiler_params=pltpu.CompilerParams(vmem_limit_bytes=16 << 20),
         name="x_rims",
-    )(mid, even)
+    )(band, even)
 
 
 def corner_kernel(odd_ref, to_odd_ref, to_even_ref):
@@ -457,11 +458,13 @@
     )(odd)
 
 
-def fold_kernel(mid_ref, even_ref, odd_ref, out_ref, rims_ref):
+def fold_kernel(grid_x, tix, even_ref, odd_ref, out_ref, rims_ref):
     rows, columns = out_ref.shape
+    tile = 2 * LANES
     band = even_ref.shape[1]
     gy = parity("gy")
-    out_ref[...] = mid_ref[:rows, :]
+    for t in range(columns // tile):
+        out_ref[:, t * tile : (t + 1) * tile] = x_inverted(grid_x, tix, t)
     for ref, side in ((even_ref, 1 - gy), (odd_ref, gy)):
         at = pl.ds(pl.multiple_of(side * (columns - band), band), band)
         out_ref[:, at] += ref[:rows, :].astype(F32)
@@ -469,20 +472,20 @@
     rims_ref[HALF:, :] = out_ref[rows - HALF :, :]
 
 
-def fold(mid, even, odd):
-    rows = mid.shape[0] - PSFW
+def fold(grid, table, even, odd):
+    rows, columns = table.shape[0], PATCH * DEPTH
     return pl.pallas_call(
         fold_kernel,
         out_shape=(
-            jax.ShapeDtypeStruct((rows, mid.shape[1]), F32),
-            jax.ShapeDtypeStruct((2 * HALF, mid.shape[1]), F32),
+            jax.ShapeDtypeStruct((rows, columns), F32),
+            jax.ShapeDtypeStruct((2 * HALF, columns), F32),
         ),
         compiler_params=pltpu.CompilerParams(vmem_limit_bytes=16 << 20),
         cost_estimate=pl.CostEstimate(
-            flops=10_000_000, bytes_accessed=8_000_000, transcendentals=0
+            flops=200_000_000, bytes_accessed=8_000_000, transcendentals=0
         ),
         name="fold",
-    )(mid, even, odd)
+    )(grid, table, even, odd)
 
 
 def edges_kernel(out_in, rims_ref, even_ref, odd_ref, out_ref, corners_ref, total, sems):
@@ -567,17 +570,17 @@
     even = swap_even(to_even, "gy")
     odd = swap_odd(to_odd, "gy")
     spectra += [image_forward(image, p) for p in range(1, patches)]
-    middle, out_even, out_odd = respond(spectra, (even, to_even, to_odd, odd))
+    bands, table, out_even, out_odd = respond(spectra, (even, to_even, to_odd, odd))
     odd_y = swap_odd(out_odd, "gy")
     even_y = swap_even(out_even, "gy")
-    mid = middle()
-    out_odd, out_even = x_rims(mid, even_y)
+    grid, band = bands()
+    out_odd, out_even = x_rims(band, even_y)
     even_x = swap_even(out_even, "gx")
     odd_x = swap_odd(out_odd, "gx")
     out_odd, out_even = x_corners(odd_y)
     even_corner = swap_even(out_even, "gx")
     odd_corner = swap_odd(out_odd, "gx")
-    out, rims = fold(mid, even_y, odd_y)
+    out, rims = fold(grid, table, even_y, odd_y)
     out, corners = close(edges_kernel, "edges", out.shape[1], out, rims, even_x, odd_x)
     return close(close_kernel, "corners", HALF * DEPTH, out, corners, even_corner, odd_corner)
 

time: 37.7 us -> 37.7 us (level)
  waiting for transfers between devices: 2.47 us -> 2.04 us
    ppermute x5, waiting for transfers between devices: 2.45 us -> 2.02 us  [swap_odd(): return lax.ppermute(value, axis, pairs)]
where the time goes in v10:
time: 37.7 us; the launch traced here: 37.3 us
  starting transfers between devices  19.6 us (52%)
  Pallas kernels  14.3 us (38%)
  waiting for transfers between devices  2.04 us (5%)
  local copies, waits for them, and re-layouts  1.07 us (3%)
    ppermute x5, starting transfers between devices, swap_odd(): return lax.ppermute(value, axis, pairs)  17.4 us
    pallas_call x1, Pallas kernels, respond(): pl.pallas_call(functools.partial(respond_kernel, patches), out_shape=(jax...  3.66 us
    pallas_call x1, Pallas kernels, image_forward(): pl.pallas_call(functools.partial(fetching_kernel, patch), in_specs=[pl.Bl...  3.06 us
    ppermute x5, starting transfers between devices, swap_even(): lax.ppermute(value, axis, [(i, i ^ 1) for i in range(count) if i ^ 1 < co...  2.19 us
    pallas_call x1, Pallas kernels, bands(): pl.pallas_call(bands_kernel, out_shape=(jax.ShapeDtypeStruct((patches, 2,...  2.18 us
    ppermute x5, waiting for transfers between devices, swap_odd(): return lax.ppermute(value, axis, pairs)  2.02 us
    pallas_call x1, Pallas kernels, fold(): pl.pallas_call(fold_kernel, out_shape=(jax.ShapeDtypeStruct((rows, column...  1.92 us
    pallas_call x1, Pallas kernels, image_forward(): pl.pallas_call(functools.partial(image_kernel, patch), scratch_shapes=scr...  1.66 us
  transfers between devices with their start and end apart: 10, of which 3 were waited for; matrix products, arithmetic and copies ran while one was open for 0% of the time, Pallas kernels for 26%

profile of v10, /device:TPU:19, one launch (start us, length us, event | category | flops | bytes accessed | tf_op | source)
XLA Modules:
  0.0 37.3 jit_solution(11394290421906343859)
XLA Ops:
  0.0 1.0 %constant_dynamic-slice_fusion = (bf16[1,2,32,1024]{3,2,1,0:T(8,128)(2,1)S(1)}, bf16[1,2,32,1024]{3,2,1,0:T(8,128)(2,1)S(1)}) fusion(bf16[4,2,32,1024]{3,2,1,0:T(8,128)(2,1)} %psfs_ref.1, s32[]{:T(128)S(6)} %select_n.7, s32[]{:T(128)S(6)} %select_n.6), kind=kLoop, calls=%fused_computation | loop fusion | bytes 524296 | tf_op jit(solution)/shard_map/dynamic_slice | solution.py:563
  1.0 0.3 collective-permute-start.1
  1.3 0.0 copy-start.12
  1.3 4.3 %collective-permute-start = (bf16[1,2,32,1024]{3,2,1,0:T(8,128)(2,1)S(1)}, bf16[1,2,32,1024]{3,2,1,0:T(8,128)(2,1)S(1)}, u32[]{:S(2)}, u32[]{:S(2)}) collective-permute-start(bf16[1,2,32,1024]{3,2,1,0:T(8,128)(2,1)S(1)} %get-tuple-element.48), channel_id=1, source_target_pairs={{8,16},{16,8},{9,17},{17,9},{10,18},{18,10},{11,19},{19,11},{12,20... | collective-permute-start | bytes 393224 | tf_op jit(solution)/shard_map/ppermute | solution.py:555
  5.7 3.1 %image_first.1.refs_0_ = bf16[48,192,128]{2,1,0:T(8,128)(2,1)S(1)} custom-call(f32[128,4096]{1,0:T(8,128)} %image_ref, bf16[96,64]{1,0:T(8,128)(2,1)} %constant.36.clone.refs_0_.tx_ref, bf16[256,512]{1,0:T(8,128)(2,1)} %constant.37.clone.refs_1_.tz_ref, bf16[192,128]{1,0:T(8,128)(2,1)} %constant.38.clone.refs_2_.ty_ref), custom_call_target="tpu_custom_call" | custom-call | flops 4000000000 | bytes 4000000 | tf_op jit(solution)/shard_map/image_first/pallas_call | solution.py:226
  8.8 0.5 %collective-permute-done.odd_ref = bf16[1,2,32,1024]{3,2,1,0:T(8,128)(2,1)S(1)} collective-permute-done((bf16[1,2,32,1024]{3,2,1,0:T(8,128)(2,1)S(1)}, bf16[1,2,32,1024]{3,2,1,0:T(8,128)(2,1)S(1)}, u32[]{:S(2)}, u32[]{:S(2)}) %collective-permute-start) | collective-permute-done | bytes 131104 | tf_op jit(solution)/shard_map/ppermute | solution.py:555
  9.3 0.2 blend_x.1
  9.5 0.0 copy-start.1
  9.5 0.0 copy-start.2
  9.5 0.0 copy-start.5
  9.5 0.0 copy-start.6
  9.6 0.0 copy-start.7
  9.6 1.5 %collective-permute-start.2 = (bf16[2,32,1024]{2,1,0:T(8,128)(2,1)S(1)}, bf16[2,32,1024]{2,1,0:T(8,128)(2,1)S(1)}, u32[]{:S(2)}, u32[]{:S(2)}) collective-permute-start(bf16[2,32,1024]{2,1,0:T(8,128)(2,1)S(1)} %get-tuple-element.32.refs_3_), channel_id=1, source_target_pairs={{0,1},{1,0},{2,3},{3,2},{4,5},{5,4},{6,7},{7,6},{8,9},{9,8},{10,11... | collective-permute-start | bytes 393224 | tf_op jit(solution)/shard_map/ppermute | solution.py:549
  11.1 3.2 %collective-permute-start.3 = (bf16[2,32,1024]{2,1,0:T(8,128)(2,1)S(1)}, bf16[2,32,1024]{2,1,0:T(8,128)(2,1)S(1)}, u32[]{:S(2)}, u32[]{:S(2)}) collective-permute-start(bf16[2,32,1024]{2,1,0:T(8,128)(2,1)S(1)} %get-tuple-element.33.refs_4_), channel_id=1, source_target_pairs={{1,2},{2,1},{3,4},{4,3},{5,6},{6,5},{9,10},{10,9},{11,12},{12,11},... | collective-permute-start | bytes 393224 | tf_op jit(solution)/shard_map/ppermute | solution.py:555
  14.4 1.7 %image_forward.1.refs_1_ = bf16[48,192,128]{2,1,0:T(8,128)(2,1)S(1)} custom-call(f32[128,4096]{1,0:T(8,128)S(1)} %copy-done.8, bf16[96,64]{1,0:T(8,128)(2,1)S(1)} %copy-done.12, bf16[256,512]{1,0:T(8,128)(2,1)S(1)} %copy-done.9, bf16[192,128]{1,0:T(8,128)(2,1)S(1)} %copy-done.11), custom_call_target="tpu_custom_call" | custom-call | flops 4000000000 | bytes 4000000 | tf_op jit(solution)/shard_map/image_forward/pallas_call | solution.py:220
  16.0 0.0 copy-start.10
  16.0 0.0 copy-start.13
  16.1 1.3 %collective-permute-done.3.refs_5_ = bf16[2,32,1024]{2,1,0:T(8,128)(2,1)S(1)} collective-permute-done((bf16[2,32,1024]{2,1,0:T(8,128)(2,1)S(1)}, bf16[2,32,1024]{2,1,0:T(8,128)(2,1)S(1)}, u32[]{:S(2)}, u32[]{:S(2)}) %collective-permute-start.3) | collective-permute-done | bytes 131104 | tf_op jit(solution)/shard_map/ppermute | solution.py:555
  17.4 3.7 %respond.1 = (bf16[2,24,192,256]{3,2,1,0:T(8,128)(2,1)S(1)}, bf16[160,1024]{1,0:T(8,128)(2,1)S(1)}, bf16[160,1024]{1,0:T(8,128)(2,1)S(1)}) custom-call(bf16[48,192,128]{2,1,0:T(8,128)(2,1)S(1)} %image_first.1.refs_0_, bf16[48,192,128]{2,1,0:T(8,128)(2,1)S(1)} %image_forward.1.refs_1_, bf16[2,32,1024]{2,1,0:T(8,128)(2,1)S(1)} %collective-permute-done.2.refs_2_, ...), custom_call_target="tpu_custom_call" | custom-call | tf_op jit(solution)/shard_map/respond/pallas_call | solution.py:370
  21.1 0.2 collective-permute-start.4
  21.3 3.1 %collective-permute-start.5 = (bf16[160,1024]{1,0:T(8,128)(2,1)S(1)}, bf16[160,1024]{1,0:T(8,128)(2,1)S(1)}, u32[]{:S(2)}, u32[]{:S(2)}) collective-permute-start(bf16[160,1024]{1,0:T(8,128)(2,1)S(1)} %get-tuple-element.37), channel_id=1, source_target_pairs={{1,2},{2,1},{3,4},{4,3},{5,6},{6,5},{9,10},{10,9},{11,12},{12,11},... | collective-permute-start | bytes 983048 | tf_op jit(solution)/shard_map/ppermute | solution.py:555
  24.4 0.0 copy-start.4
  24.4 2.2 %bands.1 = (f32[2,2,1600,128]{3,2,1,0:T(8,128)S(1)}, f32[32,4096]{1,0:T(8,128)S(1)}) custom-call(bf16[2,24,192,256]{3,2,1,0:T(8,128)(2,1)S(1)} %get-tuple-element.34.product_ref, bf16[128,192]{1,0:T(8,128)(2,1)S(1)} %copy-done.10, bf16[512,256]{1,0:T(8,128)(2,1)S(1)} %copy-done.2, bf16[32,192]{1,0:T(8,128)(2,1)S(1)} %copy-done.13), custom_call_target="tpu_custom_call" | custom-call | flops 2000000000 | bytes 6000000 | tf_op jit(solution)/shard_map/bands/pallas_call | solution.py:388
  26.6 0.1 x_rims.1
  26.7 0.1 collective-permute-start.6
  26.8 3.7 %collective-permute-start.7 = (bf16[16,4096]{1,0:T(8,128)(2,1)S(1)}, bf16[16,4096]{1,0:T(8,128)(2,1)S(1)}, u32[]{:S(2)}, u32[]{:S(2)}) collective-permute-start(bf16[16,4096]{1,0:T(8,128)(2,1)S(1)} %get-tuple-element.42), channel_id=1, source_target_pairs={{8,16},{16,8},{9,17},{17,9},{10,18},{18,10},{11,19},{19,11},{12,20... | collective-permute-start | bytes 393224 | tf_op jit(solution)/shard_map/ppermute | solution.py:555
  30.5 0.1 collective-permute-start.8
  30.5 3.1 %collective-permute-start.9 = (bf16[16,1024]{1,0:T(8,128)(2,1)S(1)}, bf16[16,1024]{1,0:T(8,128)(2,1)S(1)}, u32[]{:S(2)}, u32[]{:S(2)}) collective-permute-start(bf16[16,1024]{1,0:T(8,128)(2,1)S(1)} %get-tuple-element.46), channel_id=1, source_target_pairs={{8,16},{16,8},{9,17},{17,9},{10,18},{18,10},{11,19},{19,11},{12,20... | collective-permute-start | bytes 98312 | tf_op jit(solution)/shard_map/ppermute | solution.py:555
  33.7 1.9 %fold.1 = (f32[128,4096]{1,0:T(8,128)}, f32[32,4096]{1,0:T(8,128)S(1)}) custom-call(f32[2,2,1600,128]{3,2,1,0:T(8,128)S(1)} %get-tuple-element.35.grid_x, bf16[128,192]{1,0:T(8,128)(2,1)S(1)} %copy-done.4, bf16[160,1024]{1,0:T(8,128)(2,1)S(1)} %collective-permute-done.4.even_ref, bf16[160,1024]{1,0:T(8,128)(2,1)S(1)} %collective-permute-done.5.odd_ref), custom_call_target="tpu_custom_call" | custom-call | flops 200000000 | bytes 8000000 | tf_op jit(solution)/shard_map/fold/pallas_call | solution.py:477
  35.6 0.8 %edges.1 = (f32[128,4096]{1,0:T(8,128)}, f32[2,16,1024]{2,1,0:T(8,128)S(1)}) custom-call(f32[128,4096]{1,0:T(8,128)} %get-tuple-element.38.out_in, f32[32,4096]{1,0:T(8,128)S(1)} %get-tuple-element.39.rims_ref, bf16[16,4096]{1,0:T(8,128)(2,1)S(1)} %collective-permute-done.6.even_ref, ...), custom_call_target="tpu_custom_call", output_to_operand_aliasing={{0}: (0, {})} | custom-call | tf_op jit(solution)/shard_map/edges/pallas_call | solution.py:532
  36.4 0.2 collective-permute-done.9.odd_ref
  36.6 0.7 %corners.1 = f32[128,4096]{1,0:T(8,128)} custom-call(f32[128,4096]{1,0:T(8,128)} %get-tuple-element.43.out_in, f32[2,16,1024]{2,1,0:T(8,128)S(1)} %get-tuple-element.44.corners_ref, bf16[16,1024]{1,0:T(8,128)(2,1)S(1)} %collective-permute-done.8.even_ref, bf16[16,1024]{1,0:T(8,128)(2,1)S(1)} %collective-permute-done.9.odd_ref), custom_call_target="tpu_custom_call", output_to_operand_aliasing={{}: (0, {})} | custom-call | tf_op jit(solution)/shard_map/corners/pallas_call | solution.py:532
  (27 shorter events, 0.1 us)
Async XLA Ops:
  1.0 7.8 %collective-permute-start.1 = (bf16[1,2,32,1024]{3,2,1,0:T(8,128)(2,1)S(1)}, bf16[1,2,32,1024]{3,2,1,0:T(8,128)(2,1)S(1)}, u32[]{:S(2)}, u32[]{:S(2)}) collective-permute-start(bf16[1,2,32,1024]{3,2,1,0:T(8,128)(2,1)S(1)} %get-tuple-element.47), channel_id=1, source_target_pairs={{0,8},{8,0},{16,24},{24,16},{1,9},{9,1},{17,25},{25,17},{2,10},{10... | collective-permute-start | bytes 393224 | tf_op jit(solution)/shard_map/ppermute | solution.py:549
  1.3 8.0 %copy-start = (bf16[4,2,32,1024]{3,2,1,0:T(8,128)(2,1)S(1)}, bf16[4,2,32,1024]{3,2,1,0:T(8,128)(2,1)}, u32[]{:S(2)}) copy-start(bf16[4,2,32,1024]{3,2,1,0:T(8,128)(2,1)} %psfs_ref.1) | copy-start | bytes 1572868
  1.3 13.0 %copy-start.8 = (f32[128,4096]{1,0:T(8,128)S(1)}, f32[128,4096]{1,0:T(8,128)}, u32[]{:S(2)}) copy-start(f32[128,4096]{1,0:T(8,128)} %image_ref) | copy-start | bytes 6291460
  1.3 13.0 %copy-start.9 = (bf16[256,512]{1,0:T(8,128)(2,1)S(1)}, bf16[256,512]{1,0:T(8,128)(2,1)}, u32[]{:S(2)}) copy-start(bf16[256,512]{1,0:T(8,128)(2,1)} %constant.37.clone.refs_1_.tz_ref) | copy-start | bytes 786436
  1.3 13.0 %copy-start.11 = (bf16[192,128]{1,0:T(8,128)(2,1)S(1)}, bf16[192,128]{1,0:T(8,128)(2,1)}, u32[]{:S(2)}) copy-start(bf16[192,128]{1,0:T(8,128)(2,1)} %constant.38.clone.refs_2_.ty_ref) | copy-start | bytes 147460
  1.3 13.0 %copy-start.12 = (bf16[96,64]{1,0:T(8,128)(2,1)S(1)}, bf16[96,64]{1,0:T(8,128)(2,1)}, u32[]{:S(2)}) copy-start(bf16[96,64]{1,0:T(8,128)(2,1)} %constant.36.clone.refs_0_.tx_ref) | copy-start | bytes 36868
  1.3 8.0 %collective-permute-start = (bf16[1,2,32,1024]{3,2,1,0:T(8,128)(2,1)S(1)}, bf16[1,2,32,1024]{3,2,1,0:T(8,128)(2,1)S(1)}, u32[]{:S(2)}, u32[]{:S(2)}) collective-permute-start(bf16[1,2,32,1024]{3,2,1,0:T(8,128)(2,1)S(1)} %get-tuple-element.48), channel_id=1, source_target_pairs={{8,16},{16,8},{9,17},{17,9},{10,18},{18,10},{11,19},{19,11},{12,20... | collective-permute-start | bytes 393224 | tf_op jit(solution)/shard_map/ppermute | solution.py:555
  9.5 7.9 %copy-start.1 = (bf16[256,1024]{1,0:T(8,128)(2,1)S(1)}, bf16[256,1024]{1,0:T(8,128)(2,1)}, u32[]{:S(2)}) copy-start(bf16[256,1024]{1,0:T(8,128)(2,1)} %constant.44.clone.refs_7_) | copy-start | bytes 1572868
  9.5 7.8 %copy-start.2 = (bf16[512,256]{1,0:T(8,128)(2,1)S(1)}, bf16[512,256]{1,0:T(8,128)(2,1)}, u32[]{:S(2)}) copy-start(bf16[512,256]{1,0:T(8,128)(2,1)} %constant.41.clone.refs_10_.tiz) | copy-start | bytes 786436
  9.5 7.8 %copy-start.3 = (bf16[160,192]{1,0:T(8,128)(2,1)S(1)}, bf16[160,192]{1,0:T(8,128)(2,1)}, u32[]{:S(2)}) copy-start(bf16[160,192]{1,0:T(8,128)(2,1)} %constant.42.clone.refs_11_) | copy-start | bytes 184324
  9.5 7.8 %copy-start.5 = (bf16[192,64]{1,0:T(8,128)(2,1)S(1)}, bf16[192,64]{1,0:T(8,128)(2,1)}, u32[]{:S(2)}) copy-start(bf16[192,64]{1,0:T(8,128)(2,1)} %constant.45.clone.refs_8_) | copy-start | bytes 73732
  9.5 7.8 %copy-start.6 = (bf16[64,192]{1,0:T(8,128)(2,1)S(1)}, bf16[64,192]{1,0:T(8,128)(2,1)}, u32[]{:S(2)}) copy-start(bf16[64,192]{1,0:T(8,128)(2,1)} %constant.39.clone.refs_9_) | copy-start | bytes 73732
  9.6 7.8 %copy-start.7 = (bf16[96,128]{1,0:T(8,128)(2,1)S(1)}, bf16[96,128]{1,0:T(8,128)(2,1)}, u32[]{:S(2)}) copy-start(bf16[96,128]{1,0:T(8,128)(2,1)} %constant.43.clone.refs_6_) | copy-start | bytes 73732
  9.6 6.5 %collective-permute-start.2 = (bf16[2,32,1024]{2,1,0:T(8,128)(2,1)S(1)}, bf16[2,32,1024]{2,1,0:T(8,128)(2,1)S(1)}, u32[]{:S(2)}, u32[]{:S(2)}) collective-permute-start(bf16[2,32,1024]{2,1,0:T(8,128)(2,1)S(1)} %get-tuple-element.32.refs_3_), channel_id=1, source_target_pairs={{0,1},{1,0},{2,3},{3,2},{4,5},{5,4},{6,7},{7,6},{8,9},{9,8},{10,11... | collective-permute-start | bytes 393224 | tf_op jit(solution)/shard_map/ppermute | solution.py:549
  11.1 6.3 %collective-permute-start.3 = (bf16[2,32,1024]{2,1,0:T(8,128)(2,1)S(1)}, bf16[2,32,1024]{2,1,0:T(8,128)(2,1)S(1)}, u32[]{:S(2)}, u32[]{:S(2)}) collective-permute-start(bf16[2,32,1024]{2,1,0:T(8,128)(2,1)S(1)} %get-tuple-element.33.refs_4_), channel_id=1, source_target_pairs={{1,2},{2,1},{3,4},{4,3},{5,6},{6,5},{9,10},{10,9},{11,12},{12,11},... | collective-permute-start | bytes 393224 | tf_op jit(solution)/shard_map/ppermute | solution.py:555
  16.0 8.4 %copy-start.10 = (bf16[128,192]{1,0:T(8,128)(2,1)S(1)}, bf16[128,192]{1,0:T(8,128)(2,1)}, u32[]{:S(2)}) copy-start(bf16[128,192]{1,0:T(8,128)(2,1)} %constant.40.clone.tiy) | copy-start | bytes 147460
  16.0 8.4 %copy-start.13 = (bf16[32,192]{1,0:T(8,128)(2,1)S(1)}, bf16[32,192]{1,0:T(8,128)(2,1)}, u32[]{:S(2)}) copy-start(bf16[32,192]{1,0:T(8,128)(2,1)} %constant.47.tix) | copy-start | bytes 36868
  21.1 5.5 %collective-permute-start.4 = (bf16[160,1024]{1,0:T(8,128)(2,1)S(1)}, bf16[160,1024]{1,0:T(8,128)(2,1)S(1)}, u32[]{:S(2)}, u32[]{:S(2)}) collective-permute-start(bf16[160,1024]{1,0:T(8,128)(2,1)S(1)} %get-tuple-element.36), channel_id=1, source_target_pairs={{0,1},{1,0},{2,3},{3,2},{4,5},{5,4},{6,7},{7,6},{8,9},{9,8},{10,11... | collective-permute-start | bytes 983048 | tf_op jit(solution)/shard_map/ppermute | solution.py:549
  21.3 9.1 %collective-permute-start.5 = (bf16[160,1024]{1,0:T(8,128)(2,1)S(1)}, bf16[160,1024]{1,0:T(8,128)(2,1)S(1)}, u32[]{:S(2)}, u32[]{:S(2)}) collective-permute-start(bf16[160,1024]{1,0:T(8,128)(2,1)S(1)} %get-tuple-element.37), channel_id=1, source_target_pairs={{1,2},{2,1},{3,4},{4,3},{5,6},{6,5},{9,10},{10,9},{11,12},{12,11},... | collective-permute-start | bytes 983048 | tf_op jit(solution)/shard_map/ppermute | solution.py:555
  24.4 9.2 %copy-start.4 = (bf16[128,192]{1,0:T(8,128)(2,1)S(1)}, bf16[128,192]{1,0:T(8,128)(2,1)}, u32[]{:S(2)}) copy-start(bf16[128,192]{1,0:T(8,128)(2,1)} %constant.48.tix) | copy-start | bytes 147460
  26.7 8.9 %collective-permute-start.6 = (bf16[16,4096]{1,0:T(8,128)(2,1)S(1)}, bf16[16,4096]{1,0:T(8,128)(2,1)S(1)}, u32[]{:S(2)}, u32[]{:S(2)}) collective-permute-start(bf16[16,4096]{1,0:T(8,128)(2,1)S(1)} %get-tuple-element.41), channel_id=1, source_target_pairs={{0,8},{8,0},{16,24},{24,16},{1,9},{9,1},{17,25},{25,17},{2,10},{10... | collective-permute-start | bytes 393224 | tf_op jit(solution)/shard_map/ppermute | solution.py:549
  26.8 8.8 %collective-permute-start.7 = (bf16[16,4096]{1,0:T(8,128)(2,1)S(1)}, bf16[16,4096]{1,0:T(8,128)(2,1)S(1)}, u32[]{:S(2)}, u32[]{:S(2)}) collective-permute-start(bf16[16,4096]{1,0:T(8,128)(2,1)S(1)} %get-tuple-element.42), channel_id=1, source_target_pairs={{8,16},{16,8},{9,17},{17,9},{10,18},{18,10},{11,19},{19,11},{12,20... | collective-permute-start | bytes 393224 | tf_op jit(solution)/shard_map/ppermute | solution.py:555
  30.5 6.0 %collective-permute-start.8 = (bf16[16,1024]{1,0:T(8,128)(2,1)S(1)}, bf16[16,1024]{1,0:T(8,128)(2,1)S(1)}, u32[]{:S(2)}, u32[]{:S(2)}) collective-permute-start(bf16[16,1024]{1,0:T(8,128)(2,1)S(1)} %get-tuple-element.45), channel_id=1, source_target_pairs={{0,8},{8,0},{16,24},{24,16},{1,9},{9,1},{17,25},{25,17},{2,10},{10... | collective-permute-start | bytes 98312 | tf_op jit(solution)/shard_map/ppermute | solution.py:549
  30.5 6.1 %collective-permute-start.9 = (bf16[16,1024]{1,0:T(8,128)(2,1)S(1)}, bf16[16,1024]{1,0:T(8,128)(2,1)S(1)}, u32[]{:S(2)}, u32[]{:S(2)}) collective-permute-start(bf16[16,1024]{1,0:T(8,128)(2,1)S(1)} %get-tuple-element.46), channel_id=1, source_target_pairs={{8,16},{16,8},{9,17},{17,9},{10,18},{18,10},{11,19},{19,11},{12,20... | collective-permute-start | bytes 98312 | tf_op jit(solution)/shard_map/ppermute | solution.py:555
